TPU v7x, 32 devices: a whole 2x2x4 slice. The times are simulated.
32 devices in a mesh: seq: 16 (over z, y, x), head: 2 (over core).
Axes of the slice: x: 2, y: 2, z: 4, core: 2. Of those that a mesh axis runs over, the one named last changes fastest.
Arguments:
- queries: bfloat16 [8192, 2048], P('seq', 'head'), may hold values from -6 to 6
- keys: bfloat16 [8192, 2048], P('seq', 'head'), may hold values from -6 to 6
- values: bfloat16 [8192, 4096], P('seq', 'head'), may hold values from -6 to 6
- input_gate: float32 [8, 8192], P('head', 'seq'), may hold values from -8 to 15
- forget_gate: float32 [8, 8192], P('head', 'seq'), may hold values from -1 to 15
- out_weight: bfloat16 [4096, 4096], P('seq', 'head'), may hold values from -0.09375 to 0.09375
Outputs:
- mixed: bfloat16 [8192, 4096], P('seq', 'head')
All inputs are finite; a program needn't handle non-finite values.
Results may differ from a plain program's by a relative error of at most 0.02.
Values may be sent and summed in bfloat16 or wider, within the bound.
No kernel may reach another device: no remote copies, remote signals or barrier semaphores. Data moves between devices by JAX's collectives and lax.ppermute only.
A program may use at most 128 MiB of HBM per device.

v0:
```python
import jax
import jax.numpy as jnp
from jax import lax
from jax.sharding import PartitionSpec as P


def entering(part, axis, combine, identity):
    place = lax.axis_index(axis)
    gathered = jax.tree.map(lambda a: lax.all_gather(a, axis), part)
    state = jax.tree.map(lambda a, e: jnp.zeros_like(a) + jnp.asarray(e, a.dtype), part, identity)

    def one(turn, state):
        return combine(
            state, jax.tree.map(lambda a: lax.dynamic_index_in_dim(a, turn, 0, False), gathered)
        )

    return lax.fori_loop(0, place, one, state)


def summarize(keys_block, block_of_values, gate_in, gate_forget):
    scaling = keys_block.shape[1] ** (-0.5)
    cumulative = jnp.cumsum(jax.nn.log_sigmoid(gate_forget))
    total_log = cumulative[-1]
    exponent = total_log - cumulative + gate_in
    local_top = jnp.max(exponent)
    weighted = (
        keys_block.astype(jnp.float32) * (jnp.exp(exponent - local_top) * scaling)[:, None]
    ).astype(jnp.bfloat16)
    memory = jnp.dot(weighted.T, block_of_values, preferred_element_type=jnp.float32)
    norm_vec = jnp.sum(weighted.astype(jnp.float32), axis=0)
    return (cumulative, (memory, norm_vec, local_top, total_log))


def combine(preceding_state, later):
    mem_one, norm_one, top_one, log_one = preceding_state
    mem_two, norm_two, top_two, log_two = later
    top_new = jnp.maximum(top_one + log_two, top_two)
    factor_one = jnp.exp(top_one + log_two - top_new)
    factor_two = jnp.exp(top_two - top_new)
    memory = factor_one[..., None, None] * mem_one + factor_two[..., None, None] * mem_two
    norm_vec = factor_one[..., None] * norm_one + factor_two[..., None] * norm_two
    return (memory, norm_vec, top_new, log_one + log_two)


def finish(
    queries_block,
    keys_block,
    block_of_values,
    gate_in,
    cumulative,
    carry_mem,
    carry_norm,
    carry_top,
):
    scaling = keys_block.shape[1] ** (-0.5)
    length = queries_block.shape[0]
    scores = jnp.dot(queries_block, keys_block.T, preferred_element_type=jnp.float32) * scaling
    log_weight = cumulative[:, None] - cumulative[None, :] + gate_in[None, :]
    causal = jnp.arange(length)[:, None] >= jnp.arange(length)[None, :]
    log_weight = jnp.where(causal, log_weight, -1e30)
    row_top = jnp.maximum(carry_top + cumulative, jnp.max(log_weight, axis=1))
    carry_factor = jnp.exp(carry_top + cumulative - row_top)
    weights = jnp.where(causal, jnp.exp(log_weight - row_top[:, None]) * scores, 0.0)
    query_wide = queries_block.astype(jnp.float32)
    numer = carry_factor[:, None] * jnp.dot(query_wide, carry_mem, precision=lax.Precision.HIGHEST)
    numer = numer + jnp.dot(
        weights.astype(jnp.bfloat16), block_of_values, preferred_element_type=jnp.float32
    )
    denom = carry_factor * jnp.dot(
        query_wide, carry_norm, precision=lax.Precision.HIGHEST
    ) + jnp.sum(weights, axis=1)
    return (numer / jnp.maximum(jnp.abs(denom), 1.0)[:, None]).astype(jnp.bfloat16)


def body(queries, keys, values, input_gate, forget_gate, out_weight):
    local_heads = input_gate.shape[0]
    tokens_here = queries.shape[0]
    key_size = queries.shape[1] // local_heads
    value_size = values.shape[1] // local_heads
    query_heads = queries.reshape(tokens_here, local_heads, key_size)
    heads_of_keys = keys.reshape(tokens_here, local_heads, key_size)
    value_heads = values.reshape(tokens_here, local_heads, value_size)
    cumulative, summary = jax.vmap(summarize, in_axes=(1, 1, 0, 0))(
        heads_of_keys, value_heads, input_gate, forget_gate
    )
    identity = (
        jnp.zeros((local_heads, key_size, value_size), jnp.float32),
        jnp.zeros((local_heads, key_size), jnp.float32),
        jnp.full((local_heads,), -1e30, jnp.float32),
        jnp.zeros((local_heads,), jnp.float32),
    )
    piece_count = 4
    piece_width = value_size // piece_count
    pieces_done = []
    carry_rest = None
    for index_piece in range(piece_count):
        offset = index_piece * piece_width
        part_mem = lax.slice_in_dim(summary[0], offset, offset + piece_width, axis=2)
        part_identity = (
            jnp.zeros((local_heads, key_size, piece_width), jnp.float32),
            identity[1],
            identity[2],
            identity[3],
        )
        result_piece = entering(
            (part_mem, summary[1], summary[2], summary[3]), "seq", combine, part_identity
        )
        pieces_done.append(result_piece[0])
        carry_rest = result_piece
    carry = (jnp.concatenate(pieces_done, axis=2), carry_rest[1], carry_rest[2], carry_rest[3])
    hidden = jax.vmap(finish, in_axes=(1, 1, 1, 0, 0, 0, 0, 0), out_axes=1)(
        query_heads,
        heads_of_keys,
        value_heads,
        input_gate,
        cumulative,
        carry[0],
        carry[1],
        carry[2],
    )
    hidden = hidden.reshape(tokens_here, local_heads * value_size)
    all_heads = lax.all_gather(hidden, "head", axis=1, tiled=True)
    mixed = jnp.dot(
        all_heads,
        lax.all_gather(out_weight, "seq", axis=0, tiled=True),
        preferred_element_type=jnp.float32,
    )
    return mixed.astype(jnp.bfloat16)


def solution(mesh):
    return jax.shard_map(
        body,
        mesh=mesh,
        in_specs=(
            P("seq", "head"),
            P("seq", "head"),
            P("seq", "head"),
            P("head", "seq"),
            P("head", "seq"),
            P("seq", "head"),
        ),
        out_specs=P("seq", "head"),
        check_vma=False,
    )
```

profile of v0, /device:TPU:0, one launch (start us, length us, event | category | flops | bytes accessed | tf_op | source)
XLA Modules:
  0.0 732.5 jit_solution(480916676551857339)
XLA Ops:
  7.3 1.2 reduce-window.6
  9.1 0.9 fusion.59
  10.0 0.8 exponential_multiply_fusion
  10.8 2.9 copy.44
  13.7 1.5 copy.70
  15.9 1.4 fusion.65
  21.2 44.4 %all-reduce.2 = (f32[64]{0:T(128)S(1)}, f32[64]{0:T(128)S(1)}) all-reduce(f32[64]{0:T(128)S(1)} %dynamic-update-slice, f32[64]{0:T(128)S(1)} %dynamic-update-slice.1), channel_id=2, replica_groups=mesh['seq'=16,'head'=2] {'seq'}, use_global_device_ids=true, to_apply=%add | all-reduce | flops 128 | bytes 1024
  65.7 2.3 copy.45
  68.3 36.6 %all-gather.7 = f32[16,4,256]{2,1,0:T(4,128)S(1)} all-gather(f32[1,4,256]{2,1,0:T(4,128)S(1)} %bitcast.208), channel_id=5, replica_groups=mesh['seq'=16,'head'=2] {'seq'}, dimensions={0}, use_global_device_ids=true | all-gather | bytes 69632 | tf_op jit(solution)/shard_map/all_gather | solution.py:9
  105.0 0.8 fusion.23
  105.8 28.5 %all-gather.19.cloned.1.call-done = f32[64,256,128]{2,1,0:T(8,128)} async-done(((f32[4,256,128]{2,1,0:T(8,128)}), f32[64,256,128]{2,1,0:T(8,128)}) %all-gather.19.cloned.1.call-update) | async-done | bytes 8388624 | tf_op jit(solution)/shard_map/all_gather | solution.py:9
  134.5 113.7 %all-gather.21.cloned.1.call-done = f32[64,256,128]{2,1,0:T(8,128)} async-done(((f32[4,256,128]{2,1,0:T(8,128)}), f32[64,256,128]{2,1,0:T(8,128)}) %all-gather.21.cloned.1.call-update) | async-done | bytes 8388624 | tf_op jit(solution)/shard_map/all_gather | solution.py:9
  248.4 1.0 copy.31
  249.4 112.7 %all-gather.23.cloned.1.call-done = f32[64,256,128]{2,1,0:T(8,128)} async-done(((f32[4,256,128]{2,1,0:T(8,128)}), f32[64,256,128]{2,1,0:T(8,128)}) %all-gather.23.cloned.1.call-update) | async-done | bytes 8388624 | tf_op jit(solution)/shard_map/all_gather | solution.py:9
  362.2 1.0 copy.32
  363.3 1.7 fusion.53
  365.0 3.5 fusion.24
  368.5 3.7 fusion.26
  372.2 103.6 %all-gather.25.cloned.1.call-done = f32[64,256,128]{2,1,0:T(8,128)} async-done(((f32[4,256,128]{2,1,0:T(8,128)}), f32[64,256,128]{2,1,0:T(8,128)}) %all-gather.25.cloned.1.call-update) | async-done | bytes 8388624 | tf_op jit(solution)/shard_map/all_gather | solution.py:9
  475.9 1.0 copy.33
  477.5 5.8 fusion.22
  483.9 31.7 %all-gather.15.cloned.1.call-done = bf16[512,4096]{0,1:T(8,128)(2,1)} async-done(((bf16[512,2048]{0,1:T(8,128)(2,1)}), bf16[512,4096]{0,1:T(8,128)(2,1)}) %all-gather.15.cloned.1.call-update) | async-done | bytes 4194320 | tf_op jit(solution)/shard_map/all_gather | solution.py:122
  515.6 195.4 %all-gather.17.cloned.1.call-done = bf16[4096,2048]{1,0:T(8,128)(2,1)} async-done(((bf16[256,2048]{1,0:T(8,128)(2,1)}), bf16[4096,2048]{1,0:T(8,128)(2,1)}) %all-gather.17.cloned.1.call-update) | async-done | bytes 16777232 | tf_op jit(solution)/shard_map/all_gather | solution.py:125
  711.0 14.6 %convolution_convert_fusion = bf16[512,2048]{1,0:T(8,128)(2,1)} fusion(bf16[512,4096]{0,1:T(8,128)(2,1)} %all-gather.15.cloned.1.call-done, bf16[4096,2048]{1,0:T(8,128)(2,1)} %all-gather.17.cloned.1.call-done), kind=kOutput, calls=%fused_computation.49 | convolution fusion | flops 8590983168 | bytes 23068672 | tf_op jit(solution)/shard_map/dot_general | solution.py:123
  (55 shorter events, 7.4 us)
Async XLA Ops:
  6.5 127.7 %all-gather.19.cloned.1.call-start = ((), (), s32[]{:S(2)}) async-start(), calls=%async_computation.2 | async-start | bytes 8912896 | tf_op jit(solution)/shard_map/all_gather | solution.py:9
  15.9 3.6 copy-start.4
  15.9 89.0 %copy-start.3 = (f32[4,512]{1,0:T(4,128)S(1)}, f32[4,512]{1,0:T(4,128)}, u32[]{:S(2)}) copy-start(f32[4,512]{1,0:T(4,128)} %param.17) | copy-start | bytes 24580
  17.3 230.9 %all-gather.21.cloned.1.call-start = ((), (), s32[]{:S(2)}) async-start(), calls=%async_computation.3 | async-start | bytes 8912896 | tf_op jit(solution)/shard_map/all_gather | solution.py:9
  18.1 344.0 %all-gather.23.cloned.1.call-start = ((), (), s32[]{:S(2)}) async-start(), calls=%async_computation.4 | async-start | bytes 8912896 | tf_op jit(solution)/shard_map/all_gather | solution.py:9
  18.8 457.0 %all-gather.25.cloned.1.call-start = ((), (), s32[]{:S(2)}) async-start(), calls=%async_computation.5 | async-start | bytes 8912896 | tf_op jit(solution)/shard_map/all_gather | solution.py:9
  19.4 496.2 %all-gather.15.cloned.1.call-start = ((), (), s32[]{:S(2)}) async-start(), calls=%async_computation | async-start | bytes 6291456 | tf_op jit(solution)/shard_map/all_gather | solution.py:122
  475.8 1.3 copy-start
  475.9 1.5 copy-start.1
  475.9 1.7 copy-start.2
  483.3 227.7 %all-gather.17.cloned.1.call-start = ((), (), s32[]{:S(2)}) async-start(), calls=%async_computation.1 | async-start | bytes 17825792 | tf_op jit(solution)/shard_map/all_gather | solution.py:125
Sparse Core Ops, SparseCore 0:
  17.5 116.7 all-gather.18
  137.0 111.2 all-gather.20
  251.1 111.0 all-gather.22
  364.7 111.0 all-gather.24
  483.4 32.1 all-gather.14
  518.2 192.7 all-gather.16
where the time goes:
time: 736 us; the launch traced here: 732 us
  waiting for transfers between devices  588 us (80%)
  blocking collectives  81 us (11%)
  matrix products  29.9 us (4%)
  between operations  14.4 us (2%)
  local copies, waits for them, and re-layouts  13.6 us (2%)
    all_gather x4, waiting for transfers between devices, entering(): gathered = jax.tree.map(lambda a: lax.all_gather(a, axis), part)  359 us
    all_gather x1, waiting for transfers between devices, body(): lax.all_gather(out_weight, 'seq', axis=0, tiled=True)  195 us
    unnamed x1, blocking collectives  44.4 us
    all_gather x1, blocking collectives, entering(): gathered = jax.tree.map(lambda a: lax.all_gather(a, axis), part)  36.6 us
    all_gather x1, waiting for transfers between devices, body(): all_heads = lax.all_gather(hidden, 'head', axis=1, tiled=True)  31.7 us
  transfers between devices with their start and end apart: 6, of which 6 were waited for; matrix products, arithmetic and copies ran while one was open for 2% of the time, Pallas kernels for 0%

commit v1 on v0

v1 whole, which is shorter than its diff:
```python
import functools

import jax
import jax.numpy as jnp
from jax import lax
from jax.experimental import pallas as pl
from jax.experimental.pallas import tpu as pltpu
from jax.sharding import PartitionSpec as P

F32 = jnp.float32
BF16 = jnp.bfloat16
LOW = -1e30
PARTS = 4
LANES = 128


def full_spec():
    return pl.BlockSpec(memory_space=pltpu.VMEM)


def smem_spec():
    return pl.BlockSpec(memory_space=pltpu.SMEM)


def column(row):
    return jnp.transpose(jnp.broadcast_to(row, (8, row.shape[1])))[:, :1]


def summary_kernel(place_ref, k_ref, v_ref, in_ref, forget_ref, c_ref, aux_ref, g_ref):
    heads, length = in_ref.shape
    key_size = k_ref.shape[1] // heads
    value_size = v_ref.shape[1] // heads
    width = value_size // PARTS
    x = forget_ref[...]
    lf = jnp.minimum(x, 0.0) - jnp.log1p(jnp.exp(-jnp.abs(x)))
    upto = (
        lax.broadcasted_iota(jnp.int32, (length, length), 0)
        <= lax.broadcasted_iota(jnp.int32, (length, length), 1)
    ).astype(F32)
    g = jnp.dot(lf, upto, precision=lax.Precision.HIGHEST, preferred_element_type=F32)
    g_ref[...] = g
    total = g[:, length - 1 :]
    e = total - g + in_ref[...]
    top = jnp.max(e, axis=1, keepdims=True)
    scale = jnp.exp(e - top) * (key_size**-0.5)
    place = place_ref[0]
    lane = lax.broadcasted_iota(jnp.int32, (heads, LANES), 1)
    aux_ref[:, key_size:] = jnp.where(lane == 0, top, jnp.where(lane == 1, total, 0.0))
    for h in range(heads):
        weighted = (
            k_ref[:, h * key_size : (h + 1) * key_size].astype(F32) * column(scale[h : h + 1])
        ).astype(BF16)
        aux_ref[h : h + 1, :key_size] = jnp.sum(weighted.astype(F32), axis=0, keepdims=True)
        memory = lax.dot_general(
            weighted,
            v_ref[:, h * value_size : (h + 1) * value_size],
            (((0,), (0,)), ((), ())),
            preferred_element_type=F32,
        ).astype(BF16)
        for c in range(PARTS):
            c_ref[lax.bitwise_xor(place, c), h] = memory[:, c * width : (c + 1) * width]


def summarize(place, keys, values, gate_in, gate_forget):
    heads, length = gate_in.shape
    key_size = keys.shape[1] // heads
    value_size = values.shape[1] // heads
    return pl.pallas_call(
        summary_kernel,
        out_shape=(
            jax.ShapeDtypeStruct((PARTS, heads, key_size, value_size // PARTS), BF16),
            jax.ShapeDtypeStruct((heads, key_size + LANES), F32),
            jax.ShapeDtypeStruct((heads, length), F32),
        ),
        in_specs=[smem_spec()] + [full_spec()] * 4,
        out_specs=(full_spec(), full_spec(), full_spec()),
        compiler_params=pltpu.CompilerParams(vmem_limit_bytes=40 * 1024 * 1024),
    )(place, keys, values, gate_in, gate_forget)


def intra_kernel(q_ref, k_ref, v_ref, in_ref, g_ref, top_ref, norm_ref, part_ref, coef_ref):
    length, key_size = q_ref.shape
    g_row = g_ref[0]
    g_col = column(g_row)
    carry_log = g_col + top_ref[0][:, :1]
    row = lax.broadcasted_iota(jnp.int32, (length, length), 0)
    col = lax.broadcasted_iota(jnp.int32, (length, length), 1)
    causal = row >= col
    log_weight = jnp.where(causal, g_col - g_row + in_ref[0], LOW)
    row_top = jnp.maximum(carry_log, jnp.max(log_weight, axis=1, keepdims=True))
    factor = jnp.exp(carry_log - row_top)
    q = q_ref[...]
    scores = lax.dot_general(
        q, k_ref[...], (((1,), (1,)), ((), ())), preferred_element_type=F32
    ) * (key_size**-0.5)
    weights = jnp.where(causal, jnp.exp(log_weight - row_top) * scores, 0.0)
    carried = jnp.sum(q.astype(F32) * norm_ref[0], axis=1, keepdims=True)
    denom = factor * carried + jnp.sum(weights, axis=1, keepdims=True)
    inverse = 1.0 / jnp.maximum(jnp.abs(denom), 1.0)
    part_ref[...] = (
        jnp.dot(weights.astype(BF16), v_ref[...], preferred_element_type=F32) * inverse
    )
    coef_ref[0] = jnp.broadcast_to(factor * inverse, (length, LANES))


def intra(queries, keys, values, gate_in, g, carry_top, carry_norm):
    heads, length = gate_in.shape
    key_size = keys.shape[1] // heads
    value_size = values.shape[1] // heads
    per_head = lambda r, w: pl.BlockSpec((1, r, w), lambda h: (h, 0, 0))
    return pl.pallas_call(
        intra_kernel,
        grid=(heads,),
        out_shape=(
            jax.ShapeDtypeStruct((length, heads * value_size), F32),
            jax.ShapeDtypeStruct((heads, length, LANES), F32),
        ),
        in_specs=[
            pl.BlockSpec((length, key_size), lambda h: (0, h)),
            pl.BlockSpec((length, key_size), lambda h: (0, h)),
            pl.BlockSpec((length, value_size), lambda h: (0, h)),
            per_head(1, length),
            per_head(1, length),
            per_head(1, LANES),
            per_head(1, key_size),
        ],
        out_specs=(
            pl.BlockSpec((length, value_size), lambda h: (0, h)),
            per_head(length, LANES),
        ),
        compiler_params=pltpu.CompilerParams(vmem_limit_bytes=40 * 1024 * 1024),
    )(
        queries,
        keys,
        values,
        gate_in[:, None],
        g[:, None],
        jnp.broadcast_to(carry_top[:, None, None], (heads, 1, LANES)),
        carry_norm[:, None],
    )


def join_kernel(place_ref, q_ref, *refs):
    pieces, (part_ref, coef_ref, out_ref, mem_ref) = refs[:PARTS], refs[PARTS:]
    width = pieces[0].shape[-1]
    for r in range(PARTS):
        at = pl.multiple_of(lax.bitwise_xor(place_ref[0], r) * width, width)
        mem_ref[:, pl.ds(at, width)] = pieces[r][0]
    inter = jnp.dot(q_ref[...], mem_ref[...], preferred_element_type=F32)
    out_ref[...] = (coef_ref[0][:, :1] * inter + part_ref[...]).astype(BF16)


def join(place, queries, carries, part, coef):
    heads, key_size, width = carries[0].shape
    length = queries.shape[0]
    value_size = width * PARTS
    return pl.pallas_call(
        join_kernel,
        grid=(heads,),
        out_shape=jax.ShapeDtypeStruct((length, heads * value_size), BF16),
        in_specs=[smem_spec(), pl.BlockSpec((length, key_size), lambda h: (0, h))]
        + [pl.BlockSpec((1, key_size, width), lambda h: (h, 0, 0))] * PARTS
        + [
            pl.BlockSpec((length, value_size), lambda h: (0, h)),
            pl.BlockSpec((1, length, LANES), lambda h: (h, 0, 0)),
        ],
        out_specs=pl.BlockSpec((length, value_size), lambda h: (0, h)),
        scratch_shapes=[pltpu.VMEM((key_size, value_size), BF16)],
        compiler_params=pltpu.CompilerParams(vmem_limit_bytes=40 * 1024 * 1024),
    )(place, queries, *carries, part, coef)


def xor_perm(n, d):
    return [(i, i ^ d) for i in range(n)]


def windows(tops, logs, ids, lo, hi):
    lo, hi = lo[:, None], hi[:, None]
    between = (ids[None, None, :] > ids[None, :, None]) & (ids[None, None, :] < hi[:, :, None])
    weight = tops[None] + jnp.sum(jnp.where(between[..., None], logs[None, None], 0.0), axis=2)
    inside = ((ids[None] >= lo) & (ids[None] < hi))[..., None]
    weight = jnp.where(inside, weight, LOW)
    return weight, jnp.max(weight, axis=1), jnp.sum(jnp.where(inside, logs[None], 0.0), axis=1)


def ring_perms(n):
    pairs = n // 2
    order = list(range(0, pairs, 2)) + list(range(1, pairs, 2))[::-1]
    fwd = [
        (2 * order[r] + x, 2 * order[(r + 1) % pairs] + x) for r in range(pairs) for x in (0, 1)
    ]
    return order, fwd, [(d, s) for s, d in fwd]


def ring(piece, n):
    _, fwd, bwd = ring_perms(n)
    count = n // 2
    got = {0: piece}
    f = b = piece
    for t in range(1, (count - 1) // 2 + 1):
        f = lax.ppermute(f, "seq", fwd)
        b = lax.ppermute(b, "seq", bwd)
        got[t], got[-t] = f, b
    half = piece.shape[0] // 2
    got[count // 2] = (
        lax.ppermute(f[:half], "seq", fwd),
        lax.ppermute(b[half:], "seq", bwd),
    )
    return got


def place_rows(full, piece, at):
    parts = piece if isinstance(piece, tuple) else (piece,)
    for p in parts:
        full = lax.dynamic_update_slice(full, p, (at, 0))
        at = at + p.shape[0]
    return full


def gather_weight(weight, n):
    rows, cols = weight.shape
    me = lax.axis_index("seq")
    order, _, _ = ring_perms(n)
    count = len(order)
    where = [order.index(q) for q in range(count)]
    here = jnp.array(where)[me // 2]
    side = me % 2

    def row_of(distance, flip):
        src = jnp.array(order)[(here - distance) % count]
        return (2 * src + (1 - side if flip else side)) * rows

    split = cols // 2
    first, second = weight[:, :split], weight[:, split:]
    swap = functools.partial(lax.ppermute, axis_name="seq", perm=xor_perm(n, 1))
    got_second = ring(second, n)
    other = swap(first)
    full_second = jnp.zeros((n * rows, cols - split), weight.dtype)
    for d, a in got_second.items():
        full_second = place_rows(full_second, a, row_of(d, False))
        b = tuple(swap(p) for p in a) if isinstance(a, tuple) else swap(a)
        full_second = place_rows(full_second, b, row_of(d, True))
    full_first = jnp.zeros((n * rows, split), weight.dtype)
    for flip, piece in ((False, first), (True, other)):
        for d, a in ring(piece, n).items():
            full_first = place_rows(full_first, a, row_of(d, flip))
    return full_first, full_second


def scale_heads(factor, a):
    return factor[:, None, None] * a.astype(F32)


def body(queries, keys, values, input_gate, forget_gate, out_weight, n, n_head):
    me = lax.axis_index("seq")
    spot = me % PARTS
    level = me // PARTS
    place = spot.astype(jnp.int32)[None]
    key_size = keys.shape[1] // input_gate.shape[0]
    memory, aux, g = summarize(place, keys, values, input_gate, forget_gate)

    table = aux[None]
    d = 1
    while d < n:
        table = jnp.concatenate([table, lax.ppermute(table, "seq", xor_perm(n, d))], axis=0)
        d *= 2
    got = [memory[0]] + [
        lax.ppermute(memory[r], "seq", xor_perm(n, r)) for r in range(1, PARTS)
    ]
    ids = lax.bitwise_xor(me, jnp.arange(n, dtype=me.dtype))
    tops, logs = table[:, :, key_size], table[:, :, key_size + 1]

    rounds = []
    d = 1
    while d < n // PARTS:
        rounds.append(d)
        d *= 2
    base = level * PARTS
    spans = [(base, base + PARTS)]
    for d in rounds:
        spans += [
            (base - PARTS * (d - 1), base + PARTS),
            (base - PARTS * (2 * d - 1), base - PARTS * (d - 1)),
            (base - PARTS * (d - 1), base),
            (base - PARTS * (2 * d - 1), base + PARTS),
            (base - PARTS * (2 * d - 1), base),
        ]
    zero = base * 0
    spans += [(zero, base)]
    spans += [(zero, base + lax.bitwise_xor(spot, r)) for r in range(PARTS)]
    low = jnp.maximum(jnp.stack([a for a, _ in spans]), 0)
    high = jnp.maximum(jnp.stack([b for _, b in spans]), 0)
    weight, top, log = windows(tops, logs, ids, low, high)

    acc = sum(scale_heads(jnp.exp(weight[0, r] - top[0]), got[r]) for r in range(PARTS))
    window = acc.astype(BF16)
    earlier = jnp.zeros(window.shape, F32)
    for i, d in enumerate(rounds):
        own, far, near, wide, before = range(1 + 5 * i, 6 + 5 * i)
        step = d * PARTS
        come = lax.ppermute(window, "seq", [(s, s + step) for s in range(n - step)])
        earlier = scale_heads(jnp.exp(top[near] - top[before]), earlier) + scale_heads(
            jnp.exp(top[far] + log[near] - top[before]), come
        )
        if d != rounds[-1]:
            window = (
                scale_heads(jnp.exp(top[own] - top[wide]), window)
                + scale_heads(jnp.exp(top[far] + log[own] - top[wide]), come)
            ).astype(BF16)
    final = len(spans) - PARTS - 1
    carries = []
    for r in range(PARTS):
        w = final + 1 + r
        behind = jnp.sum(
            jnp.where(((ids >= base) & (ids < high[w]))[:, None], logs, 0.0), axis=0
        )
        total = scale_heads(jnp.exp(top[final] + behind - top[w]), earlier)
        for c in range(PARTS):
            total = total + scale_heads(
                jnp.where(ids[c] < high[w], jnp.exp(weight[w, c] - top[w]), 0.0), got[c]
            )
        carries.append(total.astype(BF16))
    carries = [carries[0]] + [
        lax.ppermute(carries[r], "seq", xor_perm(n, r)) for r in range(1, PARTS)
    ]

    mine = final + 1
    carry_norm = jnp.sum(
        jnp.where((ids < me)[:, None], jnp.exp(weight[mine] - top[mine]), 0.0)[..., None]
        * table[:, :, :key_size],
        axis=0,
    )
    part, coef = intra(queries, keys, values, input_gate, g, top[mine], carry_norm)
    hidden = join(place, queries, carries, part, coef)

    if n_head == 2:
        other = lax.ppermute(hidden, "head", [(0, 1), (1, 0)])
        first = lax.axis_index("head") == 0
        all_heads = jnp.concatenate(
            [jnp.where(first, hidden, other), jnp.where(first, other, hidden)], axis=1
        )
    else:
        all_heads = lax.all_gather(hidden, "head", axis=1, tiled=True)

    pieces = [
        jnp.dot(all_heads, w, preferred_element_type=F32).astype(BF16)
        for w in gather_weight(out_weight, n)
    ]
    return jnp.concatenate(pieces, axis=1)


def solution(mesh):
    return jax.shard_map(
        functools.partial(body, n=mesh.shape["seq"], n_head=mesh.shape["head"]),
        mesh=mesh,
        in_specs=(
            P("seq", "head"),
            P("seq", "head"),
            P("seq", "head"),
            P("head", "seq"),
            P("head", "seq"),
            P("seq", "head"),
        ),
        out_specs=P("seq", "head"),
        check_vma=False,
    )
```

time: 736 us -> 260 us (0.35)
  waiting for transfers between devices: 588 us -> 57.4 us
  blocking collectives: 81 us -> 0 us
  starting transfers between devices: 0.38 us -> 68.1 us
  local copies, waits for them, and re-layouts: 13.6 us -> 53.9 us
  between operations: 14.4 us -> 32.6 us
  other arithmetic: 5.17 us -> 21.9 us
  matrix products: 29.9 us -> 15.7 us
  Pallas kernels: 0 us -> 9.09 us
    all_gather x6 -> x0, waiting for transfers between devices: 586 us -> none  [the longest x4 359 us: entering(): gathered = jax.tree.map(lambda a: lax.all_gather(a, axis), part)]
    ppermute x0 -> x47, starting transfers between devices: none -> 68.1 us  [the longest x9 23.3 us: ring(): f = lax.ppermute(f, 'seq', fwd)]
    ppermute x0 -> x47, waiting for transfers between devices: none -> 57.4 us  [the longest x9 14.7 us: ring(): f = lax.ppermute(f, 'seq', fwd)]
    unnamed x1 -> x0, blocking collectives: 44.4 us -> none
    all_gather x1 -> x0, blocking collectives: 36.6 us -> none  [entering(): gathered = jax.tree.map(lambda a: lax.all_gather(a, axis), part)]
    dynamic_update_slice x0 -> x35, local copies, waits for them, and re-layouts: none -> 32.6 us  [place_rows(): full = lax.dynamic_update_slice(full, p, (at, 0))]
    dot_general x6 -> x2, matrix products: 29.9 us -> 15.7 us  [body(): jnp.dot(all_heads, w, preferred_element_type=F32).astype(BF16)]
    convert_element_type x0 -> x6, other arithmetic: none -> 9.53 us  [the longest x4 6.26 us: body(): carries.append(total.astype(BF16))]
  transfers between devices with their start and end apart: 6 -> 47, of which waited for: 6 -> 17; matrix products, arithmetic and copies ran while one was open for 2% -> 24% of each run, Pallas kernels for 0% -> 4%
where the time goes in v1:
time: 260 us; the launch traced here: 259 us
  starting transfers between devices  68.1 us (26%)
  waiting for transfers between devices  57.4 us (22%)
  local copies, waits for them, and re-layouts  53.9 us (21%)
  between operations  32.6 us (13%)
  other arithmetic  21.9 us (8%)
  matrix products  15.7 us (6%)
  Pallas kernels  9.09 us (3%)
    dynamic_update_slice x35, local copies, waits for them, and re-layouts, place_rows(): full = lax.dynamic_update_slice(full, p, (at, 0))  32.6 us
    ppermute x9, starting transfers between devices, ring(): f = lax.ppermute(f, 'seq', fwd)  23.3 us
    dot_general x2, matrix products, body(): jnp.dot(all_heads, w, preferred_element_type=F32).astype(BF16)  15.7 us
    ppermute x9, waiting for transfers between devices, ring(): f = lax.ppermute(f, 'seq', fwd)  14.7 us
    ppermute x3, waiting for transfers between devices, body(): lax.ppermute(carries[r], 'seq', xor_perm(n, r))  12.9 us
    ppermute x9, starting transfers between devices, gather_weight(): b = tuple((swap(p) for p in a)) if isinstance(a, tuple) else swap(a)  9.51 us
    another operation x2, local copies, waits for them, and re-layouts  8.61 us
    ppermute x9, starting transfers between devices, ring(): b = lax.ppermute(b, 'seq', bwd)  8.06 us
  transfers between devices with their start and end apart: 47, of which 17 were waited for; matrix products, arithmetic and copies ran while one was open for 24% of the time, Pallas kernels for 4%

profile of v1, /device:TPU:0, one launch (start us, length us, event | category | flops | bytes accessed | tf_op | source)
XLA Modules:
  0.0 258.7 jit_solution(15229934706296831328)
XLA Ops:
  10.4 4.3 %broadcast.335.clone.1 = bf16[4096,1024]{1,0:T(8,128)(2,1)} broadcast(bf16[]{:T(256)} %constant.209.clone.1), dimensions={} | broadcast | bytes 8388610 | tf_op jit(solution)/shard_map/broadcast.3
  16.0 3.1 %collective-permute-start.13 = (bf16[256,1024]{1,0:T(8,128)(2,1)}, bf16[256,1024]{1,0:T(8,128)(2,1)}, u32[]{:S(2)}, u32[]{:S(2)}) collective-permute-start(bf16[256,1024]{1,0:T(8,128)(2,1)} %get-tuple-element.42), channel_id=1, source_target_pairs={{0,8},{2,10},{8,16},{10,18},{16,24},{18,26},{24,28},{26,30},{28,20... | collective-permute-start | bytes 1572872 | tf_op jit(solution)/shard_map/ppermute | solution.py:201
  20.3 2.3 shard_map.361
  31.4 4.3 %broadcast.335.clone = bf16[4096,1024]{1,0:T(8,128)(2,1)} broadcast(bf16[]{:T(256)} %constant.209.clone.1), dimensions={} | broadcast | bytes 8388610 | tf_op jit(solution)/shard_map/broadcast.3
  64.8 3.2 %collective-permute-done.1 = f32[2,4,384]{2,1,0:T(4,128)S(1)} collective-permute-done((f32[2,4,384]{2,1,0:T(4,128)S(1)}, f32[2,4,384]{2,1,0:T(4,128)S(1)}, u32[]{:S(2)}, u32[]{:S(2)}) %collective-permute-start.1) | collective-permute-done | bytes 12320 | tf_op jit(solution)/shard_map/ppermute | solution.py:265
  69.6 2.3 collective-permute-done.2
  71.9 2.6 %collective-permute-start.3 = (f32[8,4,384]{2,1,0:T(4,128)S(1)}, f32[8,4,384]{2,1,0:T(4,128)S(1)}, u32[]{:S(2)}, u32[]{:S(2)}) collective-permute-start(f32[8,4,384]{2,1,0:T(4,128)S(1)} %pad_maximum_fusion.8), channel_id=1, source_target_pairs={{0,16},{2,18},{4,20},{6,22},{8,24},{10,26},{12,28},{14,30},{16,0},... | collective-permute-start | bytes 147464 | tf_op jit(solution)/shard_map/ppermute | solution.py:265
  74.5 2.4 collective-permute-done.3
  90.6 3.7 %collective-permute-start.7 = (bf16[4,256,128]{2,1,0:T(8,128)(2,1)}, bf16[4,256,128]{2,1,0:T(8,128)(2,1)}, u32[]{:S(2)}, u32[]{:S(2)}) collective-permute-start(bf16[4,256,128]{2,1,0:T(8,128)(2,1)} %fusion.12), channel_id=1, source_target_pairs={{0,8},{2,10},{4,12},{6,14},{8,16},{10,18},{12,20},{14,22},{16,24},... | collective-permute-start | bytes 786440 | tf_op jit(solution)/shard_map/ppermute | solution.py:301
  96.7 4.8 %shard_map.362 = (f32[512,2048]{1,0:T(8,128)S(1)}, f32[4,512,128]{2,1,0:T(8,128)S(1)}) custom-call(bf16[512,1024]{1,0:T(8,128)(2,1)S(1)} %copy-done.1, bf16[512,1024]{1,0:T(8,128)(2,1)S(1)} %copy-done.3, bf16[512,2048]{1,0:T(8,128)(2,1)S(1)} %copy-done, f32[4,1,512]{2,1,0:T(1,128)S(1)} %broadcast_in_dim.192.in_ref, ...), custom_call_target="tpu_custom_call" | custom-call | tf_op jit(solution)/shard_map/pallas_call | solution.py:111
  106.7 4.1 %collective-permute-start.8 = (bf16[4,256,128]{2,1,0:T(8,128)(2,1)S(1)}, bf16[4,256,128]{2,1,0:T(8,128)(2,1)S(1)}, u32[]{:S(2)}, u32[]{:S(2)}) collective-permute-start(bf16[4,256,128]{2,1,0:T(8,128)(2,1)S(1)} %fusion.8), channel_id=1, source_target_pairs={{0,16},{2,18},{4,20},{6,22},{8,24},{10,26},{12,28},{14,30},{1,17},... | collective-permute-start | bytes 786440 | tf_op jit(solution)/shard_map/ppermute | solution.py:301
  116.6 6.1 %collective-permute-start.22 = (bf16[256,1024]{1,0:T(8,128)(2,1)}, bf16[256,1024]{1,0:T(8,128)(2,1)S(1)}, u32[]{:S(2)}, u32[]{:S(2)}) collective-permute-start(bf16[256,1024]{1,0:T(8,128)(2,1)} %collective-permute-done.21), channel_id=1, source_target_pairs={{0,8},{2,10},{8,16},{10,18},{16,24},{18,26},{24,28},{26,30},{28,20... | collective-permute-start | bytes 1572872 | tf_op jit(solution)/shard_map/ppermute | solution.py:201
  128.6 2.7 %collective-permute-done.15 = bf16[256,1024]{1,0:T(8,128)(2,1)S(1)} collective-permute-done((bf16[256,1024]{1,0:T(8,128)(2,1)}, bf16[256,1024]{1,0:T(8,128)(2,1)S(1)}, u32[]{:S(2)}, u32[]{:S(2)}) %collective-permute-start.15) | collective-permute-done | bytes 524320 | tf_op jit(solution)/shard_map/ppermute | solution.py:201
  131.3 8.2 %collective-permute-start.35 = (bf16[256,1024]{1,0:T(8,128)(2,1)S(1)}, bf16[256,1024]{1,0:T(8,128)(2,1)S(1)}, u32[]{:S(2)}, u32[]{:S(2)}) collective-permute-start(bf16[256,1024]{1,0:T(8,128)(2,1)S(1)} %collective-permute-done.31), channel_id=1, source_target_pairs={{0,8},{2,10},{8,16},{10,18},{16,24},{18,26},{24,28},{26,30},{28,20... | collective-permute-start | bytes 1572872 | tf_op jit(solution)/shard_map/ppermute | solution.py:201
  142.5 2.2 collective-permute-start.10
  147.3 11.5 %collective-permute-done.11.refs_3_ = bf16[4,256,128]{2,1,0:T(8,128)(2,1)S(1)} collective-permute-done((bf16[4,256,128]{2,1,0:T(8,128)(2,1)S(1)}, bf16[4,256,128]{2,1,0:T(8,128)(2,1)S(1)}, u32[]{:S(2)}, u32[]{:S(2)}) %collective-permute-start.11) | collective-permute-done | bytes 262176 | tf_op jit(solution)/shard_map/ppermute | solution.py:324
  175.6 2.4 collective-permute-start.39
  182.5 6.4 %collective-permute-done.24 = bf16[256,1024]{1,0:T(8,128)(2,1)S(1)} collective-permute-done((bf16[256,1024]{1,0:T(8,128)(2,1)S(1)}, bf16[256,1024]{1,0:T(8,128)(2,1)S(1)}, u32[]{:S(2)}, u32[]{:S(2)}) %collective-permute-start.24) | collective-permute-done | bytes 524320 | tf_op jit(solution)/shard_map/ppermute | solution.py:201
  192.8 5.2 %collective-permute-done.39 = bf16[256,1024]{1,0:T(8,128)(2,1)S(1)} collective-permute-done((bf16[256,1024]{1,0:T(8,128)(2,1)S(1)}, bf16[256,1024]{1,0:T(8,128)(2,1)S(1)}, u32[]{:S(2)}, u32[]{:S(2)}) %collective-permute-start.39) | collective-permute-done | bytes 524320 | tf_op jit(solution)/shard_map/ppermute | solution.py:201
  207.9 5.0 %collective-permute-done.43 = bf16[128,1024]{1,0:T(8,128)(2,1)S(1)} collective-permute-done((bf16[128,1024]{1,0:T(8,128)(2,1)S(1)}, bf16[128,1024]{1,0:T(8,128)(2,1)S(1)}, u32[]{:S(2)}, u32[]{:S(2)}) %collective-permute-start.43) | collective-permute-done | bytes 262176 | tf_op jit(solution)/shard_map/ppermute | solution.py:206
  216.2 5.9 %collective-permute-done.44 = bf16[128,1024]{1,0:T(8,128)(2,1)S(1)} collective-permute-done((bf16[128,1024]{1,0:T(8,128)(2,1)S(1)}, bf16[128,1024]{1,0:T(8,128)(2,1)S(1)}, u32[]{:S(2)}, u32[]{:S(2)}) %collective-permute-start.44) | collective-permute-done | bytes 262176 | tf_op jit(solution)/shard_map/ppermute | solution.py:207
  234.1 4.2 %collective-permute-done.46 = bf16[128,1024]{1,0:T(8,128)(2,1)S(1)} collective-permute-done((bf16[128,1024]{1,0:T(8,128)(2,1)S(1)}, bf16[128,1024]{1,0:T(8,128)(2,1)S(1)}, u32[]{:S(2)}, u32[]{:S(2)}) %collective-permute-start.46) | collective-permute-done | bytes 262176 | tf_op jit(solution)/shard_map/ppermute | solution.py:241
  241.5 7.9 %fusion.2 = bf16[512,1024]{1,0:T(8,128)(2,1)S(1)} fusion(bf16[4096,1024]{1,0:T(8,128)(2,1)} %constant_dynamic-update-slice_fusion.23, bf16[512,2048]{1,0:T(8,128)(2,1)S(1)} %get-tuple-element.41, bf16[512,2048]{1,0:T(8,128)(2,1)S(1)} %get-tuple-element.40), kind=kOutput, calls=%fused_computation.6 | convolution fusion | flops 4303880192 | bytes 13631488 | tf_op jit(solution)/shard_map/dot_general | solution.py:346
  249.4 7.9 %fusion.3 = bf16[512,1024]{1,0:T(8,128)(2,1)S(1)} fusion(bf16[4096,1024]{1,0:T(8,128)(2,1)} %constant_dynamic-update-slice_fusion.22, bf16[512,2048]{1,0:T(8,128)(2,1)S(1)} %get-tuple-element.41, bf16[512,2048]{1,0:T(8,128)(2,1)S(1)} %get-tuple-element.40), kind=kOutput, calls=%fused_computation.7 | convolution fusion | flops 4303880192 | bytes 13631488 | tf_op jit(solution)/shard_map/dot_general | solution.py:346
  (230 shorter events, 113.7 us)
Async XLA Ops:
  16.0 85.6 %collective-permute-start.13 = (bf16[256,1024]{1,0:T(8,128)(2,1)}, bf16[256,1024]{1,0:T(8,128)(2,1)}, u32[]{:S(2)}, u32[]{:S(2)}) collective-permute-start(bf16[256,1024]{1,0:T(8,128)(2,1)} %get-tuple-element.42), channel_id=1, source_target_pairs={{0,8},{2,10},{8,16},{10,18},{16,24},{18,26},{24,28},{26,30},{28,20... | collective-permute-start | bytes 1572872 | tf_op jit(solution)/shard_map/ppermute | solution.py:201
  19.0 87.7 %collective-permute-start.14 = (bf16[256,1024]{1,0:T(8,128)(2,1)}, bf16[256,1024]{1,0:T(8,128)(2,1)}, u32[]{:S(2)}, u32[]{:S(2)}) collective-permute-start(bf16[256,1024]{1,0:T(8,128)(2,1)} %get-tuple-element.42), channel_id=1, source_target_pairs={{8,0},{10,2},{16,8},{18,10},{24,16},{26,18},{28,24},{30,26},{20,28... | collective-permute-start | bytes 1572872 | tf_op jit(solution)/shard_map/ppermute | solution.py:202
  22.6 41.7 %collective-permute-start = (f32[1,4,384]{2,1,0:T(4,128)S(1)}, f32[1,4,384]{2,1,0:T(4,128)S(1)}, u32[]{:S(2)}, u32[]{:S(2)}) collective-permute-start(f32[1,4,384]{2,1,0:T(4,128)S(1)} %bitcast.137), channel_id=1, source_target_pairs={{0,2},{2,0},{4,6},{6,4},{8,10},{10,8},{12,14},{14,12},{16,18},{18,... | collective-permute-start | bytes 18440 | tf_op jit(solution)/shard_map/ppermute | solution.py:265
  25.5 61.0 %collective-permute-start.4 = (bf16[4,256,128]{2,1,0:T(8,128)(2,1)}, bf16[4,256,128]{2,1,0:T(8,128)(2,1)S(1)}, u32[]{:S(2)}, u32[]{:S(2)}) collective-permute-start(bf16[4,256,128]{2,1,0:T(8,128)(2,1)} %get-tuple-element.47), channel_id=1, source_target_pairs={{0,2},{2,0},{4,6},{6,4},{8,10},{10,8},{12,14},{14,12},{16,18},{18,... | collective-permute-start | bytes 786440 | tf_op jit(solution)/shard_map/ppermute | solution.py:268
  26.4 60.5 %collective-permute-start.5 = (bf16[4,256,128]{2,1,0:T(8,128)(2,1)}, bf16[4,256,128]{2,1,0:T(8,128)(2,1)}, u32[]{:S(2)}, u32[]{:S(2)}) collective-permute-start(bf16[4,256,128]{2,1,0:T(8,128)(2,1)} %get-tuple-element.46), channel_id=1, source_target_pairs={{0,4},{2,6},{4,0},{6,2},{8,12},{10,14},{12,8},{14,10},{16,20},{18,... | collective-permute-start | bytes 786440 | tf_op jit(solution)/shard_map/ppermute | solution.py:268
  86.5 28.1 %collective-permute-start.21 = (bf16[256,1024]{1,0:T(8,128)(2,1)}, bf16[256,1024]{1,0:T(8,128)(2,1)}, u32[]{:S(2)}, u32[]{:S(2)}) collective-permute-start(bf16[256,1024]{1,0:T(8,128)(2,1)} %get-tuple-element.42), channel_id=1, source_target_pairs={{0,2},{2,0},{4,6},{6,4},{8,10},{10,8},{12,14},{14,12},{16,18},{18,... | collective-permute-start | bytes 1572872 | tf_op jit(solution)/shard_map/ppermute | solution.py:237
  86.9 25.8 %collective-permute-start.30 = (bf16[256,1024]{1,0:T(8,128)(2,1)}, bf16[256,1024]{1,0:T(8,128)(2,1)}, u32[]{:S(2)}, u32[]{:S(2)}) collective-permute-start(bf16[256,1024]{1,0:T(8,128)(2,1)} %get-tuple-element.44), channel_id=1, source_target_pairs={{0,2},{2,0},{4,6},{6,4},{8,10},{10,8},{12,14},{14,12},{16,18},{18,... | collective-permute-start | bytes 1572872 | tf_op jit(solution)/shard_map/ppermute | solution.py:241
  104.3 23.1 %collective-permute-start.33 = (bf16[256,1024]{1,0:T(8,128)(2,1)}, bf16[256,1024]{1,0:T(8,128)(2,1)S(1)}, u32[]{:S(2)}, u32[]{:S(2)}) collective-permute-start(bf16[256,1024]{1,0:T(8,128)(2,1)} %get-tuple-element.44), channel_id=1, source_target_pairs={{8,0},{10,2},{16,8},{18,10},{24,16},{26,18},{28,24},{30,26},{20,28... | collective-permute-start | bytes 1572872 | tf_op jit(solution)/shard_map/ppermute | solution.py:202
  114.6 26.5 %collective-permute-start.16 = (bf16[256,1024]{1,0:T(8,128)(2,1)}, bf16[256,1024]{1,0:T(8,128)(2,1)S(1)}, u32[]{:S(2)}, u32[]{:S(2)}) collective-permute-start(bf16[256,1024]{1,0:T(8,128)(2,1)} %collective-permute-done.14), channel_id=1, source_target_pairs={{8,0},{10,2},{16,8},{18,10},{24,16},{26,18},{28,24},{30,26},{20,28... | collective-permute-start | bytes 1572872 | tf_op jit(solution)/shard_map/ppermute | solution.py:202
  116.6 25.9 %collective-permute-start.22 = (bf16[256,1024]{1,0:T(8,128)(2,1)}, bf16[256,1024]{1,0:T(8,128)(2,1)S(1)}, u32[]{:S(2)}, u32[]{:S(2)}) collective-permute-start(bf16[256,1024]{1,0:T(8,128)(2,1)} %collective-permute-done.21), channel_id=1, source_target_pairs={{0,8},{2,10},{8,16},{10,18},{16,24},{18,26},{24,28},{26,30},{28,20... | collective-permute-start | bytes 1572872 | tf_op jit(solution)/shard_map/ppermute | solution.py:201
  123.5 19.0 %collective-permute-start.23 = (bf16[256,1024]{1,0:T(8,128)(2,1)}, bf16[256,1024]{1,0:T(8,128)(2,1)S(1)}, u32[]{:S(2)}, u32[]{:S(2)}) collective-permute-start(bf16[256,1024]{1,0:T(8,128)(2,1)} %collective-permute-done.21), channel_id=1, source_target_pairs={{8,0},{10,2},{16,8},{18,10},{24,16},{26,18},{28,24},{30,26},{20,28... | collective-permute-start | bytes 1572872 | tf_op jit(solution)/shard_map/ppermute | solution.py:202
  127.4 19.0 %collective-permute-start.32 = (bf16[256,1024]{1,0:T(8,128)(2,1)S(1)}, bf16[256,1024]{1,0:T(8,128)(2,1)S(1)}, u32[]{:S(2)}, u32[]{:S(2)}) collective-permute-start(bf16[256,1024]{1,0:T(8,128)(2,1)S(1)} %collective-permute-done.31), channel_id=1, source_target_pairs={{0,2},{2,0},{4,6},{6,4},{8,10},{10,8},{12,14},{14,12},{16,18},{18,... | collective-permute-start | bytes 1572872 | tf_op jit(solution)/shard_map/ppermute | solution.py:241
  131.3 28.8 %collective-permute-start.35 = (bf16[256,1024]{1,0:T(8,128)(2,1)S(1)}, bf16[256,1024]{1,0:T(8,128)(2,1)S(1)}, u32[]{:S(2)}, u32[]{:S(2)}) collective-permute-start(bf16[256,1024]{1,0:T(8,128)(2,1)S(1)} %collective-permute-done.31), channel_id=1, source_target_pairs={{0,8},{2,10},{8,16},{10,18},{16,24},{18,26},{24,28},{26,30},{28,20... | collective-permute-start | bytes 1572872 | tf_op jit(solution)/shard_map/ppermute | solution.py:201
  141.1 22.7 %collective-permute-start.34 = (bf16[256,1024]{1,0:T(8,128)(2,1)S(1)}, bf16[256,1024]{1,0:T(8,128)(2,1)S(1)}, u32[]{:S(2)}, u32[]{:S(2)}) collective-permute-start(bf16[256,1024]{1,0:T(8,128)(2,1)S(1)} %collective-permute-done.33), channel_id=1, source_target_pairs={{0,2},{2,0},{4,6},{6,4},{8,10},{10,8},{12,14},{14,12},{16,18},{18,... | collective-permute-start | bytes 1572872 | tf_op jit(solution)/shard_map/ppermute | solution.py:241
  142.5 19.1 %collective-permute-start.10 = (bf16[4,256,128]{2,1,0:T(8,128)(2,1)S(1)}, bf16[4,256,128]{2,1,0:T(8,128)(2,1)S(1)}, u32[]{:S(2)}, u32[]{:S(2)}) collective-permute-start(bf16[4,256,128]{2,1,0:T(8,128)(2,1)S(1)} %fusion.24), channel_id=1, source_target_pairs={{0,4},{2,6},{4,0},{6,2},{8,12},{10,14},{12,8},{14,10},{16,20},{18,... | collective-permute-start | bytes 786440 | tf_op jit(solution)/shard_map/ppermute | solution.py:324
  146.3 23.8 %collective-permute-start.37 = (bf16[256,1024]{1,0:T(8,128)(2,1)S(1)}, bf16[256,1024]{1,0:T(8,128)(2,1)S(1)}, u32[]{:S(2)}, u32[]{:S(2)}) collective-permute-start(bf16[256,1024]{1,0:T(8,128)(2,1)S(1)} %collective-permute-done.33), channel_id=1, source_target_pairs={{8,0},{10,2},{16,8},{18,10},{24,16},{26,18},{28,24},{30,26},{20,28... | collective-permute-start | bytes 1572872 | tf_op jit(solution)/shard_map/ppermute | solution.py:202
  168.0 20.9 %collective-permute-start.24 = (bf16[256,1024]{1,0:T(8,128)(2,1)S(1)}, bf16[256,1024]{1,0:T(8,128)(2,1)S(1)}, u32[]{:S(2)}, u32[]{:S(2)}) collective-permute-start(bf16[256,1024]{1,0:T(8,128)(2,1)S(1)} %collective-permute-done.22), channel_id=1, source_target_pairs={{0,8},{2,10},{8,16},{10,18},{16,24},{18,26},{24,28},{26,30},{28,20... | collective-permute-start | bytes 1572872 | tf_op jit(solution)/shard_map/ppermute | solution.py:201
  170.1 21.8 %collective-permute-start.38 = (bf16[256,1024]{1,0:T(8,128)(2,1)S(1)}, bf16[256,1024]{1,0:T(8,128)(2,1)S(1)}, u32[]{:S(2)}, u32[]{:S(2)}) collective-permute-start(bf16[256,1024]{1,0:T(8,128)(2,1)S(1)} %collective-permute-done.37), channel_id=1, source_target_pairs={{0,2},{2,0},{4,6},{6,4},{8,10},{10,8},{12,14},{14,12},{16,18},{18,... | collective-permute-start | bytes 1572872 | tf_op jit(solution)/shard_map/ppermute | solution.py:241
  175.6 22.4 %collective-permute-start.39 = (bf16[256,1024]{1,0:T(8,128)(2,1)S(1)}, bf16[256,1024]{1,0:T(8,128)(2,1)S(1)}, u32[]{:S(2)}, u32[]{:S(2)}) collective-permute-start(bf16[256,1024]{1,0:T(8,128)(2,1)S(1)} %collective-permute-done.35), channel_id=1, source_target_pairs={{0,8},{2,10},{8,16},{10,18},{16,24},{18,26},{24,28},{26,30},{28,20... | collective-permute-start | bytes 1572872 | tf_op jit(solution)/shard_map/ppermute | solution.py:201
  178.8 20.1 %collective-permute-start.41 = (bf16[256,1024]{1,0:T(8,128)(2,1)S(1)}, bf16[256,1024]{1,0:T(8,128)(2,1)S(1)}, u32[]{:S(2)}, u32[]{:S(2)}) collective-permute-start(bf16[256,1024]{1,0:T(8,128)(2,1)S(1)} %collective-permute-done.37), channel_id=1, source_target_pairs={{8,0},{10,2},{16,8},{18,10},{24,16},{26,18},{28,24},{30,26},{20,28... | collective-permute-start | bytes 1572872 | tf_op jit(solution)/shard_map/ppermute | solution.py:202
  181.2 20.6 %collective-permute-start.25 = (bf16[256,1024]{1,0:T(8,128)(2,1)S(1)}, bf16[256,1024]{1,0:T(8,128)(2,1)S(1)}, u32[]{:S(2)}, u32[]{:S(2)}) collective-permute-start(bf16[256,1024]{1,0:T(8,128)(2,1)S(1)} %collective-permute-done.23), channel_id=1, source_target_pairs={{8,0},{10,2},{16,8},{18,10},{24,16},{26,18},{28,24},{30,26},{20,28... | collective-permute-start | bytes 1572872 | tf_op jit(solution)/shard_map/ppermute | solution.py:202
  198.9 42.4 %collective-permute-start.12 = (bf16[512,2048]{1,0:T(8,128)(2,1)S(1)}, bf16[512,2048]{1,0:T(8,128)(2,1)S(1)}, u32[]{:S(2)}, u32[]{:S(2)}) collective-permute-start(bf16[512,2048]{1,0:T(8,128)(2,1)S(1)} %shard_map.363), channel_id=1, source_target_pairs={{0,1},{1,0},{2,3},{3,2},{4,5},{5,4},{6,7},{7,6},{8,9},{9,8},{10,11... | collective-permute-start | bytes 6291464 | tf_op jit(solution)/shard_map/ppermute | solution.py:337
  201.7 22.4 %collective-permute-start.40 = (bf16[256,1024]{1,0:T(8,128)(2,1)S(1)}, bf16[256,1024]{1,0:T(8,128)(2,1)S(1)}, u32[]{:S(2)}, u32[]{:S(2)}) collective-permute-start(bf16[256,1024]{1,0:T(8,128)(2,1)S(1)} %collective-permute-done.39), channel_id=1, source_target_pairs={{0,2},{2,0},{4,6},{6,4},{8,10},{10,8},{12,14},{14,12},{16,18},{18,... | collective-permute-start | bytes 1572872 | tf_op jit(solution)/shard_map/ppermute | solution.py:241
  202.7 20.5 %collective-permute-start.27 = (bf16[256,1024]{1,0:T(8,128)(2,1)S(1)}, bf16[256,1024]{1,0:T(8,128)(2,1)S(1)}, u32[]{:S(2)}, u32[]{:S(2)}) collective-permute-start(bf16[256,1024]{1,0:T(8,128)(2,1)S(1)} %collective-permute-done.25), channel_id=1, source_target_pairs={{8,0},{10,2},{16,8},{18,10},{24,16},{26,18},{28,24},{30,26},{20,28... | collective-permute-start | bytes 1572872 | tf_op jit(solution)/shard_map/ppermute | solution.py:202
  (53 other events, 1243.6 us)

commit v2 on v1

v2 whole, which is shorter than its diff:
```python
import functools

import jax
import jax.numpy as jnp
from jax import lax
from jax.experimental import pallas as pl
from jax.experimental.pallas import tpu as pltpu
from jax.sharding import PartitionSpec as P

F32 = jnp.float32
BF16 = jnp.bfloat16
LOW = -1e30
PARTS = 4
LANES = 128
TAIL = 16


def full_spec():
    return pl.BlockSpec(memory_space=pltpu.VMEM)


def smem_spec():
    return pl.BlockSpec(memory_space=pltpu.SMEM)


def column(row):
    return jnp.transpose(jnp.broadcast_to(row, (8, row.shape[1])))[:, :1]


def split_terms(x):
    high = x.astype(BF16).astype(F32)
    mid = (x - high).astype(BF16).astype(F32)
    return high, mid, x - high - mid


def write_tail(ref, index, norm, top, log):
    key_size = ref.shape[-2] - TAIL
    rows = key_size // LANES
    row = lax.broadcasted_iota(jnp.int32, (TAIL, LANES), 0)
    lane = lax.broadcasted_iota(jnp.int32, (TAIL, LANES), 1)
    tail = jnp.zeros((TAIL, LANES), F32)
    high = norm.astype(BF16).astype(F32)
    for i in range(rows):
        tail = jnp.where(row == i, high[i : i + 1], tail)
        tail = jnp.where(row == rows + i, (norm - high)[i : i + 1], tail)
    for i, term in enumerate(split_terms(top) + split_terms(log)):
        tail = jnp.where((row == 2 * rows) & (lane == i), term, tail)
    ref[(*index, pl.ds(key_size, TAIL))] = tail.astype(BF16)


def read_tail(ref, index):
    key_size = ref.shape[-2] - TAIL
    rows = key_size // LANES
    tail = ref[(*index, pl.ds(key_size, TAIL))].astype(F32)
    last = tail[2 * rows : 2 * rows + 1]
    term = lambda i: last[:, i : i + 1]
    norm = tail[:rows] + tail[rows : 2 * rows]
    return norm, term(0) + term(1) + term(2), term(3) + term(4) + term(5)


def read_memory(ref, index):
    return ref[(*index, pl.ds(0, ref.shape[-2] - TAIL))].astype(F32)


def write_message(ref, index, memory, norm, top, log):
    ref[(*index, pl.ds(0, memory.shape[0]))] = memory.astype(BF16)
    write_tail(ref, index, norm, top, log)


def summary_kernel(place_ref, k_ref, v_ref, in_ref, forget_ref, *refs):
    c_refs, g_ref = refs[:1], refs[1]
    c_ref = c_refs[0]
    heads, length = in_ref.shape
    key_size = k_ref.shape[1] // heads
    value_size = v_ref.shape[1] // heads
    width = value_size // PARTS
    x = forget_ref[...]
    lf = jnp.minimum(x, 0.0) - jnp.log1p(jnp.exp(-jnp.abs(x)))
    upto = (
        lax.broadcasted_iota(jnp.int32, (length, length), 0)
        <= lax.broadcasted_iota(jnp.int32, (length, length), 1)
    ).astype(F32)
    g = jnp.dot(lf, upto, precision=lax.Precision.HIGHEST, preferred_element_type=F32)
    g_ref[...] = g
    total = g[:, length - 1 :]
    e = total - g + in_ref[...]
    top = jnp.max(e, axis=1, keepdims=True)
    scale = jnp.exp(e - top) * (key_size**-0.5)
    place = place_ref[0]
    for h in range(heads):
        weighted = (
            k_ref[:, h * key_size : (h + 1) * key_size].astype(F32) * column(scale[h : h + 1])
        ).astype(BF16)
        flat = jnp.sum(weighted.astype(F32), axis=0, keepdims=True)
        norm = jnp.concatenate(
            [flat[:, i : i + LANES] for i in range(0, key_size, LANES)], axis=0
        )
        memory = lax.dot_general(
            weighted,
            v_ref[:, h * value_size : (h + 1) * value_size],
            (((0,), (0,)), ((), ())),
            preferred_element_type=F32,
        )
        for c in range(PARTS):
            write_message(
                c_ref,
                (lax.bitwise_xor(place, c), h),
                memory[:, c * width : (c + 1) * width],
                norm,
                top[h : h + 1],
                total[h : h + 1],
            )


def summarize(place, keys, values, gate_in, gate_forget):
    heads, length = gate_in.shape
    key_size = keys.shape[1] // heads
    value_size = values.shape[1] // heads
    return pl.pallas_call(
        summary_kernel,
        out_shape=(
            jax.ShapeDtypeStruct((PARTS, heads, key_size + TAIL, value_size // PARTS), BF16),
            jax.ShapeDtypeStruct((heads, length), F32),
        ),
        in_specs=[smem_spec()] + [full_spec()] * 4,
        out_specs=(full_spec(), full_spec()),
        compiler_params=pltpu.CompilerParams(vmem_limit_bytes=40 * 1024 * 1024),
    )(place, keys, values, gate_in, gate_forget)


def plane_kernel(place_ref, *refs):
    got, out_ref = refs[:PARTS], refs[PARTS]
    at = [lax.bitwise_xor(place_ref[0], r) for r in range(PARTS)]
    for h in range(out_ref.shape[0]):
        tails = [read_tail(ref, (h,)) for ref in got]
        logs = []
        for r in range(PARTS):
            log = tails[r][1]
            for c in range(PARTS):
                log = log + jnp.where(at[c] > at[r], tails[c][2], 0.0)
            logs.append(log)
        top = functools.reduce(jnp.maximum, logs)
        factors = [jnp.exp(log - top) for log in logs]
        write_message(
            out_ref,
            (h,),
            sum(f * read_memory(ref, (h,)) for f, ref in zip(factors, got)),
            sum(f * t[0] for f, t in zip(factors, tails)),
            top,
            sum(t[2] for t in tails),
        )


def pair_up(first, second, first_there, second_there):
    norm_one, top_one, log_one = first
    norm_two, top_two, log_two = second
    top_one = jnp.where(first_there, top_one, LOW)
    top_two = jnp.where(second_there, top_two, LOW)
    log_one = jnp.where(first_there, log_one, 0.0)
    log_two = jnp.where(second_there, log_two, 0.0)
    top = jnp.maximum(top_one + log_two, top_two)
    one, two = jnp.exp(top_one + log_two - top), jnp.exp(top_two - top)
    return one, two, (one * norm_one + two * norm_two, top, log_one + log_two)


def window_kernel(there_ref, one_ref, two_ref, out_ref):
    for h in range(out_ref.shape[0]):
        one, two, tail = pair_up(
            read_tail(one_ref, (h,)),
            read_tail(two_ref, (h,)),
            there_ref[0] > 0,
            there_ref[1] > 0,
        )
        write_message(
            out_ref,
            (h,),
            one * read_memory(one_ref, (h,)) + two * read_memory(two_ref, (h,)),
            *tail,
        )


def carry_kernel(place_ref, there_ref, one_ref, two_ref, *refs):
    got, outs = refs[:PARTS], refs[PARTS:]
    at = [lax.bitwise_xor(place_ref[0], r) for r in range(PARTS)]
    for h in range(one_ref.shape[0]):
        one, two, (norm, top, _) = pair_up(
            read_tail(one_ref, (h,)),
            read_tail(two_ref, (h,)),
            there_ref[0] > 0,
            there_ref[1] > 0,
        )
        memory = one * read_memory(one_ref, (h,)) + two * read_memory(two_ref, (h,))
        tails = [read_tail(ref, (h,)) for ref in got]
        for r in range(PARTS):
            base = top
            logs = []
            for c in range(PARTS):
                base = base + jnp.where(at[c] < at[r], tails[c][2], 0.0)
                log = tails[c][1]
                for b in range(PARTS):
                    log = log + jnp.where(
                        (at[b] > at[c]) & (at[b] < at[r]), tails[b][2], 0.0
                    )
                logs.append(jnp.where(at[c] < at[r], log, LOW))
            best = functools.reduce(jnp.maximum, logs, base)
            factor = jnp.exp(base - best)
            shares = [
                jnp.where(at[c] < at[r], jnp.exp(logs[c] - best), 0.0) for c in range(PARTS)
            ]
            write_message(
                outs[r],
                (h,),
                factor * memory + sum(f * read_memory(ref, (h,)) for f, ref in zip(shares, got)),
                factor * norm + sum(f * t[0] for f, t in zip(shares, tails)),
                best,
                jnp.zeros_like(best),
            )


def small_call(kernel, scalars, messages, count):
    shape = jax.ShapeDtypeStruct(messages[0].shape, BF16)
    return pl.pallas_call(
        kernel,
        out_shape=(shape,) * count,
        in_specs=[smem_spec()] * len(scalars) + [full_spec()] * len(messages),
        out_specs=(full_spec(),) * count,
        compiler_params=pltpu.CompilerParams(vmem_limit_bytes=40 * 1024 * 1024),
    )(*scalars, *messages)


def intra_kernel(q_ref, k_ref, v_ref, in_ref, g_ref, part_ref, stat_ref):
    length, key_size = q_ref.shape
    g_row = g_ref[0]
    g_col = column(g_row)
    row = lax.broadcasted_iota(jnp.int32, (length, length), 0)
    col = lax.broadcasted_iota(jnp.int32, (length, length), 1)
    causal = row >= col
    log_weight = jnp.where(causal, g_col - g_row + in_ref[0], LOW)
    row_top = jnp.max(log_weight, axis=1, keepdims=True)
    scores = lax.dot_general(
        q_ref[...], k_ref[...], (((1,), (1,)), ((), ())), preferred_element_type=F32
    ) * (key_size**-0.5)
    weights = jnp.where(causal, jnp.exp(log_weight - row_top) * scores, 0.0)
    part_ref[...] = jnp.dot(weights.astype(BF16), v_ref[...], preferred_element_type=F32)
    lane = lax.broadcasted_iota(jnp.int32, (length, LANES), 1)
    total = jnp.sum(weights, axis=1, keepdims=True)
    stat_ref[0] = jnp.where(lane == 0, row_top, jnp.where(lane == 1, total, g_col))


def intra(queries, keys, values, gate_in, g):
    heads, length = gate_in.shape
    key_size = keys.shape[1] // heads
    value_size = values.shape[1] // heads
    per_head = lambda r, w: pl.BlockSpec((1, r, w), lambda h: (h, 0, 0))
    return pl.pallas_call(
        intra_kernel,
        grid=(heads,),
        out_shape=(
            jax.ShapeDtypeStruct((length, heads * value_size), F32),
            jax.ShapeDtypeStruct((heads, length, LANES), F32),
        ),
        in_specs=[
            pl.BlockSpec((length, key_size), lambda h: (0, h)),
            pl.BlockSpec((length, key_size), lambda h: (0, h)),
            pl.BlockSpec((length, value_size), lambda h: (0, h)),
            per_head(1, length),
            per_head(1, length),
        ],
        out_specs=(
            pl.BlockSpec((length, value_size), lambda h: (0, h)),
            per_head(length, LANES),
        ),
        compiler_params=pltpu.CompilerParams(vmem_limit_bytes=40 * 1024 * 1024),
    )(queries, keys, values, gate_in[:, None], g[:, None])


def join_kernel(place_ref, q_ref, *refs):
    pieces, (part_ref, stat_ref), outs = refs[:PARTS], refs[PARTS : PARTS + 2], refs[PARTS + 2 : -1]
    mem_ref = refs[-1]
    width = pieces[0].shape[-1]
    for r in range(PARTS):
        at = pl.multiple_of(lax.bitwise_xor(place_ref[0], r) * width, width)
        mem_ref[:, pl.ds(at, width)] = pieces[r][0, : mem_ref.shape[0]]
    norm, carry_top, _ = read_tail(pieces[0], (0,))
    flat = jnp.concatenate([norm[i : i + 1] for i in range(norm.shape[0])], axis=1)
    q = q_ref[...]
    inter = jnp.dot(q, mem_ref[...], preferred_element_type=F32)
    carried = jnp.sum(q.astype(F32) * flat, axis=1, keepdims=True)
    stat = stat_ref[0]
    own_top, own_sum, carry_log = stat[:, :1], stat[:, 1:2], carry_top + stat[:, 2:3]
    row_top = jnp.maximum(carry_log, own_top)
    factor, own = jnp.exp(carry_log - row_top), jnp.exp(own_top - row_top)
    denom = factor * carried + own * own_sum
    inverse = 1.0 / jnp.maximum(jnp.abs(denom), 1.0)
    result = ((factor * inverse) * inter + (own * inverse) * part_ref[...]).astype(BF16)
    rows = outs[0].shape[0]
    for i, out in enumerate(outs):
        out[...] = result[i * rows : (i + 1) * rows]


def join(place, queries, carries, part, stat, chunks):
    heads, rows, width = carries[0].shape
    key_size = rows - TAIL
    length = queries.shape[0]
    value_size = width * PARTS
    piece = length // chunks
    return pl.pallas_call(
        join_kernel,
        grid=(heads,),
        out_shape=(jax.ShapeDtypeStruct((piece, heads * value_size), BF16),) * chunks,
        in_specs=[smem_spec(), pl.BlockSpec((length, key_size), lambda h: (0, h))]
        + [pl.BlockSpec((1, rows, width), lambda h: (h, 0, 0))] * PARTS
        + [
            pl.BlockSpec((length, value_size), lambda h: (0, h)),
            pl.BlockSpec((1, length, LANES), lambda h: (h, 0, 0)),
        ],
        out_specs=(pl.BlockSpec((piece, value_size), lambda h: (0, h)),) * chunks,
        scratch_shapes=[pltpu.VMEM((key_size, value_size), BF16)],
        compiler_params=pltpu.CompilerParams(vmem_limit_bytes=40 * 1024 * 1024),
    )(place, queries, *carries, part, stat)


def project_kernel(count, *refs):
    ops, w_ref, out_ref = refs[:count], refs[count], refs[count + 1]
    at, total = 0, None
    for a in ops:
        term = jnp.dot(
            a[...], w_ref[at : at + a.shape[1]], preferred_element_type=F32
        )
        total = term if total is None else total + term
        at += a.shape[1]
    out_ref[...] = total.astype(BF16)


def project(operands, weight, block=256):
    rows, cols = operands[0].shape[0], weight.shape[1]
    block = min(block, cols)
    depth = weight.shape[0]
    return pl.pallas_call(
        functools.partial(project_kernel, len(operands)),
        grid=(cols // block,),
        out_shape=jax.ShapeDtypeStruct((rows, cols), BF16),
        in_specs=[pl.BlockSpec(a.shape, lambda i: (0, 0)) for a in operands]
        + [pl.BlockSpec((depth, block), lambda i: (0, i))],
        out_specs=pl.BlockSpec((rows, block), lambda i: (0, i)),
        compiler_params=pltpu.CompilerParams(vmem_limit_bytes=40 * 1024 * 1024),
        cost_estimate=pl.CostEstimate(
            flops=2 * rows * cols * depth,
            bytes_accessed=2 * (rows * depth + depth * cols + rows * cols),
            transcendentals=0,
        ),
    )(*operands, weight)


def xor_perm(n, d):
    return [(i, i ^ d) for i in range(n)]


def ring_perms(n):
    pairs = n // 2
    order = list(range(0, pairs, 2)) + list(range(1, pairs, 2))[::-1]
    fwd = [
        (2 * order[r] + x, 2 * order[(r + 1) % pairs] + x) for r in range(pairs) for x in (0, 1)
    ]
    return order, fwd, [(d, s) for s, d in fwd]


def ring(piece, n):
    _, fwd, bwd = ring_perms(n)
    count = n // 2
    got = {0: piece}
    f = b = piece
    for t in range(1, (count - 1) // 2 + 1):
        f = lax.ppermute(f, "seq", fwd)
        b = lax.ppermute(b, "seq", bwd)
        got[t], got[-t] = f, b
    half = piece.shape[0] // 2
    got[count // 2] = (
        lax.ppermute(f[:half], "seq", fwd),
        lax.ppermute(b[half:], "seq", bwd),
    )
    return got


def gather_weight(weight, n, first):
    rows, cols = weight.shape
    me = lax.axis_index("seq")
    order, _, _ = ring_perms(n)
    count = len(order)
    where = [order.index(q) for q in range(count)]
    here = jnp.array(where)[me // 2]
    side = me % 2
    share = cols // 2
    mine = lax.dynamic_slice_in_dim(weight, side * share, share, 1)
    theirs = lax.dynamic_slice_in_dim(weight, (1 - side) * share, share, 1)
    other = lax.ppermute(theirs, "seq", xor_perm(n, 1))
    full = jnp.zeros((n * rows, share), weight.dtype)
    for flip, piece in ((False, mine), (True, other)):
        for d, a in ring(piece, n).items():
            src = jnp.array(order)[(here - d) % count]
            at = (2 * src + (1 - side if flip else side)) * rows - first
            at = jnp.where(at < 0, at + n * rows, at)
            for p in a if isinstance(a, tuple) else (a,):
                full = lax.dynamic_update_slice(full, p, (at, 0))
                at = at + p.shape[0]
    return full


def body(queries, keys, values, input_gate, forget_gate, out_weight, n, n_head):
    me = lax.axis_index("seq")
    place = (me % PARTS).astype(jnp.int32)[None]
    level = (me // PARTS).astype(jnp.int32)
    memory, g = summarize(place, keys, values, input_gate, forget_gate)
    got = [memory[0]] + [
        lax.ppermute(memory[r], "seq", xor_perm(n, r)) for r in range(1, PARTS)
    ]
    (window,) = small_call(plane_kernel, (place,), got, 1)
    levels = n // PARTS
    d, earlier, there = 1, None, None
    while d < levels:
        step = d * PARTS
        come = lax.ppermute(window, "seq", [(s, s + step) for s in range(n - step)])
        here = (level >= d).astype(jnp.int32)
        one = jnp.ones_like(here)
        if earlier is None:
            earlier, there = come, here
            if 2 * d >= levels:
                come, here = jnp.zeros_like(come), jnp.zeros_like(here)
        elif 2 * d < levels:
            (earlier,) = small_call(window_kernel, (jnp.stack([here, there]),), (come, earlier), 1)
            there = one
        if 2 * d < levels:
            (window,) = small_call(window_kernel, (jnp.stack([here, one]),), (come, window), 1)
        d *= 2
    carries = small_call(
        carry_kernel, (place, jnp.stack([here, there])), (come, earlier, *got), PARTS
    )
    carries = [carries[0]] + [
        lax.ppermute(carries[r], "seq", xor_perm(n, r)) for r in range(1, PARTS)
    ]
    part, stat = intra(queries, keys, values, input_gate, g)
    chunks = 4
    hidden = join(place, queries, carries, part, stat, chunks)

    if n_head == 2:
        first = lax.axis_index("head") * (n * out_weight.shape[0] // 2)
    else:
        first = 0
    weight = gather_weight(out_weight, n, first)

    def all_heads(a):
        if n_head == 2:
            return [a, lax.ppermute(a, "head", [(0, 1), (1, 0)])]
        return [lax.all_gather(a, "head", axis=1, tiled=True)]

    sent = [lax.ppermute(a, "seq", xor_perm(n, 1)) for a in hidden]
    share = weight.shape[1]
    side = me % 2
    rows = hidden[0].shape[0]
    mixed = jnp.zeros((queries.shape[0], 2 * share), BF16)
    for i, a in enumerate(hidden):
        mixed = lax.dynamic_update_slice(
            mixed, project(all_heads(a), weight), (i * rows, side * share)
        )
    for i, a in enumerate(sent):
        back = lax.ppermute(project(all_heads(a), weight), "seq", xor_perm(n, 1))
        mixed = lax.dynamic_update_slice(mixed, back, (i * rows, (1 - side) * share))
    return mixed


def solution(mesh):
    return jax.shard_map(
        functools.partial(body, n=mesh.shape["seq"], n_head=mesh.shape["head"]),
        mesh=mesh,
        in_specs=(
            P("seq", "head"),
            P("seq", "head"),
            P("seq", "head"),
            P("head", "seq"),
            P("head", "seq"),
            P("seq", "head"),
        ),
        out_specs=P("seq", "head"),
        check_vma=False,
    )
```

time: 260 us -> 229 us (0.88)
  Pallas kernels: 9.09 us -> 57.4 us
  other arithmetic: 21.9 us -> 0.15 us
  between operations: 32.6 us -> 12.2 us
  starting transfers between devices: 68.1 us -> 51.5 us
  matrix products: 15.7 us -> 0 us
  local copies, waits for them, and re-layouts: 53.9 us -> 42.6 us
  waiting for transfers between devices: 57.4 us -> 63.8 us
    pallas_call x1 -> x12, Pallas kernels: 2.07 us -> 50.1 us  [the longest x8 39.7 us: project(): pl.pallas_call(functools.partial(project_kernel, len(operands)), grid=(co...]
    ppermute x3, waiting for transfers between devices: 0.01 us -> 20.5 us  [body(): lax.ppermute(memory[r], 'seq', xor_perm(n, r))]
    ppermute x2, waiting for transfers between devices: 0.01 us -> 18 us  [body(): come = lax.ppermute(window, 'seq', [(s, s + step) for s in range(n - step)])]
    dot_general x2 -> x0, matrix products: 15.7 us -> none  [body(): jnp.dot(all_heads, w, preferred_element_type=F32).astype(BF16)]
    ppermute x3, waiting for transfers between devices: 12.9 us -> 0.01 us  [body(): lax.ppermute(carries[r], 'seq', xor_perm(n, r))]
    ppermute x9 -> x6, starting transfers between devices: 23.3 us -> 11.2 us  [ring(): f = lax.ppermute(f, 'seq', fwd)]
    convert_element_type x6 -> x0, other arithmetic: 9.53 us -> none  [the longest x4 6.26 us: body(): carries.append(total.astype(BF16))]
    another operation x5 -> x0, local copies, waits for them, and re-layouts: 8.8 us -> none
  transfers between devices with their start and end apart: 47 -> 41, of which waited for: 17 -> 8; matrix products, arithmetic and copies ran while one was open for 24% -> 11% of each run, Pallas kernels for 4% -> 25%
where the time goes in v2:
time: 229 us; the launch traced here: 228 us
  waiting for transfers between devices  63.8 us (28%)
  Pallas kernels  57.4 us (25%)
  starting transfers between devices  51.5 us (22%)
  local copies, waits for them, and re-layouts  42.6 us (19%)
  between operations  12.2 us (5%)
    pallas_call x8, Pallas kernels, project(): pl.pallas_call(functools.partial(project_kernel, len(operands)), grid=(co...  39.7 us
    dynamic_update_slice x18, local copies, waits for them, and re-layouts, gather_weight(): full = lax.dynamic_update_slice(full, p, (at, 0))  24.5 us
    ppermute x3, waiting for transfers between devices, body(): lax.ppermute(memory[r], 'seq', xor_perm(n, r))  20.5 us
    ppermute x2, waiting for transfers between devices, body(): come = lax.ppermute(window, 'seq', [(s, s + step) for s in range(n - step)])  18 us
    ppermute x4, waiting for transfers between devices, body(): sent = [lax.ppermute(a, 'seq', xor_perm(n, 1)) for a in hidden]  17.5 us
    ppermute x6, starting transfers between devices, ring(): f = lax.ppermute(f, 'seq', fwd)  11.2 us
    ppermute x2, starting transfers between devices, body(): come = lax.ppermute(window, 'seq', [(s, s + step) for s in range(n - step)])  8.35 us
    ppermute x6, waiting for transfers between devices, ring(): f = lax.ppermute(f, 'seq', fwd)  7.77 us
  transfers between devices with their start and end apart: 41, of which 8 were waited for; matrix products, arithmetic and copies ran while one was open for 11% of the time, Pallas kernels for 25%

profile of v2, /device:TPU:0, one launch (start us, length us, event | category | flops | bytes accessed | tf_op | source)
XLA Modules:
  0.0 227.8 jit_solution(12068547802524430701)
XLA Ops:
  10.4 4.4 %broadcast_in_dim.19 = bf16[4096,1024]{1,0:T(8,128)(2,1)} broadcast(bf16[]{:T(256)} %constant.140.clone.1), dimensions={} | broadcast | bytes 8388610 | tf_op jit(solution)/shard_map/broadcast_in_dim | solution.py:397
  16.0 3.1 %collective-permute-start.9 = (bf16[256,1024]{1,0:T(8,128)(2,1)}, bf16[256,1024]{1,0:T(8,128)(2,1)}, u32[]{:S(2)}, u32[]{:S(2)}) collective-permute-start(bf16[256,1024]{1,0:T(8,128)(2,1)} %get-tuple-element.30), channel_id=1, source_target_pairs={{0,8},{2,10},{8,16},{10,18},{16,24},{18,26},{24,28},{26,30},{28,20... | collective-permute-start | bytes 1572872 | tf_op jit(solution)/shard_map/ppermute | solution.py:374
  23.5 7.8 %collective-permute-done.9 = bf16[256,1024]{1,0:T(8,128)(2,1)} collective-permute-done((bf16[256,1024]{1,0:T(8,128)(2,1)}, bf16[256,1024]{1,0:T(8,128)(2,1)}, u32[]{:S(2)}, u32[]{:S(2)}) %collective-permute-start.9) | collective-permute-done | bytes 524320 | tf_op jit(solution)/shard_map/ppermute | solution.py:374
  33.3 2.7 %collective-permute-start.2 = (bf16[4,272,128]{2,1,0:T(8,128)(2,1)S(1)}, bf16[4,272,128]{2,1,0:T(8,128)(2,1)S(1)}, u32[]{:S(2)}, u32[]{:S(2)}) collective-permute-start(bf16[4,272,128]{2,1,0:T(8,128)(2,1)S(1)} %get-tuple-element.31), channel_id=1, source_target_pairs={{0,6},{2,4},{4,2},{6,0},{8,14},{10,12},{12,10},{14,8},{16,22},{18,... | collective-permute-start | bytes 835592 | tf_op jit(solution)/shard_map/ppermute | solution.py:415
  36.0 20.5 %collective-permute-done.1.refs_2_ = bf16[4,272,128]{2,1,0:T(8,128)(2,1)S(1)} collective-permute-done((bf16[4,272,128]{2,1,0:T(8,128)(2,1)S(1)}, bf16[4,272,128]{2,1,0:T(8,128)(2,1)S(1)}, u32[]{:S(2)}, u32[]{:S(2)}) %collective-permute-start.1) | collective-permute-done | bytes 278560 | tf_op jit(solution)/shard_map/ppermute | solution.py:415
  64.2 2.9 %collective-permute-done.3.one_ref.two_ref = bf16[4,272,128]{2,1,0:T(8,128)(2,1)} collective-permute-done((bf16[4,272,128]{2,1,0:T(8,128)(2,1)}, bf16[4,272,128]{2,1,0:T(8,128)(2,1)}, u32[]{:S(2)}, u32[]{:S(2)}) %collective-permute-start.3) | collective-permute-done | bytes 278560 | tf_op jit(solution)/shard_map/ppermute | solution.py:422
  69.2 6.4 %collective-permute-start.4 = (bf16[4,272,128]{2,1,0:T(8,128)(2,1)}, bf16[4,272,128]{2,1,0:T(8,128)(2,1)}, u32[]{:S(2)}, u32[]{:S(2)}) collective-permute-start(bf16[4,272,128]{2,1,0:T(8,128)(2,1)} %shard_map.219), channel_id=1, source_target_pairs={{0,16},{2,18},{4,20},{6,22},{8,24},{10,26},{12,28},{14,30},{1,17},... | collective-permute-start | bytes 835592 | tf_op jit(solution)/shard_map/ppermute | solution.py:422
  75.5 2.5 %collective-permute-start.19 = (bf16[256,1024]{1,0:T(8,128)(2,1)}, bf16[256,1024]{1,0:T(8,128)(2,1)}, u32[]{:S(2)}, u32[]{:S(2)}) collective-permute-start(bf16[256,1024]{1,0:T(8,128)(2,1)} %collective-permute-done.17), channel_id=1, source_target_pairs={{8,0},{10,2},{16,8},{18,10},{24,16},{26,18},{28,24},{30,26},{20,28... | collective-permute-start | bytes 1572872 | tf_op jit(solution)/shard_map/ppermute | solution.py:375
  78.1 15.1 %collective-permute-done.4.one_ref = bf16[4,272,128]{2,1,0:T(8,128)(2,1)} collective-permute-done((bf16[4,272,128]{2,1,0:T(8,128)(2,1)}, bf16[4,272,128]{2,1,0:T(8,128)(2,1)}, u32[]{:S(2)}, u32[]{:S(2)}) %collective-permute-start.4) | collective-permute-done | bytes 278560 | tf_op jit(solution)/shard_map/ppermute | solution.py:422
  96.1 3.2 %shard_map.220 = (bf16[4,272,128]{2,1,0:T(8,128)(2,1)S(1)}, bf16[4,272,128]{2,1,0:T(8,128)(2,1)}, bf16[4,272,128]{2,1,0:T(8,128)(2,1)}, bf16[4,272,128]{2,1,0:T(8,128)(2,1)S(1)}) custom-call(s32[1]{0:T(128)} %bitcast.place_ref, s32[2]{0:T(128)S(1)} %pad_add_fusion.there_ref, bf16[4,272,128]{2,1,0:T(8,128)(2,1)} %collective-permute-done.4.one_ref, ...), custom_call_target="tpu_custom_call" | custom-call | tf_op jit(solution)/shard_map/pallas_call | solution.py:222
  109.6 5.1 %shard_map.221 = (f32[512,2048]{1,0:T(8,128)S(1)}, f32[4,512,128]{2,1,0:T(8,128)S(1)}) custom-call(bf16[512,1024]{1,0:T(8,128)(2,1)S(1)} %copy-done.2, bf16[512,1024]{1,0:T(8,128)(2,1)S(1)} %copy-done.1, bf16[512,2048]{1,0:T(8,128)(2,1)S(1)} %copy-done, f32[4,1,512]{2,1,0:T(1,128)S(1)} %broadcast_in_dim.17.in_ref, f32[4,1,512]{2,1,0:T(1,128)S(1)} %broadcast_in_dim.18.g_ref), custom_call_target="tpu_custom_call" | custom-call | tf_op jit(solution)/shard_map/pallas_call | solution.py:255
  116.6 3.9 %collective-permute-start.7 = (bf16[4,272,128]{2,1,0:T(8,128)(2,1)}, bf16[4,272,128]{2,1,0:T(8,128)(2,1)S(1)}, u32[]{:S(2)}, u32[]{:S(2)}) collective-permute-start(bf16[4,272,128]{2,1,0:T(8,128)(2,1)} %copy-done.14), channel_id=1, source_target_pairs={{0,6},{2,4},{4,2},{6,0},{8,14},{10,12},{12,10},{14,8},{16,22},{18,... | collective-permute-start | bytes 835592 | tf_op jit(solution)/shard_map/ppermute | solution.py:439
  131.2 4.0 %shard_map.222 = (bf16[128,2048]{1,0:T(8,128)(2,1)S(1)}, bf16[128,2048]{1,0:T(8,128)(2,1)S(1)}, bf16[128,2048]{1,0:T(8,128)(2,1)S(1)}, bf16[128,2048]{1,0:T(8,128)(2,1)S(1)}) custom-call(s32[1]{0:T(128)} %bitcast.place_ref, bf16[512,1024]{1,0:T(8,128)(2,1)S(1)} %copy-done.3, bf16[4,272,128]{2,1,0:T(8,128)(2,1)S(1)} %copy-done.11, ...), custom_call_target="tpu_custom_call" | custom-call | tf_op jit(solution)/shard_map/pallas_call | solution.py:307
  153.5 7.8 %collective-permute-done.35.refs_0_ = bf16[128,2048]{1,0:T(8,128)(2,1)S(1)} collective-permute-done((bf16[128,2048]{1,0:T(8,128)(2,1)S(1)}, bf16[128,2048]{1,0:T(8,128)(2,1)S(1)}, u32[]{:S(2)}, u32[]{:S(2)}) %collective-permute-start.35) | collective-permute-done | bytes 524320 | tf_op jit(solution)/shard_map/ppermute | solution.py:456
  167.5 4.1 %collective-permute-done.32.refs_0_ = bf16[128,2048]{1,0:T(8,128)(2,1)S(1)} collective-permute-done((bf16[128,2048]{1,0:T(8,128)(2,1)S(1)}, bf16[128,2048]{1,0:T(8,128)(2,1)S(1)}, u32[]{:S(2)}, u32[]{:S(2)}) %collective-permute-start.32) | collective-permute-done | bytes 524320 | tf_op jit(solution)/shard_map/ppermute | solution.py:456
  172.5 4.7 %collective-permute-done.29.refs_0_ = bf16[128,2048]{1,0:T(8,128)(2,1)S(1)} collective-permute-done((bf16[128,2048]{1,0:T(8,128)(2,1)S(1)}, bf16[128,2048]{1,0:T(8,128)(2,1)S(1)}, u32[]{:S(2)}, u32[]{:S(2)}) %collective-permute-start.29) | collective-permute-done | bytes 524320 | tf_op jit(solution)/shard_map/ppermute | solution.py:456
  180.6 4.9 %shard_map.230 = bf16[128,1024]{1,0:T(8,128)(2,1)S(1)} custom-call(bf16[128,2048]{1,0:T(8,128)(2,1)S(1)} %collective-permute-done.38.refs_0_, bf16[128,2048]{1,0:T(8,128)(2,1)S(1)} %collective-permute-done.39.refs_1_, bf16[4096,1024]{1,0:T(8,128)(2,1)} %constant_dynamic-update-slice_fusion.2.refs_2_), custom_call_target="tpu_custom_call" | custom-call | flops 1073741824 | bytes 9699328 | tf_op jit(solution)/shard_map/pallas_call | solution.py:339
  185.6 5.0 %shard_map.229 = bf16[128,1024]{1,0:T(8,128)(2,1)S(1)} custom-call(bf16[128,2048]{1,0:T(8,128)(2,1)S(1)} %collective-permute-done.35.refs_0_, bf16[128,2048]{1,0:T(8,128)(2,1)S(1)} %collective-permute-done.36.refs_1_, bf16[4096,1024]{1,0:T(8,128)(2,1)} %constant_dynamic-update-slice_fusion.2.refs_2_), custom_call_target="tpu_custom_call" | custom-call | flops 1073741824 | bytes 9699328 | tf_op jit(solution)/shard_map/pallas_call | solution.py:339
  191.0 5.0 %shard_map.228 = bf16[128,1024]{1,0:T(8,128)(2,1)S(1)} custom-call(bf16[128,2048]{1,0:T(8,128)(2,1)S(1)} %collective-permute-done.32.refs_0_, bf16[128,2048]{1,0:T(8,128)(2,1)S(1)} %collective-permute-done.33.refs_1_, bf16[4096,1024]{1,0:T(8,128)(2,1)} %constant_dynamic-update-slice_fusion.2.refs_2_), custom_call_target="tpu_custom_call" | custom-call | flops 1073741824 | bytes 9699328 | tf_op jit(solution)/shard_map/pallas_call | solution.py:339
  197.2 5.0 %shard_map.227 = bf16[128,1024]{1,0:T(8,128)(2,1)S(1)} custom-call(bf16[128,2048]{1,0:T(8,128)(2,1)S(1)} %collective-permute-done.29.refs_0_, bf16[128,2048]{1,0:T(8,128)(2,1)S(1)} %collective-permute-done.30.refs_1_, bf16[4096,1024]{1,0:T(8,128)(2,1)} %constant_dynamic-update-slice_fusion.2.refs_2_), custom_call_target="tpu_custom_call" | custom-call | flops 1073741824 | bytes 9699328 | tf_op jit(solution)/shard_map/pallas_call | solution.py:339
  203.2 4.9 %shard_map.225 = bf16[128,1024]{1,0:T(8,128)(2,1)S(1)} custom-call(bf16[128,2048]{1,0:T(8,128)(2,1)S(1)} %get-tuple-element.27.refs_0_, bf16[128,2048]{1,0:T(8,128)(2,1)S(1)} %collective-permute-done.27.refs_1_, bf16[4096,1024]{1,0:T(8,128)(2,1)} %constant_dynamic-update-slice_fusion.2.refs_2_), custom_call_target="tpu_custom_call" | custom-call | flops 1073741824 | bytes 9699328 | tf_op jit(solution)/shard_map/pallas_call | solution.py:339
  209.4 4.9 %shard_map.224 = bf16[128,1024]{1,0:T(8,128)(2,1)S(1)} custom-call(bf16[128,2048]{1,0:T(8,128)(2,1)S(1)} %get-tuple-element.26.refs_0_, bf16[128,2048]{1,0:T(8,128)(2,1)S(1)} %collective-permute-done.26.refs_1_, bf16[4096,1024]{1,0:T(8,128)(2,1)} %constant_dynamic-update-slice_fusion.2.refs_2_), custom_call_target="tpu_custom_call" | custom-call | flops 1073741824 | bytes 9699328 | tf_op jit(solution)/shard_map/pallas_call | solution.py:339
  215.3 4.9 %shard_map.223 = bf16[128,1024]{1,0:T(8,128)(2,1)S(1)} custom-call(bf16[128,2048]{1,0:T(8,128)(2,1)S(1)} %get-tuple-element.25.refs_0_, bf16[128,2048]{1,0:T(8,128)(2,1)S(1)} %collective-permute-done.8.refs_1_, bf16[4096,1024]{1,0:T(8,128)(2,1)} %constant_dynamic-update-slice_fusion.2.refs_2_), custom_call_target="tpu_custom_call" | custom-call | flops 1073741824 | bytes 9699328 | tf_op jit(solution)/shard_map/pallas_call | solution.py:339
  220.6 5.0 %shard_map.226 = bf16[128,1024]{1,0:T(8,128)(2,1)S(1)} custom-call(bf16[128,2048]{1,0:T(8,128)(2,1)S(1)} %get-tuple-element.28.refs_0_, bf16[128,2048]{1,0:T(8,128)(2,1)S(1)} %collective-permute-done.28.refs_1_, bf16[4096,1024]{1,0:T(8,128)(2,1)} %constant_dynamic-update-slice_fusion.2.refs_2_), custom_call_target="tpu_custom_call" | custom-call | flops 1073741824 | bytes 9699328 | tf_op jit(solution)/shard_map/pallas_call | solution.py:339
  (145 shorter events, 77.9 us)
Async XLA Ops:
  23.0 37.5 %collective-permute-start.10 = (bf16[256,1024]{1,0:T(8,128)(2,1)}, bf16[256,1024]{1,0:T(8,128)(2,1)}, u32[]{:S(2)}, u32[]{:S(2)}) collective-permute-start(bf16[256,1024]{1,0:T(8,128)(2,1)} %get-tuple-element.30), channel_id=1, source_target_pairs={{8,0},{10,2},{16,8},{18,10},{24,16},{26,18},{28,24},{30,26},{20,28... | collective-permute-start | bytes 1572872 | tf_op jit(solution)/shard_map/ppermute | solution.py:375
  23.4 37.0 %collective-permute-start.17 = (bf16[256,1024]{1,0:T(8,128)(2,1)}, bf16[256,1024]{1,0:T(8,128)(2,1)}, u32[]{:S(2)}, u32[]{:S(2)}) collective-permute-start(bf16[256,1024]{1,0:T(8,128)(2,1)} %get-tuple-element.35), channel_id=1, source_target_pairs={{0,2},{2,0},{4,6},{6,4},{8,10},{10,8},{12,14},{14,12},{16,18},{18,... | collective-permute-start | bytes 1572872 | tf_op jit(solution)/shard_map/ppermute | solution.py:396
  31.2 31.2 %collective-permute-start.11 = (bf16[256,1024]{1,0:T(8,128)(2,1)}, bf16[256,1024]{1,0:T(8,128)(2,1)}, u32[]{:S(2)}, u32[]{:S(2)}) collective-permute-start(bf16[256,1024]{1,0:T(8,128)(2,1)} %collective-permute-done.9), channel_id=1, source_target_pairs={{0,8},{2,10},{8,16},{10,18},{16,24},{18,26},{24,28},{26,30},{28,20... | collective-permute-start | bytes 1572872 | tf_op jit(solution)/shard_map/ppermute | solution.py:374
  33.1 23.5 %collective-permute-start.1 = (bf16[4,272,128]{2,1,0:T(8,128)(2,1)S(1)}, bf16[4,272,128]{2,1,0:T(8,128)(2,1)S(1)}, u32[]{:S(2)}, u32[]{:S(2)}) collective-permute-start(bf16[4,272,128]{2,1,0:T(8,128)(2,1)S(1)} %get-tuple-element.32), channel_id=1, source_target_pairs={{0,4},{2,6},{4,0},{6,2},{8,12},{10,14},{12,8},{14,10},{16,20},{18,... | collective-permute-start | bytes 835592 | tf_op jit(solution)/shard_map/ppermute | solution.py:415
  33.3 23.2 %collective-permute-start.2 = (bf16[4,272,128]{2,1,0:T(8,128)(2,1)S(1)}, bf16[4,272,128]{2,1,0:T(8,128)(2,1)S(1)}, u32[]{:S(2)}, u32[]{:S(2)}) collective-permute-start(bf16[4,272,128]{2,1,0:T(8,128)(2,1)S(1)} %get-tuple-element.31), channel_id=1, source_target_pairs={{0,6},{2,4},{4,2},{6,0},{8,14},{10,12},{12,10},{14,8},{16,22},{18,... | collective-permute-start | bytes 835592 | tf_op jit(solution)/shard_map/ppermute | solution.py:415
  60.4 41.4 %collective-permute-start.12 = (bf16[256,1024]{1,0:T(8,128)(2,1)}, bf16[256,1024]{1,0:T(8,128)(2,1)}, u32[]{:S(2)}, u32[]{:S(2)}) collective-permute-start(bf16[256,1024]{1,0:T(8,128)(2,1)} %collective-permute-done.10), channel_id=1, source_target_pairs={{8,0},{10,2},{16,8},{18,10},{24,16},{26,18},{28,24},{30,26},{20,28... | collective-permute-start | bytes 1572872 | tf_op jit(solution)/shard_map/ppermute | solution.py:375
  60.4 41.4 %collective-permute-start.18 = (bf16[256,1024]{1,0:T(8,128)(2,1)}, bf16[256,1024]{1,0:T(8,128)(2,1)}, u32[]{:S(2)}, u32[]{:S(2)}) collective-permute-start(bf16[256,1024]{1,0:T(8,128)(2,1)} %collective-permute-done.17), channel_id=1, source_target_pairs={{0,8},{2,10},{8,16},{10,18},{16,24},{18,26},{24,28},{26,30},{28,20... | collective-permute-start | bytes 1572872 | tf_op jit(solution)/shard_map/ppermute | solution.py:374
  62.5 54.1 %collective-permute-start.13 = (bf16[256,1024]{1,0:T(8,128)(2,1)}, bf16[256,1024]{1,0:T(8,128)(2,1)}, u32[]{:S(2)}, u32[]{:S(2)}) collective-permute-start(bf16[256,1024]{1,0:T(8,128)(2,1)} %collective-permute-done.11), channel_id=1, source_target_pairs={{0,8},{2,10},{8,16},{10,18},{16,24},{18,26},{24,28},{26,30},{28,20... | collective-permute-start | bytes 1572872 | tf_op jit(solution)/shard_map/ppermute | solution.py:374
  69.2 24.0 %collective-permute-start.4 = (bf16[4,272,128]{2,1,0:T(8,128)(2,1)}, bf16[4,272,128]{2,1,0:T(8,128)(2,1)}, u32[]{:S(2)}, u32[]{:S(2)}) collective-permute-start(bf16[4,272,128]{2,1,0:T(8,128)(2,1)} %shard_map.219), channel_id=1, source_target_pairs={{0,16},{2,18},{4,20},{6,22},{8,24},{10,26},{12,28},{14,30},{1,17},... | collective-permute-start | bytes 835592 | tf_op jit(solution)/shard_map/ppermute | solution.py:422
  75.5 47.8 %collective-permute-start.19 = (bf16[256,1024]{1,0:T(8,128)(2,1)}, bf16[256,1024]{1,0:T(8,128)(2,1)}, u32[]{:S(2)}, u32[]{:S(2)}) collective-permute-start(bf16[256,1024]{1,0:T(8,128)(2,1)} %collective-permute-done.17), channel_id=1, source_target_pairs={{8,0},{10,2},{16,8},{18,10},{24,16},{26,18},{28,24},{30,26},{20,28... | collective-permute-start | bytes 1572872 | tf_op jit(solution)/shard_map/ppermute | solution.py:375
  100.7 23.2 %collective-permute-start.5 = (bf16[4,272,128]{2,1,0:T(8,128)(2,1)}, bf16[4,272,128]{2,1,0:T(8,128)(2,1)}, u32[]{:S(2)}, u32[]{:S(2)}) collective-permute-start(bf16[4,272,128]{2,1,0:T(8,128)(2,1)} %get-tuple-element.19), channel_id=1, source_target_pairs={{0,2},{2,0},{4,6},{6,4},{8,10},{10,8},{12,14},{14,12},{16,18},{18,... | collective-permute-start | bytes 835592 | tf_op jit(solution)/shard_map/ppermute | solution.py:439
  101.8 23.6 %collective-permute-start.6 = (bf16[4,272,128]{2,1,0:T(8,128)(2,1)}, bf16[4,272,128]{2,1,0:T(8,128)(2,1)}, u32[]{:S(2)}, u32[]{:S(2)}) collective-permute-start(bf16[4,272,128]{2,1,0:T(8,128)(2,1)} %get-tuple-element.20), channel_id=1, source_target_pairs={{0,4},{2,6},{4,0},{6,2},{8,12},{10,14},{12,8},{14,10},{16,20},{18,... | collective-permute-start | bytes 835592 | tf_op jit(solution)/shard_map/ppermute | solution.py:439
  101.8 35.0 %collective-permute-start.14 = (bf16[256,1024]{1,0:T(8,128)(2,1)}, bf16[256,1024]{1,0:T(8,128)(2,1)}, u32[]{:S(2)}, u32[]{:S(2)}) collective-permute-start(bf16[256,1024]{1,0:T(8,128)(2,1)} %collective-permute-done.12), channel_id=1, source_target_pairs={{8,0},{10,2},{16,8},{18,10},{24,16},{26,18},{28,24},{30,26},{20,28... | collective-permute-start | bytes 1572872 | tf_op jit(solution)/shard_map/ppermute | solution.py:375
  123.4 20.2 %collective-permute-start.20 = (bf16[256,1024]{1,0:T(8,128)(2,1)}, bf16[256,1024]{1,0:T(8,128)(2,1)S(1)}, u32[]{:S(2)}, u32[]{:S(2)}) collective-permute-start(bf16[256,1024]{1,0:T(8,128)(2,1)} %collective-permute-done.18), channel_id=1, source_target_pairs={{0,8},{2,10},{8,16},{10,18},{16,24},{18,26},{24,28},{26,30},{28,20... | collective-permute-start | bytes 1572872 | tf_op jit(solution)/shard_map/ppermute | solution.py:374
  123.9 20.5 %collective-permute-start.21 = (bf16[256,1024]{1,0:T(8,128)(2,1)}, bf16[256,1024]{1,0:T(8,128)(2,1)S(1)}, u32[]{:S(2)}, u32[]{:S(2)}) collective-permute-start(bf16[256,1024]{1,0:T(8,128)(2,1)} %collective-permute-done.19), channel_id=1, source_target_pairs={{8,0},{10,2},{16,8},{18,10},{24,16},{26,18},{28,24},{30,26},{20,28... | collective-permute-start | bytes 1572872 | tf_op jit(solution)/shard_map/ppermute | solution.py:375
  139.7 21.6 %collective-permute-start.35 = (bf16[128,2048]{1,0:T(8,128)(2,1)S(1)}, bf16[128,2048]{1,0:T(8,128)(2,1)S(1)}, u32[]{:S(2)}, u32[]{:S(2)}) collective-permute-start(bf16[128,2048]{1,0:T(8,128)(2,1)S(1)} %get-tuple-element.27.refs_0_), channel_id=1, source_target_pairs={{0,2},{2,0},{4,6},{6,4},{8,10},{10,8},{12,14},{14,12},{16,18},{18,... | collective-permute-start | bytes 1572872 | tf_op jit(solution)/shard_map/ppermute | solution.py:456
  143.6 28.0 %collective-permute-start.32 = (bf16[128,2048]{1,0:T(8,128)(2,1)S(1)}, bf16[128,2048]{1,0:T(8,128)(2,1)S(1)}, u32[]{:S(2)}, u32[]{:S(2)}) collective-permute-start(bf16[128,2048]{1,0:T(8,128)(2,1)S(1)} %get-tuple-element.26.refs_0_), channel_id=1, source_target_pairs={{0,2},{2,0},{4,6},{6,4},{8,10},{10,8},{12,14},{14,12},{16,18},{18,... | collective-permute-start | bytes 1572872 | tf_op jit(solution)/shard_map/ppermute | solution.py:456
  150.1 27.1 %collective-permute-start.29 = (bf16[128,2048]{1,0:T(8,128)(2,1)S(1)}, bf16[128,2048]{1,0:T(8,128)(2,1)S(1)}, u32[]{:S(2)}, u32[]{:S(2)}) collective-permute-start(bf16[128,2048]{1,0:T(8,128)(2,1)S(1)} %get-tuple-element.25.refs_0_), channel_id=1, source_target_pairs={{0,2},{2,0},{4,6},{6,4},{8,10},{10,8},{12,14},{14,12},{16,18},{18,... | collective-permute-start | bytes 1572872 | tf_op jit(solution)/shard_map/ppermute | solution.py:456
  178.1 24.2 %collective-permute-start.27 = (bf16[128,2048]{1,0:T(8,128)(2,1)S(1)}, bf16[128,2048]{1,0:T(8,128)(2,1)S(1)}, u32[]{:S(2)}, u32[]{:S(2)}) collective-permute-start(bf16[128,2048]{1,0:T(8,128)(2,1)S(1)} %get-tuple-element.27.refs_0_), channel_id=1, source_target_pairs={{0,1},{1,0},{2,3},{3,2},{4,5},{5,4},{6,7},{7,6},{8,9},{9,8},{10,11... | collective-permute-start | bytes 1572872 | tf_op jit(solution)/shard_map/ppermute | solution.py:453
  179.4 28.8 %collective-permute-start.26 = (bf16[128,2048]{1,0:T(8,128)(2,1)S(1)}, bf16[128,2048]{1,0:T(8,128)(2,1)S(1)}, u32[]{:S(2)}, u32[]{:S(2)}) collective-permute-start(bf16[128,2048]{1,0:T(8,128)(2,1)S(1)} %get-tuple-element.26.refs_0_), channel_id=1, source_target_pairs={{0,1},{1,0},{2,3},{3,2},{4,5},{5,4},{6,7},{7,6},{8,9},{9,8},{10,11... | collective-permute-start | bytes 1572872 | tf_op jit(solution)/shard_map/ppermute | solution.py:453
  180.5 33.8 %collective-permute-start.8 = (bf16[128,2048]{1,0:T(8,128)(2,1)S(1)}, bf16[128,2048]{1,0:T(8,128)(2,1)S(1)}, u32[]{:S(2)}, u32[]{:S(2)}) collective-permute-start(bf16[128,2048]{1,0:T(8,128)(2,1)S(1)} %get-tuple-element.25.refs_0_), channel_id=1, source_target_pairs={{0,1},{1,0},{2,3},{3,2},{4,5},{5,4},{6,7},{7,6},{8,9},{9,8},{10,11... | collective-permute-start | bytes 1572872 | tf_op jit(solution)/shard_map/ppermute | solution.py:453
  190.5 30.1 %collective-permute-start.28 = (bf16[128,2048]{1,0:T(8,128)(2,1)S(1)}, bf16[128,2048]{1,0:T(8,128)(2,1)S(1)}, u32[]{:S(2)}, u32[]{:S(2)}) collective-permute-start(bf16[128,2048]{1,0:T(8,128)(2,1)S(1)} %get-tuple-element.28.refs_0_), channel_id=1, source_target_pairs={{0,1},{1,0},{2,3},{3,2},{4,5},{5,4},{6,7},{7,6},{8,9},{9,8},{10,11... | collective-permute-start | bytes 1572872 | tf_op jit(solution)/shard_map/ppermute | solution.py:453
  196.1 29.7 %collective-permute-start.40 = (bf16[128,1024]{1,0:T(8,128)(2,1)S(1)}, bf16[128,1024]{1,0:T(8,128)(2,1)S(1)}, u32[]{:S(2)}, u32[]{:S(2)}) collective-permute-start(bf16[128,1024]{1,0:T(8,128)(2,1)S(1)} %shard_map.230), channel_id=1, source_target_pairs={{0,2},{2,0},{4,6},{6,4},{8,10},{10,8},{12,14},{14,12},{16,18},{18,... | collective-permute-start | bytes 786440 | tf_op jit(solution)/shard_map/ppermute | solution.py:466
  202.2 23.5 %collective-permute-start.37 = (bf16[128,1024]{1,0:T(8,128)(2,1)S(1)}, bf16[128,1024]{1,0:T(8,128)(2,1)S(1)}, u32[]{:S(2)}, u32[]{:S(2)}) collective-permute-start(bf16[128,1024]{1,0:T(8,128)(2,1)S(1)} %shard_map.229), channel_id=1, source_target_pairs={{0,2},{2,0},{4,6},{6,4},{8,10},{10,8},{12,14},{14,12},{16,18},{18,... | collective-permute-start | bytes 786440 | tf_op jit(solution)/shard_map/ppermute | solution.py:466
  (34 other events, 386.1 us)

commit v3 on v2

--- a/solution.py
+++ b/solution.py
@@ -11,8 +11,11 @@
 BF16 = jnp.bfloat16
 LOW = -1e30
 PARTS = 4
+CHUNKS = 4
 LANES = 128
+MIB = 1024 * 1024
 TAIL = 16
+PLACE, SIDE, THERE, ROWS = 0, 1, 2, 3
 
 
 def full_spec():
@@ -67,9 +70,8 @@
     write_tail(ref, index, norm, top, log)
 
 
-def summary_kernel(place_ref, k_ref, v_ref, in_ref, forget_ref, *refs):
-    c_refs, g_ref = refs[:1], refs[1]
-    c_ref = c_refs[0]
+def summary_kernel(info_ref, k_ref, v_ref, in_ref, forget_ref, *refs):
+    outs, g_ref, c_ref = refs[:PARTS], refs[PARTS], refs[PARTS + 1]
     heads, length = in_ref.shape
     key_size = k_ref.shape[1] // heads
     value_size = v_ref.shape[1] // heads
@@ -86,7 +88,7 @@
     e = total - g + in_ref[...]
     top = jnp.max(e, axis=1, keepdims=True)
     scale = jnp.exp(e - top) * (key_size**-0.5)
-    place = place_ref[0]
+    place = info_ref[PLACE]
     for h in range(heads):
         weighted = (
             k_ref[:, h * key_size : (h + 1) * key_size].astype(F32) * column(scale[h : h + 1])
@@ -100,37 +102,32 @@
             v_ref[:, h * value_size : (h + 1) * value_size],
             (((0,), (0,)), ((), ())),
             preferred_element_type=F32,
-        )
+        ).astype(BF16)
         for c in range(PARTS):
-            write_message(
-                c_ref,
-                (lax.bitwise_xor(place, c), h),
-                memory[:, c * width : (c + 1) * width],
-                norm,
-                top[h : h + 1],
-                total[h : h + 1],
-            )
-
-
-def summarize(place, keys, values, gate_in, gate_forget):
+            c_ref[c] = memory[:, c * width : (c + 1) * width]
+        for r in range(PARTS):
+            outs[r][h, :key_size] = c_ref[lax.bitwise_xor(place, r)]
+            write_tail(outs[r], (h,), norm, top[h : h + 1], total[h : h + 1])
+
+
+def summarize(info, keys, values, gate_in, gate_forget):
     heads, length = gate_in.shape
     key_size = keys.shape[1] // heads
-    value_size = values.shape[1] // heads
+    width = values.shape[1] // heads // PARTS
     return pl.pallas_call(
         summary_kernel,
-        out_shape=(
-            jax.ShapeDtypeStruct((PARTS, heads, key_size + TAIL, value_size // PARTS), BF16),
-            jax.ShapeDtypeStruct((heads, length), F32),
-        ),
+        out_shape=(jax.ShapeDtypeStruct((heads, key_size + TAIL, width), BF16),) * PARTS
+        + (jax.ShapeDtypeStruct((heads, length), F32),),
         in_specs=[smem_spec()] + [full_spec()] * 4,
-        out_specs=(full_spec(), full_spec()),
-        compiler_params=pltpu.CompilerParams(vmem_limit_bytes=40 * 1024 * 1024),
-    )(place, keys, values, gate_in, gate_forget)
-
-
-def plane_kernel(place_ref, *refs):
+        out_specs=(full_spec(),) * (PARTS + 1),
+        scratch_shapes=[pltpu.VMEM((PARTS, key_size, width), BF16)],
+        compiler_params=pltpu.CompilerParams(vmem_limit_bytes=14 * MIB),
+    )(info, keys, values, gate_in, gate_forget)
+
+
+def plane_kernel(info_ref, *refs):
     got, out_ref = refs[:PARTS], refs[PARTS]
-    at = [lax.bitwise_xor(place_ref[0], r) for r in range(PARTS)]
+    at = [lax.bitwise_xor(info_ref[PLACE], r) for r in range(PARTS)]
     for h in range(out_ref.shape[0]):
         tails = [read_tail(ref, (h,)) for ref in got]
         logs = []
@@ -151,6 +148,10 @@
         )
 
 
+def is_there(info_ref, steps):
+    return info_ref[THERE] >= steps
+
+
 def pair_up(first, second, first_there, second_there):
     norm_one, top_one, log_one = first
     norm_two, top_two, log_two = second
@@ -163,13 +164,13 @@
     return one, two, (one * norm_one + two * norm_two, top, log_one + log_two)
 
 
-def window_kernel(there_ref, one_ref, two_ref, out_ref):
+def window_kernel(there, info_ref, one_ref, two_ref, out_ref):
     for h in range(out_ref.shape[0]):
         one, two, tail = pair_up(
             read_tail(one_ref, (h,)),
             read_tail(two_ref, (h,)),
-            there_ref[0] > 0,
-            there_ref[1] > 0,
+            is_there(info_ref, there[0]),
+            is_there(info_ref, there[1]),
         )
         write_message(
             out_ref,
@@ -179,15 +180,15 @@
         )
 
 
-def carry_kernel(place_ref, there_ref, one_ref, two_ref, *refs):
+def carry_kernel(there, info_ref, one_ref, two_ref, *refs):
     got, outs = refs[:PARTS], refs[PARTS:]
-    at = [lax.bitwise_xor(place_ref[0], r) for r in range(PARTS)]
+    at = [lax.bitwise_xor(info_ref[PLACE], r) for r in range(PARTS)]
     for h in range(one_ref.shape[0]):
         one, two, (norm, top, _) = pair_up(
             read_tail(one_ref, (h,)),
             read_tail(two_ref, (h,)),
-            there_ref[0] > 0,
-            there_ref[1] > 0,
+            is_there(info_ref, there[0]),
+            is_there(info_ref, there[1]),
         )
         memory = one * read_memory(one_ref, (h,)) + two * read_memory(two_ref, (h,))
         tails = [read_tail(ref, (h,)) for ref in got]
@@ -217,15 +218,15 @@
             )
 
 
-def small_call(kernel, scalars, messages, count):
+def small_call(kernel, info, messages, count):
     shape = jax.ShapeDtypeStruct(messages[0].shape, BF16)
     return pl.pallas_call(
         kernel,
         out_shape=(shape,) * count,
-        in_specs=[smem_spec()] * len(scalars) + [full_spec()] * len(messages),
+        in_specs=[smem_spec()] + [full_spec()] * len(messages),
         out_specs=(full_spec(),) * count,
-        compiler_params=pltpu.CompilerParams(vmem_limit_bytes=40 * 1024 * 1024),
-    )(*scalars, *messages)
+        compiler_params=pltpu.CompilerParams(vmem_limit_bytes=16 * MIB),
+    )(info, *messages)
 
 
 def intra_kernel(q_ref, k_ref, v_ref, in_ref, g_ref, part_ref, stat_ref):
@@ -270,16 +271,16 @@
             pl.BlockSpec((length, value_size), lambda h: (0, h)),
             per_head(length, LANES),
         ),
-        compiler_params=pltpu.CompilerParams(vmem_limit_bytes=40 * 1024 * 1024),
+        compiler_params=pltpu.CompilerParams(vmem_limit_bytes=40 * MIB),
     )(queries, keys, values, gate_in[:, None], g[:, None])
 
 
-def join_kernel(place_ref, q_ref, *refs):
+def join_kernel(info_ref, q_ref, *refs):
     pieces, (part_ref, stat_ref), outs = refs[:PARTS], refs[PARTS : PARTS + 2], refs[PARTS + 2 : -1]
     mem_ref = refs[-1]
     width = pieces[0].shape[-1]
     for r in range(PARTS):
-        at = pl.multiple_of(lax.bitwise_xor(place_ref[0], r) * width, width)
+        at = pl.multiple_of(lax.bitwise_xor(info_ref[PLACE], r) * width, width)
         mem_ref[:, pl.ds(at, width)] = pieces[r][0, : mem_ref.shape[0]]
     norm, carry_top, _ = read_tail(pieces[0], (0,))
     flat = jnp.concatenate([norm[i : i + 1] for i in range(norm.shape[0])], axis=1)
@@ -298,7 +299,7 @@
         out[...] = result[i * rows : (i + 1) * rows]
 
 
-def join(place, queries, carries, part, stat, chunks):
+def join(info, queries, carries, part, stat, chunks):
     heads, rows, width = carries[0].shape
     key_size = rows - TAIL
     length = queries.shape[0]
@@ -316,40 +317,83 @@
         ],
         out_specs=(pl.BlockSpec((piece, value_size), lambda h: (0, h)),) * chunks,
         scratch_shapes=[pltpu.VMEM((key_size, value_size), BF16)],
-        compiler_params=pltpu.CompilerParams(vmem_limit_bytes=40 * 1024 * 1024),
-    )(place, queries, *carries, part, stat)
-
-
-def project_kernel(count, *refs):
-    ops, w_ref, out_ref = refs[:count], refs[count], refs[count + 1]
-    at, total = 0, None
-    for a in ops:
-        term = jnp.dot(
-            a[...], w_ref[at : at + a.shape[1]], preferred_element_type=F32
+        compiler_params=pltpu.CompilerParams(vmem_limit_bytes=40 * MIB),
+    )(info, queries, *carries, part, stat)
+
+
+def fetch_weight(info_ref, pieces, first_column, w_ref, sems):
+    copies = []
+    for i, piece in enumerate(pieces):
+        rows = piece.shape[0]
+        at = pl.multiple_of(info_ref[ROWS + i], rows)
+        copies.append(
+            pltpu.make_async_copy(
+                piece.at[:, pl.ds(first_column, w_ref.shape[1])],
+                w_ref.at[pl.ds(at, rows)],
+                sems.at[i],
+            )
         )
-        total = term if total is None else total + term
-        at += a.shape[1]
-    out_ref[...] = total.astype(BF16)
-
-
-def project(operands, weight, block=256):
-    rows, cols = operands[0].shape[0], weight.shape[1]
-    block = min(block, cols)
-    depth = weight.shape[0]
+    for copy in copies:
+        copy.start()
+    for copy in copies:
+        copy.wait()
+
+
+def project_kernel(shape, first_column, tile, info_ref, *refs):
+    chunks, per_chunk = shape
+    ops, pieces = refs[: chunks * per_chunk], refs[chunks * per_chunk : -5]
+    out_ref, w_ref, result_ref, sems, out_sem = refs[-5:]
+    fetch_weight(info_ref, pieces, first_column, w_ref, sems)
+    rows = ops[0].shape[0]
+
+    @pl.loop(0, w_ref.shape[1] // tile)
+    def _(i):
+        columns = pl.ds(pl.multiple_of(i * tile, tile), tile)
+        for chunk in range(chunks):
+            at, total = 0, None
+            for a in ops[chunk * per_chunk : (chunk + 1) * per_chunk]:
+                term = jnp.dot(
+                    a[...],
+                    w_ref[pl.ds(at, a.shape[1]), columns],
+                    preferred_element_type=F32,
+                )
+                total = term if total is None else total + term
+                at += a.shape[1]
+            result_ref[pl.ds(chunk * rows, rows), columns] = total.astype(BF16)
+
+    cols = w_ref.shape[1]
+    at = 0 if out_ref.shape[1] == cols else pl.multiple_of(info_ref[SIDE] * cols, cols)
+    copy = pltpu.make_async_copy(result_ref, out_ref.at[:, pl.ds(at, cols)], out_sem)
+    copy.start()
+    copy.wait()
+
+
+def project(info, operands, pieces, first_column, cols, out_cols):
+    flat = [a for chunk in operands for a in chunk]
+    rows = sum(chunk[0].shape[0] for chunk in operands)
+    depth = sum(p.shape[0] for p in pieces)
     return pl.pallas_call(
-        functools.partial(project_kernel, len(operands)),
-        grid=(cols // block,),
-        out_shape=jax.ShapeDtypeStruct((rows, cols), BF16),
-        in_specs=[pl.BlockSpec(a.shape, lambda i: (0, 0)) for a in operands]
-        + [pl.BlockSpec((depth, block), lambda i: (0, i))],
-        out_specs=pl.BlockSpec((rows, block), lambda i: (0, i)),
-        compiler_params=pltpu.CompilerParams(vmem_limit_bytes=40 * 1024 * 1024),
+        functools.partial(
+            project_kernel, (len(operands), len(operands[0])), first_column, min(cols, 256)
+        ),
+        out_shape=jax.ShapeDtypeStruct((rows, out_cols), BF16),
+        in_specs=[smem_spec()]
+        + [full_spec()] * len(flat)
+        + [pl.BlockSpec(memory_space=pl.ANY)] * len(pieces),
+        out_specs=pl.BlockSpec(memory_space=pl.ANY),
+        scratch_shapes=[
+            pltpu.VMEM((depth, cols), BF16),
+            pltpu.VMEM((rows, cols), BF16),
+            pltpu.SemaphoreType.DMA((len(pieces),)),
+            pltpu.SemaphoreType.DMA,
+        ],
+        compiler_params=pltpu.CompilerParams(vmem_limit_bytes=58 * MIB),
         cost_estimate=pl.CostEstimate(
             flops=2 * rows * cols * depth,
             bytes_accessed=2 * (rows * depth + depth * cols + rows * cols),
             transcendentals=0,
         ),
-    )(*operands, weight)
+    )(info, *flat, *pieces)
 
 
 def xor_perm(n, d):
@@ -365,106 +409,144 @@
     return order, fwd, [(d, s) for s, d in fwd]
 
 
-def ring(piece, n):
-    _, fwd, bwd = ring_perms(n)
+def piece_list(n):
     count = n // 2
-    got = {0: piece}
-    f = b = piece
+    result = [(0, 0)]
     for t in range(1, (count - 1) // 2 + 1):
-        f = lax.ppermute(f, "seq", fwd)
-        b = lax.ppermute(b, "seq", bwd)
-        got[t], got[-t] = f, b
-    half = piece.shape[0] // 2
-    got[count // 2] = (
-        lax.ppermute(f[:half], "seq", fwd),
-        lax.ppermute(b[half:], "seq", bwd),
-    )
-    return got
-
-
-def gather_weight(weight, n, first):
-    rows, cols = weight.shape
-    me = lax.axis_index("seq")
+        result += [(t, 0), (-t, 0)]
+    return result + [(count // 2, 0), (count // 2, 1)]
+
+
+def device_table(n, n_head, rows):
     order, _, _ = ring_perms(n)
     count = len(order)
-    where = [order.index(q) for q in range(count)]
-    here = jnp.array(where)[me // 2]
-    side = me % 2
-    share = cols // 2
-    mine = lax.dynamic_slice_in_dim(weight, side * share, share, 1)
-    theirs = lax.dynamic_slice_in_dim(weight, (1 - side) * share, share, 1)
-    other = lax.ppermute(theirs, "seq", xor_perm(n, 1))
-    full = jnp.zeros((n * rows, share), weight.dtype)
-    for flip, piece in ((False, mine), (True, other)):
-        for d, a in ring(piece, n).items():
-            src = jnp.array(order)[(here - d) % count]
-            at = (2 * src + (1 - side if flip else side)) * rows - first
-            at = jnp.where(at < 0, at + n * rows, at)
-            for p in a if isinstance(a, tuple) else (a,):
-                full = lax.dynamic_update_slice(full, p, (at, 0))
-                at = at + p.shape[0]
-    return full
+    table = []
+    for me in range(n):
+        here = order.index(me // 2)
+        for head in range(n_head):
+            first = head * (n * rows // 2) if n_head == 2 else 0
+            line = [me % PARTS, me % 2, me // PARTS]
+            for flip in (0, 1):
+                for d, half in piece_list(n):
+                    src = 2 * order[(here - d) % count] + ((me % 2) ^ flip)
+                    line.append((src * rows - first) % (n * rows) + half * (rows // 2))
+            table.append(line)
+    return jnp.array(table, jnp.int32)
+
+
+def after(value, *others):
+    return lax.optimization_barrier((value, *others))[0]
+
+
+class Ring:
+    def __init__(self, piece, n):
+        _, self.fwd, self.bwd = ring_perms(n)
+        self.count = n // 2
+        self.got = [piece]
+        self.ends = (piece, piece)
+        self.done = 0
+
+    def step(self, *gate):
+        f, b = self.ends
+        self.done += 1
+        if 2 * self.done == self.count:
+            half = f.shape[0] // 2
+            f, b = f[:half], b[half:]
+        if gate:
+            f, b, *_ = lax.optimization_barrier((f, b, *gate))
+        f, b = lax.ppermute(f, "seq", self.fwd), lax.ppermute(b, "seq", self.bwd)
+        self.ends = (f, b)
+        self.got += [f, b]
+
+    def more(self):
+        return 2 * self.done < self.count
 
 
 def body(queries, keys, values, input_gate, forget_gate, out_weight, n, n_head):
     me = lax.axis_index("seq")
-    place = (me % PARTS).astype(jnp.int32)[None]
-    level = (me // PARTS).astype(jnp.int32)
-    memory, g = summarize(place, keys, values, input_gate, forget_gate)
+    table = device_table(n, n_head, out_weight.shape[0])
+    info = lax.dynamic_index_in_dim(
+        table, me * n_head + lax.axis_index("head"), 0, keepdims=False
+    )
+    side = lax.bitwise_and(me, 1)
+    share = out_weight.shape[1] // 2
+    mine = lax.dynamic_slice_in_dim(out_weight, side * share, share, 1)
+    theirs = lax.dynamic_slice_in_dim(out_weight, (1 - side) * share, share, 1)
+    ring_mine = Ring(mine, n)
+    ring_mine.step()
+    *memory, g = summarize(info, keys, values, input_gate, forget_gate)
     got = [memory[0]] + [
         lax.ppermute(memory[r], "seq", xor_perm(n, r)) for r in range(1, PARTS)
     ]
-    (window,) = small_call(plane_kernel, (place,), got, 1)
+    got = list(lax.optimization_barrier((*got, *ring_mine.ends))[:PARTS])
+    if ring_mine.more():
+        ring_mine.step()
+    (window,) = small_call(plane_kernel, info, got, 1)
+    other = lax.ppermute(after(theirs, window), "seq", xor_perm(n, 1))
     levels = n // PARTS
-    d, earlier, there = 1, None, None
+    d, earlier, there = 1, None, 0
     while d < levels:
         step = d * PARTS
         come = lax.ppermute(window, "seq", [(s, s + step) for s in range(n - step)])
-        here = (level >= d).astype(jnp.int32)
-        one = jnp.ones_like(here)
+        here, there = d, 1
         if earlier is None:
-            earlier, there = come, here
-            if 2 * d >= levels:
-                come, here = jnp.zeros_like(come), jnp.zeros_like(here)
+            earlier = come
         elif 2 * d < levels:
-            (earlier,) = small_call(window_kernel, (jnp.stack([here, there]),), (come, earlier), 1)
-            there = one
+            kernel = functools.partial(window_kernel, (here, there))
+            (earlier,) = small_call(kernel, info, (come, earlier), 1)
         if 2 * d < levels:
-            (window,) = small_call(window_kernel, (jnp.stack([here, one]),), (come, window), 1)
+            kernel = functools.partial(window_kernel, (here, 0))
+            (window,) = small_call(kernel, info, (come, window), 1)
         d *= 2
+    if come is earlier:
+        come, here = jnp.zeros_like(come), levels
+    come, other, *_ = lax.optimization_barrier((come, other, *ring_mine.ends))
     carries = small_call(
-        carry_kernel, (place, jnp.stack([here, there])), (come, earlier, *got), PARTS
+        functools.partial(carry_kernel, (here, there)), info, (come, earlier, *got), PARTS
     )
+    part, stat = intra(queries, keys, values, input_gate, after(g, *carries))
+    if ring_mine.more():
+        ring_mine.step(stat)
     carries = [carries[0]] + [
         lax.ppermute(carries[r], "seq", xor_perm(n, r)) for r in range(1, PARTS)
     ]
-    part, stat = intra(queries, keys, values, input_gate, g)
-    chunks = 4
-    hidden = join(place, queries, carries, part, stat, chunks)
-
-    if n_head == 2:
-        first = lax.axis_index("head") * (n * out_weight.shape[0] // 2)
-    else:
-        first = 0
-    weight = gather_weight(out_weight, n, first)
+    ring_other = Ring(other, n)
+    rings = (ring_other, ring_mine)
+    hidden = join(info, queries, carries, part, stat, CHUNKS)
 
     def all_heads(a):
         if n_head == 2:
             return [a, lax.ppermute(a, "head", [(0, 1), (1, 0)])]
         return [lax.all_gather(a, "head", axis=1, tiled=True)]
 
-    sent = [lax.ppermute(a, "seq", xor_perm(n, 1)) for a in hidden]
-    share = weight.shape[1]
-    side = me % 2
-    rows = hidden[0].shape[0]
-    mixed = jnp.zeros((queries.shape[0], 2 * share), BF16)
+    swap = xor_perm(n, 1)
+    own, sent, gate = [], [], (hidden[0],)
     for i, a in enumerate(hidden):
-        mixed = lax.dynamic_update_slice(
-            mixed, project(all_heads(a), weight), (i * rows, side * share)
-        )
-    for i, a in enumerate(sent):
-        back = lax.ppermute(project(all_heads(a), weight), "seq", xor_perm(n, 1))
-        mixed = lax.dynamic_update_slice(mixed, back, (i * rows, (1 - side) * share))
+        a, *_ = lax.optimization_barrier((a, *gate))
+        come = lax.ppermute(a, "seq", swap)
+        late = i == len(hidden) - 1
+        for ring in rings:
+            if ring.more() and (ring is ring_other or late):
+                ring.step(*gate)
+        own.append(all_heads(a))
+        sent.append(all_heads(come))
+        gate = (come, *ring_other.ends, *own[-2:-1], *sent[-2:-1])
+        gate = jax.tree.leaves(gate)
+    while any(ring.more() for ring in rings):
+        for ring in rings:
+            if ring.more():
+                ring.step()
+    pieces = ring_mine.got + ring_other.got
+    halves = 2
+    width = share // halves
+    returned = []
+    for i in range(halves):
+        result = project(info, sent, pieces, i * width, width, width)
+        returned.append(lax.ppermute(result, "seq", swap))
+    own[0][0] = after(own[0][0], result)
+    mixed = project(info, own, pieces, 0, share, 2 * share)
+    for i, a in enumerate(returned):
+        mixed = lax.dynamic_update_slice(mixed, a, (0, (1 - side) * share + i * width))
     return mixed
 
 

time: 229 us -> 177 us (0.77)
  local copies, waits for them, and re-layouts: 42.6 us -> 8.04 us
  Pallas kernels: 57.4 us -> 42.9 us
  waiting for transfers between devices: 63.8 us -> 76.5 us
  between operations: 12.2 us -> 0.42 us
  starting transfers between devices: 51.5 us -> 47.9 us
    dynamic_update_slice x26 -> x2, local copies, waits for them, and re-layouts: 25.4 us -> 1.66 us  [body(): lax.dynamic_update_slice(mixed, a, (0, (1 - side) * share + i * width))]
    ppermute x25 -> x23, waiting for transfers between devices: 25.3 us -> 48.1 us  [the longest x16 39.9 us: step(): f, b = (lax.ppermute(f, 'seq', self.fwd), lax.ppermute(b, 'seq', self.bwd))]
    pallas_call x9 -> x4, Pallas kernels: 41.9 us -> 30.5 us  [the longest x3 27.7 us: project(): pl.pallas_call(functools.partial(project_kernel, (len(operands), len(oper...]
    ppermute x2, waiting for transfers between devices: 18 us -> 7.64 us  [body(): come = lax.ppermute(window, 'seq', [(s, s + step) for s in range(n - step)])]
    ppermute x3, waiting for transfers between devices: 0.01 us -> 5.31 us  [body(): lax.ppermute(carries[r], 'seq', xor_perm(n, r))]
    ppermute x3, waiting for transfers between devices: 20.5 us -> 15.5 us  [body(): lax.ppermute(memory[r], 'seq', xor_perm(n, r))]
    unnamed x34 -> x68, local copies, waits for them, and re-layouts: 7.55 us -> 2.64 us
    broadcast_in_dim x2 -> x0, local copies, waits for them, and re-layouts: 4.63 us -> none  [the longest x1 4.38 us: gather_weight(): full = jnp.zeros((n * rows, share), weight.dtype)]
  transfers between devices with their start and end apart: 41 -> 39, of which waited for: 8 -> 22; matrix products, arithmetic and copies ran while one was open for 11% -> 1% of each run, Pallas kernels for 25% -> 21%
where the time goes in v3:
time: 177 us; the launch traced here: 176 us
  waiting for transfers between devices  76.5 us (43%)
  starting transfers between devices  47.9 us (27%)
  Pallas kernels  42.9 us (24%)
  local copies, waits for them, and re-layouts  8.04 us (5%)
    ppermute x16, waiting for transfers between devices, step(): f, b = (lax.ppermute(f, 'seq', self.fwd), lax.ppermute(b, 'seq', self.bwd))  39.9 us
    pallas_call x3, Pallas kernels, project(): pl.pallas_call(functools.partial(project_kernel, (len(operands), len(oper...  27.7 us
    ppermute x16, starting transfers between devices, step(): f, b = (lax.ppermute(f, 'seq', self.fwd), lax.ppermute(b, 'seq', self.bwd))  23.3 us
    ppermute x3, waiting for transfers between devices, body(): lax.ppermute(memory[r], 'seq', xor_perm(n, r))  15.5 us
    ppermute x2, starting transfers between devices, body(): come = lax.ppermute(window, 'seq', [(s, s + step) for s in range(n - step)])  9.48 us
    ppermute x2, waiting for transfers between devices, body(): come = lax.ppermute(window, 'seq', [(s, s + step) for s in range(n - step)])  7.64 us
    ppermute x4, waiting for transfers between devices, body(): come = lax.ppermute(a, 'seq', swap)  6.6 us
    ppermute x3, waiting for transfers between devices, body(): lax.ppermute(carries[r], 'seq', xor_perm(n, r))  5.31 us
  transfers between devices with their start and end apart: 39, of which 22 were waited for; matrix products, arithmetic and copies ran while one was open for 1% of the time, Pallas kernels for 21%

profile of v3, /device:TPU:0, one launch (start us, length us, event | category | flops | bytes accessed | tf_op | source)
XLA Modules:
  0.0 175.7 jit_solution(12265138172180446814)
XLA Ops:
  2.2 3.0 %collective-permute-start.3 = (bf16[256,1024]{1,0:T(8,128)(2,1)S(1)}, bf16[256,1024]{1,0:T(8,128)(2,1)S(1)}, u32[]{:S(2)}, u32[]{:S(2)}) collective-permute-start(bf16[256,1024]{1,0:T(8,128)(2,1)S(1)} %get-tuple-element.86.refs_8_), channel_id=1, source_target_pairs={{0,8},{2,10},{8,16},{10,18},{16,24},{18,26},{24,28},{26,30},{28,20... | collective-permute-start | bytes 1572872 | tf_op jit(solution)/shard_map/ppermute | solution.py:457
  7.2 2.8 %shard_map.73 = (bf16[4,272,128]{2,1,0:T(8,128)(2,1)S(1)}, bf16[4,272,128]{2,1,0:T(8,128)(2,1)S(1)}, bf16[4,272,128]{2,1,0:T(8,128)(2,1)S(1)}, bf16[4,272,128]{2,1,0:T(8,128)(2,1)S(1)}, f32[4,512]{1,0:T(4,128)S(1)}) custom-call(s32[21]{0:T(128)S(1)} %fusion.info_ref, bf16[512,1024]{1,0:T(8,128)(2,1)S(1)} %copy-done.1, bf16[512,2048]{1,0:T(8,128)(2,1)S(1)} %copy-done, ...), custom_call_target="tpu_custom_call" | custom-call | tf_op jit(solution)/shard_map/pallas_call | solution.py:117
  13.6 6.1 %collective-permute-done.refs_1_ = bf16[4,272,128]{2,1,0:T(8,128)(2,1)S(1)} collective-permute-done((bf16[4,272,128]{2,1,0:T(8,128)(2,1)S(1)}, bf16[4,272,128]{2,1,0:T(8,128)(2,1)S(1)}, u32[]{:S(2)}, u32[]{:S(2)}) %collective-permute-start) | collective-permute-done | bytes 278560 | tf_op jit(solution)/shard_map/ppermute | solution.py:479
  19.7 9.4 %collective-permute-done.1.refs_2_ = bf16[4,272,128]{2,1,0:T(8,128)(2,1)S(1)} collective-permute-done((bf16[4,272,128]{2,1,0:T(8,128)(2,1)S(1)}, bf16[4,272,128]{2,1,0:T(8,128)(2,1)S(1)}, u32[]{:S(2)}, u32[]{:S(2)}) %collective-permute-start.1) | collective-permute-done | bytes 278560 | tf_op jit(solution)/shard_map/ppermute | solution.py:479
  35.2 3.2 %collective-permute-done.5.one_ref.two_ref = bf16[4,272,128]{2,1,0:T(8,128)(2,1)S(1)} collective-permute-done((bf16[4,272,128]{2,1,0:T(8,128)(2,1)S(1)}, bf16[4,272,128]{2,1,0:T(8,128)(2,1)S(1)}, u32[]{:S(2)}, u32[]{:S(2)}) %collective-permute-start.5) | collective-permute-done | bytes 278560 | tf_op jit(solution)/shard_map/ppermute | solution.py:490
  39.3 8.2 %collective-permute-start.6 = (bf16[4,272,128]{2,1,0:T(8,128)(2,1)S(1)}, bf16[4,272,128]{2,1,0:T(8,128)(2,1)S(1)}, u32[]{:S(2)}, u32[]{:S(2)}) collective-permute-start(bf16[4,272,128]{2,1,0:T(8,128)(2,1)S(1)} %shard_map.75), channel_id=1, source_target_pairs={{0,16},{2,18},{4,20},{6,22},{8,24},{10,26},{12,28},{14,30},{1,17},... | collective-permute-start | bytes 835592 | tf_op jit(solution)/shard_map/ppermute | solution.py:490
  49.9 4.4 %collective-permute-done.6.one_ref = bf16[4,272,128]{2,1,0:T(8,128)(2,1)S(1)} collective-permute-done((bf16[4,272,128]{2,1,0:T(8,128)(2,1)S(1)}, bf16[4,272,128]{2,1,0:T(8,128)(2,1)S(1)}, u32[]{:S(2)}, u32[]{:S(2)}) %collective-permute-start.6) | collective-permute-done | bytes 278560 | tf_op jit(solution)/shard_map/ppermute | solution.py:490
  59.9 5.1 %shard_map.77 = (f32[512,2048]{1,0:T(8,128)S(1)}, f32[4,512,128]{2,1,0:T(8,128)S(1)}) custom-call(bf16[512,1024]{1,0:T(8,128)(2,1)S(1)} %copy-done.3, bf16[512,1024]{1,0:T(8,128)(2,1)S(1)} %copy-done.2, bf16[512,2048]{1,0:T(8,128)(2,1)S(1)} %copy-done, f32[4,1,512]{2,1,0:T(1,128)S(1)} %broadcast_in_dim.6.in_ref, f32[4,1,512]{2,1,0:T(1,128)S(1)} %broadcast_in_dim.7.g_ref), custom_call_target="tpu_custom_call" | custom-call | tf_op jit(solution)/shard_map/pallas_call | solution.py:256
  66.0 4.4 %collective-permute-done.11.refs_2_ = bf16[4,272,128]{2,1,0:T(8,128)(2,1)S(1)} collective-permute-done((bf16[4,272,128]{2,1,0:T(8,128)(2,1)S(1)}, bf16[4,272,128]{2,1,0:T(8,128)(2,1)S(1)}, u32[]{:S(2)}, u32[]{:S(2)}) %collective-permute-start.11) | collective-permute-done | bytes 278560 | tf_op jit(solution)/shard_map/ppermute | solution.py:511
  70.3 3.4 %shard_map.78 = (bf16[128,2048]{1,0:T(8,128)(2,1)S(1)}, bf16[128,2048]{1,0:T(8,128)(2,1)S(1)}, bf16[128,2048]{1,0:T(8,128)(2,1)S(1)}, bf16[128,2048]{1,0:T(8,128)(2,1)S(1)}) custom-call(s32[21]{0:T(128)S(1)} %fusion.info_ref, bf16[512,1024]{1,0:T(8,128)(2,1)S(1)} %copy-done.3, bf16[4,272,128]{2,1,0:T(8,128)(2,1)S(1)} %get-tuple-element.55.refs_0_, ...), custom_call_target="tpu_custom_call" | custom-call | tf_op jit(solution)/shard_map/pallas_call | solution.py:308
  73.8 5.3 %collective-permute-start.15 = (bf16[256,1024]{1,0:T(8,128)(2,1)S(1)}, bf16[256,1024]{1,0:T(8,128)(2,1)S(1)}, u32[]{:S(2)}, u32[]{:S(2)}) collective-permute-start(bf16[256,1024]{1,0:T(8,128)(2,1)S(1)} %collective-permute-done.7.refs_17_), channel_id=1, source_target_pairs={{0,8},{2,10},{8,16},{10,18},{16,24},{18,26},{24,28},{26,30},{28,20... | collective-permute-start | bytes 1572872 | tf_op jit(solution)/shard_map/ppermute | solution.py:457
  80.2 6.5 %collective-permute-done.15.refs_18_ = bf16[256,1024]{1,0:T(8,128)(2,1)S(1)} collective-permute-done((bf16[256,1024]{1,0:T(8,128)(2,1)S(1)}, bf16[256,1024]{1,0:T(8,128)(2,1)S(1)}, u32[]{:S(2)}, u32[]{:S(2)}) %collective-permute-start.15) | collective-permute-done | bytes 524320 | tf_op jit(solution)/shard_map/ppermute | solution.py:457
  88.9 3.0 %collective-permute-start.19 = (bf16[256,1024]{1,0:T(8,128)(2,1)S(1)}, bf16[256,1024]{1,0:T(8,128)(2,1)S(1)}, u32[]{:S(2)}, u32[]{:S(2)}) collective-permute-start(bf16[256,1024]{1,0:T(8,128)(2,1)S(1)} %collective-permute-done.15.refs_18_), channel_id=1, source_target_pairs={{0,8},{2,10},{8,16},{10,18},{16,24},{18,26},{24,28},{26,30},{28,20... | collective-permute-start | bytes 1572872 | tf_op jit(solution)/shard_map/ppermute | solution.py:457
  93.4 6.6 %collective-permute-done.19.refs_20_ = bf16[256,1024]{1,0:T(8,128)(2,1)S(1)} collective-permute-done((bf16[256,1024]{1,0:T(8,128)(2,1)S(1)}, bf16[256,1024]{1,0:T(8,128)(2,1)S(1)}, u32[]{:S(2)}, u32[]{:S(2)}) %collective-permute-start.19) | collective-permute-done | bytes 524320 | tf_op jit(solution)/shard_map/ppermute | solution.py:457
  100.1 2.6 %collective-permute-done.20.refs_21_ = bf16[256,1024]{1,0:T(8,128)(2,1)S(1)} collective-permute-done((bf16[256,1024]{1,0:T(8,128)(2,1)S(1)}, bf16[256,1024]{1,0:T(8,128)(2,1)S(1)}, u32[]{:S(2)}, u32[]{:S(2)}) %collective-permute-start.20) | collective-permute-done | bytes 524320 | tf_op jit(solution)/shard_map/ppermute | solution.py:457
  105.9 6.8 %collective-permute-done.24.refs_22_ = bf16[256,1024]{1,0:T(8,128)(2,1)S(1)} collective-permute-done((bf16[256,1024]{1,0:T(8,128)(2,1)S(1)}, bf16[256,1024]{1,0:T(8,128)(2,1)S(1)}, u32[]{:S(2)}, u32[]{:S(2)}) %collective-permute-start.24) | collective-permute-done | bytes 524320 | tf_op jit(solution)/shard_map/ppermute | solution.py:457
  114.9 3.0 %collective-permute-done.22.refs_4_ = bf16[128,2048]{1,0:T(8,128)(2,1)} collective-permute-done((bf16[128,2048]{1,0:T(8,128)(2,1)S(1)}, bf16[128,2048]{1,0:T(8,128)(2,1)}, u32[]{:S(2)}, u32[]{:S(2)}) %collective-permute-start.22) | collective-permute-done | bytes 524320 | tf_op jit(solution)/shard_map/ppermute | solution.py:526
  118.5 2.7 %collective-permute-start.29 = (bf16[256,1024]{1,0:T(8,128)(2,1)S(1)}, bf16[256,1024]{1,0:T(8,128)(2,1)S(1)}, u32[]{:S(2)}, u32[]{:S(2)}) collective-permute-start(bf16[256,1024]{1,0:T(8,128)(2,1)S(1)} %collective-permute-done.8.refs_11_), channel_id=1, source_target_pairs={{0,8},{2,10},{8,16},{10,18},{16,24},{18,26},{24,28},{26,30},{28,20... | collective-permute-start | bytes 1572872 | tf_op jit(solution)/shard_map/ppermute | solution.py:457
  121.5 2.4 %collective-permute-start.33 = (bf16[128,1024]{1,0:T(8,128)(2,1)S(1)}, bf16[128,1024]{1,0:T(8,128)(2,1)S(1)}, u32[]{:S(2)}, u32[]{:S(2)}) collective-permute-start(bf16[128,1024]{1,0:T(8,128)(2,1)S(1)} %slice.18), channel_id=1, source_target_pairs={{0,8},{2,10},{8,16},{10,18},{16,24},{18,26},{24,28},{26,30},{28,20... | collective-permute-start | bytes 786440 | tf_op jit(solution)/shard_map/ppermute | solution.py:457
  123.9 3.4 %collective-permute-done.27.refs_6_ = bf16[128,2048]{1,0:T(8,128)(2,1)} collective-permute-done((bf16[128,2048]{1,0:T(8,128)(2,1)S(1)}, bf16[128,2048]{1,0:T(8,128)(2,1)}, u32[]{:S(2)}, u32[]{:S(2)}) %collective-permute-start.27) | collective-permute-done | bytes 524320 | tf_op jit(solution)/shard_map/ppermute | solution.py:526
  134.2 5.5 %collective-permute-done.34.refs_25_ = bf16[128,1024]{1,0:T(8,128)(2,1)S(1)} collective-permute-done((bf16[128,1024]{1,0:T(8,128)(2,1)S(1)}, bf16[128,1024]{1,0:T(8,128)(2,1)S(1)}, u32[]{:S(2)}, u32[]{:S(2)}) %collective-permute-start.34) | collective-permute-done | bytes 262176 | tf_op jit(solution)/shard_map/ppermute | solution.py:457
  142.6 7.9 %shard_map.81 = bf16[512,512]{1,0:T(8,128)(2,1)} custom-call(s32[21]{0:T(128)} %copy-done.5, bf16[128,2048]{1,0:T(8,128)(2,1)} %copy-done.24, bf16[128,2048]{1,0:T(8,128)(2,1)} %copy-done.26, bf16[128,2048]{1,0:T(8,128)(2,1)} %copy-done.25, bf16[128,2048]{1,0:T(8,128)(2,1)} %copy-done.27, bf16[128,2048]{1,0:T(8,128)(2,1)} %collective-permute-done.22.refs_4_, ...), custom_call_target="tpu_custom_call" | custom-call | flops 2147483648 | bytes 8912896 | tf_op jit(solution)/shard_map/pallas_call | solution.py:375
  152.1 8.0 %shard_map.79 = bf16[512,512]{1,0:T(8,128)(2,1)} custom-call(s32[21]{0:T(128)} %copy-done.5, bf16[128,2048]{1,0:T(8,128)(2,1)} %copy-done.24, bf16[128,2048]{1,0:T(8,128)(2,1)} %copy-done.26, bf16[128,2048]{1,0:T(8,128)(2,1)} %copy-done.25, bf16[128,2048]{1,0:T(8,128)(2,1)} %copy-done.27, bf16[128,2048]{1,0:T(8,128)(2,1)} %collective-permute-done.22.refs_4_, ...), custom_call_target="tpu_custom_call" | custom-call | flops 2147483648 | bytes 8912896 | tf_op jit(solution)/shard_map/pallas_call | solution.py:375
  160.7 11.8 %shard_map.80 = bf16[512,2048]{1,0:T(8,128)(2,1)} custom-call(s32[21]{0:T(128)} %copy-done.5, bf16[128,2048]{1,0:T(8,128)(2,1)} %copy-done.7, bf16[128,2048]{1,0:T(8,128)(2,1)} %copy-done.32, bf16[128,2048]{1,0:T(8,128)(2,1)} %copy-done.8, bf16[128,2048]{1,0:T(8,128)(2,1)} %copy-done.33, bf16[128,2048]{1,0:T(8,128)(2,1)} %copy-done.9, ...), custom_call_target="tpu_custom_call" | custom-call | flops 4294967296 | bytes 13631488 | tf_op jit(solution)/shard_map/pallas_call | solution.py:375
  (141 shorter events, 49.9 us)
Async XLA Ops:
  2.2 26.8 %collective-permute-start.3 = (bf16[256,1024]{1,0:T(8,128)(2,1)S(1)}, bf16[256,1024]{1,0:T(8,128)(2,1)S(1)}, u32[]{:S(2)}, u32[]{:S(2)}) collective-permute-start(bf16[256,1024]{1,0:T(8,128)(2,1)S(1)} %get-tuple-element.86.refs_8_), channel_id=1, source_target_pairs={{0,8},{2,10},{8,16},{10,18},{16,24},{18,26},{24,28},{26,30},{28,20... | collective-permute-start | bytes 1572872 | tf_op jit(solution)/shard_map/ppermute | solution.py:457
  5.3 23.8 %collective-permute-start.4 = (bf16[256,1024]{1,0:T(8,128)(2,1)S(1)}, bf16[256,1024]{1,0:T(8,128)(2,1)}, u32[]{:S(2)}, u32[]{:S(2)}) collective-permute-start(bf16[256,1024]{1,0:T(8,128)(2,1)S(1)} %get-tuple-element.86.refs_8_), channel_id=1, source_target_pairs={{8,0},{10,2},{16,8},{18,10},{24,16},{26,18},{28,24},{30,26},{20,28... | collective-permute-start | bytes 1572872 | tf_op jit(solution)/shard_map/ppermute | solution.py:457
  12.0 17.0 %collective-permute-start.1 = (bf16[4,272,128]{2,1,0:T(8,128)(2,1)S(1)}, bf16[4,272,128]{2,1,0:T(8,128)(2,1)S(1)}, u32[]{:S(2)}, u32[]{:S(2)}) collective-permute-start(bf16[4,272,128]{2,1,0:T(8,128)(2,1)S(1)} %get-tuple-element.47), channel_id=1, source_target_pairs={{0,4},{2,6},{4,0},{6,2},{8,12},{10,14},{12,8},{14,10},{16,20},{18,... | collective-permute-start | bytes 835592 | tf_op jit(solution)/shard_map/ppermute | solution.py:479
  13.6 15.5 %collective-permute-start.2 = (bf16[4,272,128]{2,1,0:T(8,128)(2,1)S(1)}, bf16[4,272,128]{2,1,0:T(8,128)(2,1)S(1)}, u32[]{:S(2)}, u32[]{:S(2)}) collective-permute-start(bf16[4,272,128]{2,1,0:T(8,128)(2,1)S(1)} %get-tuple-element.48), channel_id=1, source_target_pairs={{0,6},{2,4},{4,2},{6,0},{8,14},{10,12},{12,10},{14,8},{16,22},{18,... | collective-permute-start | bytes 835592 | tf_op jit(solution)/shard_map/ppermute | solution.py:479
  31.4 16.1 %collective-permute-start.7 = (bf16[256,1024]{1,0:T(8,128)(2,1)S(1)}, bf16[256,1024]{1,0:T(8,128)(2,1)S(1)}, u32[]{:S(2)}, u32[]{:S(2)}) collective-permute-start(bf16[256,1024]{1,0:T(8,128)(2,1)S(1)} %copy-done.31), channel_id=1, source_target_pairs={{0,2},{2,0},{4,6},{6,4},{8,10},{10,8},{12,14},{14,12},{16,18},{18,... | collective-permute-start | bytes 1572872 | tf_op jit(solution)/shard_map/ppermute | solution.py:485
  33.2 16.5 %collective-permute-start.8 = (bf16[256,1024]{1,0:T(8,128)(2,1)S(1)}, bf16[256,1024]{1,0:T(8,128)(2,1)S(1)}, u32[]{:S(2)}, u32[]{:S(2)}) collective-permute-start(bf16[256,1024]{1,0:T(8,128)(2,1)S(1)} %collective-permute-done.3.refs_9_), channel_id=1, source_target_pairs={{0,8},{2,10},{8,16},{10,18},{16,24},{18,26},{24,28},{26,30},{28,20... | collective-permute-start | bytes 1572872 | tf_op jit(solution)/shard_map/ppermute | solution.py:457
  33.2 16.7 %collective-permute-start.9 = (bf16[256,1024]{1,0:T(8,128)(2,1)}, bf16[256,1024]{1,0:T(8,128)(2,1)S(1)}, u32[]{:S(2)}, u32[]{:S(2)}) collective-permute-start(bf16[256,1024]{1,0:T(8,128)(2,1)} %collective-permute-done.4.refs_10_), channel_id=1, source_target_pairs={{8,0},{10,2},{16,8},{18,10},{24,16},{26,18},{28,24},{30,26},{20,28... | collective-permute-start | bytes 1572872 | tf_op jit(solution)/shard_map/ppermute | solution.py:457
  39.3 14.9 %collective-permute-start.6 = (bf16[4,272,128]{2,1,0:T(8,128)(2,1)S(1)}, bf16[4,272,128]{2,1,0:T(8,128)(2,1)S(1)}, u32[]{:S(2)}, u32[]{:S(2)}) collective-permute-start(bf16[4,272,128]{2,1,0:T(8,128)(2,1)S(1)} %shard_map.75), channel_id=1, source_target_pairs={{0,16},{2,18},{4,20},{6,22},{8,24},{10,26},{12,28},{14,30},{1,17},... | collective-permute-start | bytes 835592 | tf_op jit(solution)/shard_map/ppermute | solution.py:490
  57.8 12.6 %collective-permute-start.11 = (bf16[4,272,128]{2,1,0:T(8,128)(2,1)S(1)}, bf16[4,272,128]{2,1,0:T(8,128)(2,1)S(1)}, u32[]{:S(2)}, u32[]{:S(2)}) collective-permute-start(bf16[4,272,128]{2,1,0:T(8,128)(2,1)S(1)} %get-tuple-element.57), channel_id=1, source_target_pairs={{0,4},{2,6},{4,0},{6,2},{8,12},{10,14},{12,8},{14,10},{16,20},{18,... | collective-permute-start | bytes 835592 | tf_op jit(solution)/shard_map/ppermute | solution.py:511
  59.2 11.2 %collective-permute-start.12 = (bf16[4,272,128]{2,1,0:T(8,128)(2,1)S(1)}, bf16[4,272,128]{2,1,0:T(8,128)(2,1)S(1)}, u32[]{:S(2)}, u32[]{:S(2)}) collective-permute-start(bf16[4,272,128]{2,1,0:T(8,128)(2,1)S(1)} %get-tuple-element.58), channel_id=1, source_target_pairs={{0,6},{2,4},{4,2},{6,0},{8,14},{10,12},{12,10},{14,8},{16,22},{18,... | collective-permute-start | bytes 835592 | tf_op jit(solution)/shard_map/ppermute | solution.py:511
  73.8 12.9 %collective-permute-start.15 = (bf16[256,1024]{1,0:T(8,128)(2,1)S(1)}, bf16[256,1024]{1,0:T(8,128)(2,1)S(1)}, u32[]{:S(2)}, u32[]{:S(2)}) collective-permute-start(bf16[256,1024]{1,0:T(8,128)(2,1)S(1)} %collective-permute-done.7.refs_17_), channel_id=1, source_target_pairs={{0,8},{2,10},{8,16},{10,18},{16,24},{18,26},{24,28},{26,30},{28,20... | collective-permute-start | bytes 1572872 | tf_op jit(solution)/shard_map/ppermute | solution.py:457
  80.2 12.8 %collective-permute-start.21 = (bf16[128,2048]{1,0:T(8,128)(2,1)S(1)}, bf16[128,2048]{1,0:T(8,128)(2,1)S(1)}, u32[]{:S(2)}, u32[]{:S(2)}) collective-permute-start(bf16[128,2048]{1,0:T(8,128)(2,1)S(1)} %get-tuple-element.84.refs_0_), channel_id=1, source_target_pairs={{0,1},{1,0},{2,3},{3,2},{4,5},{5,4},{6,7},{7,6},{8,9},{9,8},{10,11... | collective-permute-start | bytes 1572872 | tf_op jit(solution)/shard_map/ppermute | solution.py:519
  88.9 11.1 %collective-permute-start.19 = (bf16[256,1024]{1,0:T(8,128)(2,1)S(1)}, bf16[256,1024]{1,0:T(8,128)(2,1)S(1)}, u32[]{:S(2)}, u32[]{:S(2)}) collective-permute-start(bf16[256,1024]{1,0:T(8,128)(2,1)S(1)} %collective-permute-done.15.refs_18_), channel_id=1, source_target_pairs={{0,8},{2,10},{8,16},{10,18},{16,24},{18,26},{24,28},{26,30},{28,20... | collective-permute-start | bytes 1572872 | tf_op jit(solution)/shard_map/ppermute | solution.py:457
  91.9 10.9 %collective-permute-start.17 = (bf16[128,2048]{1,0:T(8,128)(2,1)S(1)}, bf16[128,2048]{1,0:T(8,128)(2,1)S(1)}, u32[]{:S(2)}, u32[]{:S(2)}) collective-permute-start(bf16[128,2048]{1,0:T(8,128)(2,1)S(1)} %get-tuple-element.69.refs_2_), channel_id=1, source_target_pairs={{0,2},{2,0},{4,6},{6,4},{8,10},{10,8},{12,14},{14,12},{16,18},{18,... | collective-permute-start | bytes 1572872 | tf_op jit(solution)/shard_map/ppermute | solution.py:526
  92.9 13.0 %collective-permute-start.26 = (bf16[128,2048]{1,0:T(8,128)(2,1)S(1)}, bf16[128,2048]{1,0:T(8,128)(2,1)S(1)}, u32[]{:S(2)}, u32[]{:S(2)}) collective-permute-start(bf16[128,2048]{1,0:T(8,128)(2,1)S(1)} %get-tuple-element.69.refs_2_), channel_id=1, source_target_pairs={{0,1},{1,0},{2,3},{3,2},{4,5},{5,4},{6,7},{7,6},{8,9},{9,8},{10,11... | collective-permute-start | bytes 1572872 | tf_op jit(solution)/shard_map/ppermute | solution.py:519
  105.0 12.9 %collective-permute-start.22 = (bf16[128,2048]{1,0:T(8,128)(2,1)S(1)}, bf16[128,2048]{1,0:T(8,128)(2,1)}, u32[]{:S(2)}, u32[]{:S(2)}) collective-permute-start(bf16[128,2048]{1,0:T(8,128)(2,1)S(1)} %get-tuple-element.73.refs_4_), channel_id=1, source_target_pairs={{0,2},{2,0},{4,6},{6,4},{8,10},{10,8},{12,14},{14,12},{16,18},{18,... | collective-permute-start | bytes 1572872 | tf_op jit(solution)/shard_map/ppermute | solution.py:526
  105.9 12.0 %collective-permute-start.18 = (bf16[128,2048]{1,0:T(8,128)(2,1)S(1)}, bf16[128,2048]{1,0:T(8,128)(2,1)S(1)}, u32[]{:S(2)}, u32[]{:S(2)}) collective-permute-start(bf16[128,2048]{1,0:T(8,128)(2,1)S(1)} %collective-permute-done.17.refs_2_), channel_id=1, source_target_pairs={{0,1},{1,0},{2,3},{3,2},{4,5},{5,4},{6,7},{7,6},{8,9},{9,8},{10,11... | collective-permute-start | bytes 1572872 | tf_op jit(solution)/shard_map/ppermute | solution.py:519
  121.5 12.5 %collective-permute-start.33 = (bf16[128,1024]{1,0:T(8,128)(2,1)S(1)}, bf16[128,1024]{1,0:T(8,128)(2,1)S(1)}, u32[]{:S(2)}, u32[]{:S(2)}) collective-permute-start(bf16[128,1024]{1,0:T(8,128)(2,1)S(1)} %slice.18), channel_id=1, source_target_pairs={{0,8},{2,10},{8,16},{10,18},{16,24},{18,26},{24,28},{26,30},{28,20... | collective-permute-start | bytes 786440 | tf_op jit(solution)/shard_map/ppermute | solution.py:457
  123.9 18.7 %collective-permute-start.23 = (bf16[128,2048]{1,0:T(8,128)(2,1)}, bf16[128,2048]{1,0:T(8,128)(2,1)}, u32[]{:S(2)}, u32[]{:S(2)}) collective-permute-start(bf16[128,2048]{1,0:T(8,128)(2,1)} %collective-permute-done.22.refs_4_), channel_id=1, source_target_pairs={{0,1},{1,0},{2,3},{3,2},{4,5},{5,4},{6,7},{7,6},{8,9},{9,8},{10,11... | collective-permute-start | bytes 1572872 | tf_op jit(solution)/shard_map/ppermute | solution.py:519
  127.2 15.3 %collective-permute-start.28 = (bf16[128,2048]{1,0:T(8,128)(2,1)}, bf16[128,2048]{1,0:T(8,128)(2,1)}, u32[]{:S(2)}, u32[]{:S(2)}) collective-permute-start(bf16[128,2048]{1,0:T(8,128)(2,1)} %collective-permute-done.27.refs_6_), channel_id=1, source_target_pairs={{0,1},{1,0},{2,3},{3,2},{4,5},{5,4},{6,7},{7,6},{8,9},{9,8},{10,11... | collective-permute-start | bytes 1572872 | tf_op jit(solution)/shard_map/ppermute | solution.py:519
  139.6 21.1 %collective-permute-start.35 = (bf16[128,2048]{1,0:T(8,128)(2,1)S(1)}, bf16[128,2048]{1,0:T(8,128)(2,1)}, u32[]{:S(2)}, u32[]{:S(2)}) collective-permute-start(bf16[128,2048]{1,0:T(8,128)(2,1)S(1)} %get-tuple-element.73.refs_4_), channel_id=1, source_target_pairs={{0,1},{1,0},{2,3},{3,2},{4,5},{5,4},{6,7},{7,6},{8,9},{9,8},{10,11... | collective-permute-start | bytes 1572872 | tf_op jit(solution)/shard_map/ppermute | solution.py:519
  141.0 19.7 %collective-permute-start.36 = (bf16[128,2048]{1,0:T(8,128)(2,1)S(1)}, bf16[128,2048]{1,0:T(8,128)(2,1)}, u32[]{:S(2)}, u32[]{:S(2)}) collective-permute-start(bf16[128,2048]{1,0:T(8,128)(2,1)S(1)} %get-tuple-element.77.refs_6_), channel_id=1, source_target_pairs={{0,1},{1,0},{2,3},{3,2},{4,5},{5,4},{6,7},{7,6},{8,9},{9,8},{10,11... | collective-permute-start | bytes 1572872 | tf_op jit(solution)/shard_map/ppermute | solution.py:519
  150.6 21.9 %collective-permute-start.37 = (bf16[512,512]{1,0:T(8,128)(2,1)}, bf16[512,512]{1,0:T(8,128)(2,1)S(1)}, u32[]{:S(2)}, u32[]{:S(2)}) collective-permute-start(bf16[512,512]{1,0:T(8,128)(2,1)} %shard_map.81), channel_id=1, source_target_pairs={{0,2},{2,0},{4,6},{6,4},{8,10},{10,8},{12,14},{14,12},{16,18},{18,... | collective-permute-start | bytes 1572872 | tf_op jit(solution)/shard_map/ppermute | solution.py:545
  160.1 14.8 %collective-permute-start.38 = (bf16[512,512]{1,0:T(8,128)(2,1)}, bf16[512,512]{1,0:T(8,128)(2,1)S(1)}, u32[]{:S(2)}, u32[]{:S(2)}) collective-permute-start(bf16[512,512]{1,0:T(8,128)(2,1)} %shard_map.79), channel_id=1, source_target_pairs={{0,2},{2,0},{4,6},{6,4},{8,10},{10,8},{12,14},{14,12},{16,18},{18,... | collective-permute-start | bytes 1572872 | tf_op jit(solution)/shard_map/ppermute | solution.py:545
  (49 other events, 1328.2 us)

commit v4 on v3

--- a/solution.py
+++ b/solution.py
@@ -321,7 +321,7 @@
     )(info, queries, *carries, part, stat)
 
 
-def fetch_weight(info_ref, pieces, first_column, w_ref, sems):
+def weight_copies(info_ref, pieces, first_column, w_ref, sems):
     copies = []
     for i, piece in enumerate(pieces):
         rows = piece.shape[0]
@@ -333,48 +333,56 @@
                 sems.at[i],
             )
         )
-    for copy in copies:
-        copy.start()
-    for copy in copies:
-        copy.wait()
+    return copies
 
 
 def project_kernel(shape, first_column, tile, info_ref, *refs):
     chunks, per_chunk = shape
     ops, pieces = refs[: chunks * per_chunk], refs[chunks * per_chunk : -5]
-    out_ref, w_ref, result_ref, sems, out_sem = refs[-5:]
-    fetch_weight(info_ref, pieces, first_column, w_ref, sems)
+    out_ref, w_ref, result_ref, sems, out_sems = refs[-5:]
+    tiles = w_ref.shape[0]
+    fetches = [
+        weight_copies(info_ref, pieces, first_column + t * tile, w_ref.at[t], sems.at[t])
+        for t in range(tiles)
+    ]
+    for fetch in fetches:
+        for copy in fetch:
+            copy.start()
     rows = ops[0].shape[0]
-
-    @pl.loop(0, w_ref.shape[1] // tile)
-    def _(i):
-        columns = pl.ds(pl.multiple_of(i * tile, tile), tile)
+    cols = tiles * tile
+    at = 0 if out_ref.shape[1] == cols else pl.multiple_of(info_ref[SIDE] * cols, cols)
+    stores = []
+    for t in range(tiles):
+        for copy in fetches[t]:
+            copy.wait()
         for chunk in range(chunks):
-            at, total = 0, None
+            depth, total = 0, None
             for a in ops[chunk * per_chunk : (chunk + 1) * per_chunk]:
                 term = jnp.dot(
                     a[...],
-                    w_ref[pl.ds(at, a.shape[1]), columns],
+                    w_ref[t, depth : depth + a.shape[1]],
                     preferred_element_type=F32,
                 )
                 total = term if total is None else total + term
-                at += a.shape[1]
-            result_ref[pl.ds(chunk * rows, rows), columns] = total.astype(BF16)
-
-    cols = w_ref.shape[1]
-    at = 0 if out_ref.shape[1] == cols else pl.multiple_of(info_ref[SIDE] * cols, cols)
-    copy = pltpu.make_async_copy(result_ref, out_ref.at[:, pl.ds(at, cols)], out_sem)
-    copy.start()
-    copy.wait()
+                depth += a.shape[1]
+            result_ref[t, chunk * rows : (chunk + 1) * rows] = total.astype(BF16)
+        store = pltpu.make_async_copy(
+            result_ref.at[t], out_ref.at[:, pl.ds(at + t * tile, tile)], out_sems.at[t]
+        )
+        store.start()
+        stores.append(store)
+    for store in stores:
+        store.wait()
 
 
 def project(info, operands, pieces, first_column, cols, out_cols):
     flat = [a for chunk in operands for a in chunk]
     rows = sum(chunk[0].shape[0] for chunk in operands)
     depth = sum(p.shape[0] for p in pieces)
+    tile = min(cols, 256)
     return pl.pallas_call(
         functools.partial(
-            project_kernel, (len(operands), len(operands[0])), first_column, min(cols, 256)
+            project_kernel, (len(operands), len(operands[0])), first_column, tile
         ),
         out_shape=jax.ShapeDtypeStruct((rows, out_cols), BF16),
         in_specs=[smem_spec()]
@@ -382,12 +390,12 @@
         + [pl.BlockSpec(memory_space=pl.ANY)] * len(pieces),
         out_specs=pl.BlockSpec(memory_space=pl.ANY),
         scratch_shapes=[
-            pltpu.VMEM((depth, cols), BF16),
-            pltpu.VMEM((rows, cols), BF16),
-            pltpu.SemaphoreType.DMA((len(pieces),)),
-            pltpu.SemaphoreType.DMA,
+            pltpu.VMEM((cols // tile, depth, tile), BF16),
+            pltpu.VMEM((cols // tile, rows, tile), BF16),
+            pltpu.SemaphoreType.DMA((cols // tile, len(pieces))),
+            pltpu.SemaphoreType.DMA((cols // tile,)),
         ],
-        compiler_params=pltpu.CompilerParams(vmem_limit_bytes=58 * MIB),
+        compiler_params=pltpu.CompilerParams(vmem_limit_bytes=50 * MIB),
         cost_estimate=pl.CostEstimate(
             flops=2 * rows * cols * depth,
             bytes_accessed=2 * (rows * depth + depth * cols + rows * cols),
@@ -409,12 +417,12 @@
     return order, fwd, [(d, s) for s, d in fwd]
 
 
-def piece_list(n):
+def distances(n):
     count = n // 2
-    result = [(0, 0)]
+    result = [0]
     for t in range(1, (count - 1) // 2 + 1):
-        result += [(t, 0), (-t, 0)]
-    return result + [(count // 2, 0), (count // 2, 1)]
+        result += [t, -t]
+    return result + [count // 2]
 
 
 def device_table(n, n_head, rows):
@@ -427,9 +435,9 @@
             first = head * (n * rows // 2) if n_head == 2 else 0
             line = [me % PARTS, me % 2, me // PARTS]
             for flip in (0, 1):
-                for d, half in piece_list(n):
+                for d in distances(n):
                     src = 2 * order[(here - d) % count] + ((me % 2) ^ flip)
-                    line.append((src * rows - first) % (n * rows) + half * (rows // 2))
+                    line.append((src * rows - first) % (n * rows))
             table.append(line)
     return jnp.array(table, jnp.int32)
 
@@ -439,24 +447,25 @@
 
 
 class Ring:
-    def __init__(self, piece, n):
+    def __init__(self, piece, n, last_forward):
         _, self.fwd, self.bwd = ring_perms(n)
         self.count = n // 2
+        self.last_forward = last_forward
         self.got = [piece]
         self.ends = (piece, piece)
         self.done = 0
 
     def step(self, *gate):
-        f, b = self.ends
+        ends = self.ends
         self.done += 1
+        if gate:
+            ends = lax.optimization_barrier((*ends, *gate))[:2]
+        perms = (self.fwd, self.bwd)
         if 2 * self.done == self.count:
-            half = f.shape[0] // 2
-            f, b = f[:half], b[half:]
-        if gate:
-            f, b, *_ = lax.optimization_barrier((f, b, *gate))
-        f, b = lax.ppermute(f, "seq", self.fwd), lax.ppermute(b, "seq", self.bwd)
-        self.ends = (f, b)
-        self.got += [f, b]
+            at = 0 if self.last_forward else 1
+            ends, perms = ends[at : at + 1], perms[at : at + 1]
+        self.ends = tuple(lax.ppermute(e, "seq", p) for e, p in zip(ends, perms))
+        self.got += self.ends
 
     def more(self):
         return 2 * self.done < self.count
@@ -472,7 +481,7 @@
     share = out_weight.shape[1] // 2
     mine = lax.dynamic_slice_in_dim(out_weight, side * share, share, 1)
     theirs = lax.dynamic_slice_in_dim(out_weight, (1 - side) * share, share, 1)
-    ring_mine = Ring(mine, n)
+    ring_mine = Ring(mine, n, True)
     ring_mine.step()
     *memory, g = summarize(info, keys, values, input_gate, forget_gate)
     got = [memory[0]] + [
@@ -505,12 +514,12 @@
         functools.partial(carry_kernel, (here, there)), info, (come, earlier, *got), PARTS
     )
     part, stat = intra(queries, keys, values, input_gate, after(g, *carries))
-    if ring_mine.more():
-        ring_mine.step(stat)
     carries = [carries[0]] + [
         lax.ppermute(carries[r], "seq", xor_perm(n, r)) for r in range(1, PARTS)
     ]
-    ring_other = Ring(other, n)
+    if ring_mine.more():
+        ring_mine.step(stat)
+    ring_other = Ring(other, n, False)
     rings = (ring_other, ring_mine)
     hidden = join(info, queries, carries, part, stat, CHUNKS)
 
@@ -524,18 +533,18 @@
     for i, a in enumerate(hidden):
         a, *_ = lax.optimization_barrier((a, *gate))
         come = lax.ppermute(a, "seq", swap)
-        late = i == len(hidden) - 1
+        late, ends = i == len(hidden) - 1, ring_mine.ends
+        while late and ring_other.done + 1 < n // 4:
+            ring_other.step(*gate)
+        while late and ring_mine.done + 1 < n // 4:
+            ring_mine.step(*gate)
         for ring in rings:
             if ring.more() and (ring is ring_other or late):
                 ring.step(*gate)
         own.append(all_heads(a))
         sent.append(all_heads(come))
-        gate = (come, *ring_other.ends, *own[-2:-1], *sent[-2:-1])
+        gate = (come, *ends, *ring_other.ends, *own[-2:-1], *sent[-2:-1])
         gate = jax.tree.leaves(gate)
-    while any(ring.more() for ring in rings):
-        for ring in rings:
-            if ring.more():
-                ring.step()
     pieces = ring_mine.got + ring_other.got
     halves = 2
     width = share // halves

time: 177 us -> 171 us (0.966)
  Pallas kernels: 42.9 us -> 37.3 us
  waiting for transfers between devices: 76.5 us -> 73.7 us
  starting transfers between devices: 47.9 us -> 49.8 us
    ppermute x16 -> x14, waiting for transfers between devices: 39.9 us -> 32.3 us  [step(): self.ends = tuple((lax.ppermute(e, 'seq', p) for e, p in zip(ends, perms)))]
    pallas_call x3, Pallas kernels: 27.7 us -> 21.5 us  [project(): pl.pallas_call(functools.partial(project_kernel, (len(operands), len(oper...]
    ppermute x3, waiting for transfers between devices: 5.31 us -> 0.01 us  [body(): lax.ppermute(carries[r], 'seq', xor_perm(n, r))]
    ppermute x2, waiting for transfers between devices: 1.57 us -> 6.73 us  [body(): returned.append(lax.ppermute(result, 'seq', swap))]
    ppermute x4, waiting for transfers between devices: 6.6 us -> 10.6 us  [body(): come = lax.ppermute(a, 'seq', swap)]
    unnamed x68 -> x52, local copies, waits for them, and re-layouts: 2.64 us -> 5.29 us
    ppermute x16 -> x14, starting transfers between devices: 23.3 us -> 25.8 us  [step(): self.ends = tuple((lax.ppermute(e, 'seq', p) for e, p in zip(ends, perms)))]
  transfers between devices with their start and end apart: 39 -> 37, of which waited for: 22 -> 18; matrix products, arithmetic and copies ran while one was open for 1% -> 1% of each run, Pallas kernels for 21% -> 20%
where the time goes in v4:
time: 171 us; the launch traced here: 170 us
  waiting for transfers between devices  73.7 us (43%)
  starting transfers between devices  49.8 us (29%)
  Pallas kernels  37.3 us (22%)
  local copies, waits for them, and re-layouts  9.07 us (5%)
    ppermute x14, waiting for transfers between devices, step(): self.ends = tuple((lax.ppermute(e, 'seq', p) for e, p in zip(ends, perms)))  32.3 us
    ppermute x14, starting transfers between devices, step(): self.ends = tuple((lax.ppermute(e, 'seq', p) for e, p in zip(ends, perms)))  25.8 us
    pallas_call x3, Pallas kernels, project(): pl.pallas_call(functools.partial(project_kernel, (len(operands), len(oper...  21.5 us
    ppermute x3, waiting for transfers between devices, body(): lax.ppermute(memory[r], 'seq', xor_perm(n, r))  15.5 us
    ppermute x4, waiting for transfers between devices, body(): come = lax.ppermute(a, 'seq', swap)  10.6 us
    ppermute x2, starting transfers between devices, body(): come = lax.ppermute(window, 'seq', [(s, s + step) for s in range(n - step)])  9.48 us
    ppermute x2, waiting for transfers between devices, body(): come = lax.ppermute(window, 'seq', [(s, s + step) for s in range(n - step)])  7.67 us
    ppermute x2, waiting for transfers between devices, body(): returned.append(lax.ppermute(result, 'seq', swap))  6.73 us
  transfers between devices with their start and end apart: 37, of which 18 were waited for; matrix products, arithmetic and copies ran while one was open for 1% of the time, Pallas kernels for 20%

profile of v4, /device:TPU:0, one launch (start us, length us, event | category | flops | bytes accessed | tf_op | source)
XLA Modules:
  0.0 170.2 jit_solution(3520723134239659743)
XLA Ops:
  1.4 3.1 %collective-permute-start.3 = (bf16[256,1024]{1,0:T(8,128)(2,1)S(1)}, bf16[256,1024]{1,0:T(8,128)(2,1)}, u32[]{:S(2)}, u32[]{:S(2)}) collective-permute-start(bf16[256,1024]{1,0:T(8,128)(2,1)S(1)} %get-tuple-element.82.refs_8_), channel_id=1, source_target_pairs={{0,8},{2,10},{8,16},{10,18},{16,24},{18,26},{24,28},{26,30},{28,20... | collective-permute-start | bytes 1572872 | tf_op jit(solution)/shard_map/ppermute | solution.py:467
  6.5 2.8 %shard_map.73 = (bf16[4,272,128]{2,1,0:T(8,128)(2,1)S(1)}, bf16[4,272,128]{2,1,0:T(8,128)(2,1)S(1)}, bf16[4,272,128]{2,1,0:T(8,128)(2,1)S(1)}, bf16[4,272,128]{2,1,0:T(8,128)(2,1)S(1)}, f32[4,512]{1,0:T(4,128)S(1)}) custom-call(s32[19]{0:T(128)S(1)} %fusion.info_ref, bf16[512,1024]{1,0:T(8,128)(2,1)S(1)} %copy-done.1, bf16[512,2048]{1,0:T(8,128)(2,1)S(1)} %copy-done, ...), custom_call_target="tpu_custom_call" | custom-call | tf_op jit(solution)/shard_map/pallas_call | solution.py:117
  12.9 6.1 %collective-permute-done.refs_1_ = bf16[4,272,128]{2,1,0:T(8,128)(2,1)S(1)} collective-permute-done((bf16[4,272,128]{2,1,0:T(8,128)(2,1)S(1)}, bf16[4,272,128]{2,1,0:T(8,128)(2,1)S(1)}, u32[]{:S(2)}, u32[]{:S(2)}) %collective-permute-start) | collective-permute-done | bytes 278560 | tf_op jit(solution)/shard_map/ppermute | solution.py:488
  19.0 9.4 %collective-permute-done.1.refs_2_ = bf16[4,272,128]{2,1,0:T(8,128)(2,1)S(1)} collective-permute-done((bf16[4,272,128]{2,1,0:T(8,128)(2,1)S(1)}, bf16[4,272,128]{2,1,0:T(8,128)(2,1)S(1)}, u32[]{:S(2)}, u32[]{:S(2)}) %collective-permute-start.1) | collective-permute-done | bytes 278560 | tf_op jit(solution)/shard_map/ppermute | solution.py:488
  34.5 3.3 %collective-permute-done.5.one_ref.two_ref = bf16[4,272,128]{2,1,0:T(8,128)(2,1)S(1)} collective-permute-done((bf16[4,272,128]{2,1,0:T(8,128)(2,1)S(1)}, bf16[4,272,128]{2,1,0:T(8,128)(2,1)S(1)}, u32[]{:S(2)}, u32[]{:S(2)}) %collective-permute-start.5) | collective-permute-done | bytes 278560 | tf_op jit(solution)/shard_map/ppermute | solution.py:499
  38.6 8.2 %collective-permute-start.6 = (bf16[4,272,128]{2,1,0:T(8,128)(2,1)S(1)}, bf16[4,272,128]{2,1,0:T(8,128)(2,1)S(1)}, u32[]{:S(2)}, u32[]{:S(2)}) collective-permute-start(bf16[4,272,128]{2,1,0:T(8,128)(2,1)S(1)} %shard_map.75), channel_id=1, source_target_pairs={{0,16},{2,18},{4,20},{6,22},{8,24},{10,26},{12,28},{14,30},{1,17},... | collective-permute-start | bytes 835592 | tf_op jit(solution)/shard_map/ppermute | solution.py:499
  46.8 2.3 %collective-permute-done.8.refs_11_ = bf16[256,1024]{1,0:T(8,128)(2,1)S(1)} collective-permute-done((bf16[256,1024]{1,0:T(8,128)(2,1)}, bf16[256,1024]{1,0:T(8,128)(2,1)S(1)}, u32[]{:S(2)}, u32[]{:S(2)}) %collective-permute-start.8) | collective-permute-done | bytes 524320 | tf_op jit(solution)/shard_map/ppermute | solution.py:467
  49.1 4.4 %collective-permute-done.6.one_ref = bf16[4,272,128]{2,1,0:T(8,128)(2,1)S(1)} collective-permute-done((bf16[4,272,128]{2,1,0:T(8,128)(2,1)S(1)}, bf16[4,272,128]{2,1,0:T(8,128)(2,1)S(1)}, u32[]{:S(2)}, u32[]{:S(2)}) %collective-permute-start.6) | collective-permute-done | bytes 278560 | tf_op jit(solution)/shard_map/ppermute | solution.py:499
  59.1 5.1 %shard_map.77 = (f32[512,2048]{1,0:T(8,128)S(1)}, f32[4,512,128]{2,1,0:T(8,128)S(1)}) custom-call(bf16[512,1024]{1,0:T(8,128)(2,1)S(1)} %copy-done.3, bf16[512,1024]{1,0:T(8,128)(2,1)S(1)} %copy-done.2, bf16[512,2048]{1,0:T(8,128)(2,1)S(1)} %copy-done, f32[4,1,512]{2,1,0:T(1,128)S(1)} %broadcast_in_dim.6.in_ref, f32[4,1,512]{2,1,0:T(1,128)S(1)} %broadcast_in_dim.7.g_ref), custom_call_target="tpu_custom_call" | custom-call | tf_op jit(solution)/shard_map/pallas_call | solution.py:256
  64.2 7.1 %collective-permute-start.15 = (bf16[256,1024]{1,0:T(8,128)(2,1)S(1)}, bf16[256,1024]{1,0:T(8,128)(2,1)}, u32[]{:S(2)}, u32[]{:S(2)}) collective-permute-start(bf16[256,1024]{1,0:T(8,128)(2,1)S(1)} %collective-permute-done.8.refs_11_), channel_id=1, source_target_pairs={{0,8},{2,10},{8,16},{10,18},{16,24},{18,26},{24,28},{26,30},{28,20... | collective-permute-start | bytes 1572872 | tf_op jit(solution)/shard_map/ppermute | solution.py:467
  71.4 4.1 %shard_map.78 = (bf16[128,2048]{1,0:T(8,128)(2,1)S(1)}, bf16[128,2048]{1,0:T(8,128)(2,1)S(1)}, bf16[128,2048]{1,0:T(8,128)(2,1)}, bf16[128,2048]{1,0:T(8,128)(2,1)}) custom-call(s32[19]{0:T(128)S(1)} %fusion.info_ref, bf16[512,1024]{1,0:T(8,128)(2,1)S(1)} %copy-done.3, bf16[4,272,128]{2,1,0:T(8,128)(2,1)S(1)} %get-tuple-element.53.refs_0_, ...), custom_call_target="tpu_custom_call" | custom-call | tf_op jit(solution)/shard_map/pallas_call | solution.py:308
  75.5 3.5 %collective-permute-start.17 = (bf16[256,1024]{1,0:T(8,128)(2,1)S(1)}, bf16[256,1024]{1,0:T(8,128)(2,1)S(1)}, u32[]{:S(2)}, u32[]{:S(2)}) collective-permute-start(bf16[256,1024]{1,0:T(8,128)(2,1)S(1)} %collective-permute-done.7.refs_16_), channel_id=1, source_target_pairs={{0,8},{2,10},{8,16},{10,18},{16,24},{18,26},{24,28},{26,30},{28,20... | collective-permute-start | bytes 1572872 | tf_op jit(solution)/shard_map/ppermute | solution.py:467
  80.2 2.7 %collective-permute-done.15.refs_13_ = bf16[256,1024]{1,0:T(8,128)(2,1)} collective-permute-done((bf16[256,1024]{1,0:T(8,128)(2,1)S(1)}, bf16[256,1024]{1,0:T(8,128)(2,1)}, u32[]{:S(2)}, u32[]{:S(2)}) %collective-permute-start.15) | collective-permute-done | bytes 524320 | tf_op jit(solution)/shard_map/ppermute | solution.py:467
  85.1 6.9 %collective-permute-done.17.refs_17_ = bf16[256,1024]{1,0:T(8,128)(2,1)S(1)} collective-permute-done((bf16[256,1024]{1,0:T(8,128)(2,1)S(1)}, bf16[256,1024]{1,0:T(8,128)(2,1)S(1)}, u32[]{:S(2)}, u32[]{:S(2)}) %collective-permute-start.17) | collective-permute-done | bytes 524320 | tf_op jit(solution)/shard_map/ppermute | solution.py:467
  92.5 2.2 %collective-permute-start.21 = (bf16[256,1024]{1,0:T(8,128)(2,1)S(1)}, bf16[256,1024]{1,0:T(8,128)(2,1)S(1)}, u32[]{:S(2)}, u32[]{:S(2)}) collective-permute-start(bf16[256,1024]{1,0:T(8,128)(2,1)S(1)} %collective-permute-done.17.refs_17_), channel_id=1, source_target_pairs={{0,8},{2,10},{8,16},{10,18},{16,24},{18,26},{24,28},{26,30},{28,20... | collective-permute-start | bytes 1572872 | tf_op jit(solution)/shard_map/ppermute | solution.py:467
  97.3 7.9 %collective-permute-done.21.refs_19_ = bf16[256,1024]{1,0:T(8,128)(2,1)S(1)} collective-permute-done((bf16[256,1024]{1,0:T(8,128)(2,1)S(1)}, bf16[256,1024]{1,0:T(8,128)(2,1)S(1)}, u32[]{:S(2)}, u32[]{:S(2)}) %collective-permute-start.21) | collective-permute-done | bytes 524320 | tf_op jit(solution)/shard_map/ppermute | solution.py:467
  106.7 5.8 %collective-permute-start.26 = (bf16[256,1024]{1,0:T(8,128)(2,1)S(1)}, bf16[256,1024]{1,0:T(8,128)(2,1)S(1)}, u32[]{:S(2)}, u32[]{:S(2)}) collective-permute-start(bf16[256,1024]{1,0:T(8,128)(2,1)S(1)} %collective-permute-done.21.refs_19_), channel_id=1, source_target_pairs={{0,8},{2,10},{8,16},{10,18},{16,24},{18,26},{24,28},{26,30},{28,20... | collective-permute-start | bytes 1572872 | tf_op jit(solution)/shard_map/ppermute | solution.py:467
  113.9 8.3 %collective-permute-done.26.refs_21_ = bf16[256,1024]{1,0:T(8,128)(2,1)S(1)} collective-permute-done((bf16[256,1024]{1,0:T(8,128)(2,1)S(1)}, bf16[256,1024]{1,0:T(8,128)(2,1)S(1)}, u32[]{:S(2)}, u32[]{:S(2)}) %collective-permute-start.26) | collective-permute-done | bytes 524320 | tf_op jit(solution)/shard_map/ppermute | solution.py:467
  122.2 2.2 %collective-permute-done.27.refs_22_ = bf16[256,1024]{1,0:T(8,128)(2,1)S(1)} collective-permute-done((bf16[256,1024]{1,0:T(8,128)(2,1)S(1)}, bf16[256,1024]{1,0:T(8,128)(2,1)S(1)}, u32[]{:S(2)}, u32[]{:S(2)}) %collective-permute-start.27) | collective-permute-done | bytes 524320 | tf_op jit(solution)/shard_map/ppermute | solution.py:467
  127.0 9.0 %collective-permute-done.29.refs_6_ = bf16[128,2048]{1,0:T(8,128)(2,1)} collective-permute-done((bf16[128,2048]{1,0:T(8,128)(2,1)}, bf16[128,2048]{1,0:T(8,128)(2,1)}, u32[]{:S(2)}, u32[]{:S(2)}) %collective-permute-start.29) | collective-permute-done | bytes 524320 | tf_op jit(solution)/shard_map/ppermute | solution.py:535
  138.2 5.9 %shard_map.81 = bf16[512,512]{1,0:T(8,128)(2,1)S(1)} custom-call(s32[19]{0:T(128)S(1)} %fusion.info_ref, bf16[128,2048]{1,0:T(8,128)(2,1)S(1)} %collective-permute-done.13.refs_0_, bf16[128,2048]{1,0:T(8,128)(2,1)S(1)} %collective-permute-done.14.refs_1_, bf16[128,2048]{1,0:T(8,128)(2,1)S(1)} %collective-permute-done.19.refs_2_, ...), custom_call_target="tpu_custom_call" | custom-call | flops 2147483648 | bytes 8912896 | tf_op jit(solution)/shard_map/pallas_call | solution.py:383
  144.5 6.0 %shard_map.79 = bf16[512,512]{1,0:T(8,128)(2,1)S(1)} custom-call(s32[19]{0:T(128)S(1)} %fusion.info_ref, bf16[128,2048]{1,0:T(8,128)(2,1)S(1)} %collective-permute-done.13.refs_0_, bf16[128,2048]{1,0:T(8,128)(2,1)S(1)} %collective-permute-done.14.refs_1_, bf16[128,2048]{1,0:T(8,128)(2,1)S(1)} %collective-permute-done.19.refs_2_, ...), custom_call_target="tpu_custom_call" | custom-call | flops 2147483648 | bytes 8912896 | tf_op jit(solution)/shard_map/pallas_call | solution.py:383
  152.2 9.6 %shard_map.80 = bf16[512,2048]{1,0:T(8,128)(2,1)} custom-call(s32[19]{0:T(128)S(1)} %fusion.info_ref, bf16[128,2048]{1,0:T(8,128)(2,1)S(1)} %copy-done.7, bf16[128,2048]{1,0:T(8,128)(2,1)S(1)} %copy-done.11, bf16[128,2048]{1,0:T(8,128)(2,1)S(1)} %copy-done.9, bf16[128,2048]{1,0:T(8,128)(2,1)S(1)} %copy-done.13, bf16[128,2048]{1,0:T(8,128)(2,1)} %get-tuple-element.73.refs_4_, ...), custom_call_target="tpu_custom_call" | custom-call | flops 4294967296 | bytes 13631488 | tf_op jit(solution)/shard_map/pallas_call | solution.py:383
  162.7 6.7 %collective-permute-done.36 = bf16[512,512]{1,0:T(8,128)(2,1)S(1)} collective-permute-done((bf16[512,512]{1,0:T(8,128)(2,1)S(1)}, bf16[512,512]{1,0:T(8,128)(2,1)S(1)}, u32[]{:S(2)}, u32[]{:S(2)}) %collective-permute-start.36) | collective-permute-done | bytes 524320 | tf_op jit(solution)/shard_map/ppermute | solution.py:554
  (117 shorter events, 37.3 us)
Async XLA Ops:
  1.4 26.9 %collective-permute-start.3 = (bf16[256,1024]{1,0:T(8,128)(2,1)S(1)}, bf16[256,1024]{1,0:T(8,128)(2,1)}, u32[]{:S(2)}, u32[]{:S(2)}) collective-permute-start(bf16[256,1024]{1,0:T(8,128)(2,1)S(1)} %get-tuple-element.82.refs_8_), channel_id=1, source_target_pairs={{0,8},{2,10},{8,16},{10,18},{16,24},{18,26},{24,28},{26,30},{28,20... | collective-permute-start | bytes 1572872 | tf_op jit(solution)/shard_map/ppermute | solution.py:467
  4.5 23.8 %collective-permute-start.4 = (bf16[256,1024]{1,0:T(8,128)(2,1)S(1)}, bf16[256,1024]{1,0:T(8,128)(2,1)}, u32[]{:S(2)}, u32[]{:S(2)}) collective-permute-start(bf16[256,1024]{1,0:T(8,128)(2,1)S(1)} %get-tuple-element.82.refs_8_), channel_id=1, source_target_pairs={{8,0},{10,2},{16,8},{18,10},{24,16},{26,18},{28,24},{30,26},{20,28... | collective-permute-start | bytes 1572872 | tf_op jit(solution)/shard_map/ppermute | solution.py:467
  11.3 17.0 %collective-permute-start.1 = (bf16[4,272,128]{2,1,0:T(8,128)(2,1)S(1)}, bf16[4,272,128]{2,1,0:T(8,128)(2,1)S(1)}, u32[]{:S(2)}, u32[]{:S(2)}) collective-permute-start(bf16[4,272,128]{2,1,0:T(8,128)(2,1)S(1)} %get-tuple-element.45), channel_id=1, source_target_pairs={{0,4},{2,6},{4,0},{6,2},{8,12},{10,14},{12,8},{14,10},{16,20},{18,... | collective-permute-start | bytes 835592 | tf_op jit(solution)/shard_map/ppermute | solution.py:488
  12.8 15.5 %collective-permute-start.2 = (bf16[4,272,128]{2,1,0:T(8,128)(2,1)S(1)}, bf16[4,272,128]{2,1,0:T(8,128)(2,1)S(1)}, u32[]{:S(2)}, u32[]{:S(2)}) collective-permute-start(bf16[4,272,128]{2,1,0:T(8,128)(2,1)S(1)} %get-tuple-element.46), channel_id=1, source_target_pairs={{0,6},{2,4},{4,2},{6,0},{8,14},{10,12},{12,10},{14,8},{16,22},{18,... | collective-permute-start | bytes 835592 | tf_op jit(solution)/shard_map/ppermute | solution.py:488
  30.7 16.1 %collective-permute-start.7 = (bf16[256,1024]{1,0:T(8,128)(2,1)S(1)}, bf16[256,1024]{1,0:T(8,128)(2,1)S(1)}, u32[]{:S(2)}, u32[]{:S(2)}) collective-permute-start(bf16[256,1024]{1,0:T(8,128)(2,1)S(1)} %get-tuple-element.51), channel_id=1, source_target_pairs={{0,2},{2,0},{4,6},{6,4},{8,10},{10,8},{12,14},{14,12},{16,18},{18,... | collective-permute-start | bytes 1572872 | tf_op jit(solution)/shard_map/ppermute | solution.py:494
  32.5 16.6 %collective-permute-start.8 = (bf16[256,1024]{1,0:T(8,128)(2,1)}, bf16[256,1024]{1,0:T(8,128)(2,1)S(1)}, u32[]{:S(2)}, u32[]{:S(2)}) collective-permute-start(bf16[256,1024]{1,0:T(8,128)(2,1)} %collective-permute-done.3.refs_9_), channel_id=1, source_target_pairs={{0,8},{2,10},{8,16},{10,18},{16,24},{18,26},{24,28},{26,30},{28,20... | collective-permute-start | bytes 1572872 | tf_op jit(solution)/shard_map/ppermute | solution.py:467
  32.5 16.7 %collective-permute-start.9 = (bf16[256,1024]{1,0:T(8,128)(2,1)}, bf16[256,1024]{1,0:T(8,128)(2,1)S(1)}, u32[]{:S(2)}, u32[]{:S(2)}) collective-permute-start(bf16[256,1024]{1,0:T(8,128)(2,1)} %collective-permute-done.4.refs_10_), channel_id=1, source_target_pairs={{8,0},{10,2},{16,8},{18,10},{24,16},{26,18},{28,24},{30,26},{20,28... | collective-permute-start | bytes 1572872 | tf_op jit(solution)/shard_map/ppermute | solution.py:467
  38.6 14.9 %collective-permute-start.6 = (bf16[4,272,128]{2,1,0:T(8,128)(2,1)S(1)}, bf16[4,272,128]{2,1,0:T(8,128)(2,1)S(1)}, u32[]{:S(2)}, u32[]{:S(2)}) collective-permute-start(bf16[4,272,128]{2,1,0:T(8,128)(2,1)S(1)} %shard_map.75), channel_id=1, source_target_pairs={{0,16},{2,18},{4,20},{6,22},{8,24},{10,26},{12,28},{14,30},{1,17},... | collective-permute-start | bytes 835592 | tf_op jit(solution)/shard_map/ppermute | solution.py:499
  55.5 15.9 %collective-permute-start.10 = (bf16[4,272,128]{2,1,0:T(8,128)(2,1)S(1)}, bf16[4,272,128]{2,1,0:T(8,128)(2,1)S(1)}, u32[]{:S(2)}, u32[]{:S(2)}) collective-permute-start(bf16[4,272,128]{2,1,0:T(8,128)(2,1)S(1)} %get-tuple-element.54), channel_id=1, source_target_pairs={{0,2},{2,0},{4,6},{6,4},{8,10},{10,8},{12,14},{14,12},{16,18},{18,... | collective-permute-start | bytes 835592 | tf_op jit(solution)/shard_map/ppermute | solution.py:518
  57.0 14.4 %collective-permute-start.11 = (bf16[4,272,128]{2,1,0:T(8,128)(2,1)S(1)}, bf16[4,272,128]{2,1,0:T(8,128)(2,1)S(1)}, u32[]{:S(2)}, u32[]{:S(2)}) collective-permute-start(bf16[4,272,128]{2,1,0:T(8,128)(2,1)S(1)} %get-tuple-element.55), channel_id=1, source_target_pairs={{0,4},{2,6},{4,0},{6,2},{8,12},{10,14},{12,8},{14,10},{16,20},{18,... | collective-permute-start | bytes 835592 | tf_op jit(solution)/shard_map/ppermute | solution.py:518
  58.4 13.0 %collective-permute-start.12 = (bf16[4,272,128]{2,1,0:T(8,128)(2,1)S(1)}, bf16[4,272,128]{2,1,0:T(8,128)(2,1)S(1)}, u32[]{:S(2)}, u32[]{:S(2)}) collective-permute-start(bf16[4,272,128]{2,1,0:T(8,128)(2,1)S(1)} %get-tuple-element.56), channel_id=1, source_target_pairs={{0,6},{2,4},{4,2},{6,0},{8,14},{10,12},{12,10},{14,8},{16,22},{18,... | collective-permute-start | bytes 835592 | tf_op jit(solution)/shard_map/ppermute | solution.py:518
  64.2 18.6 %collective-permute-start.15 = (bf16[256,1024]{1,0:T(8,128)(2,1)S(1)}, bf16[256,1024]{1,0:T(8,128)(2,1)}, u32[]{:S(2)}, u32[]{:S(2)}) collective-permute-start(bf16[256,1024]{1,0:T(8,128)(2,1)S(1)} %collective-permute-done.8.refs_11_), channel_id=1, source_target_pairs={{0,8},{2,10},{8,16},{10,18},{16,24},{18,26},{24,28},{26,30},{28,20... | collective-permute-start | bytes 1572872 | tf_op jit(solution)/shard_map/ppermute | solution.py:467
  71.4 13.7 %collective-permute-start.16 = (bf16[256,1024]{1,0:T(8,128)(2,1)S(1)}, bf16[256,1024]{1,0:T(8,128)(2,1)S(1)}, u32[]{:S(2)}, u32[]{:S(2)}) collective-permute-start(bf16[256,1024]{1,0:T(8,128)(2,1)S(1)} %collective-permute-done.9.refs_12_), channel_id=1, source_target_pairs={{8,0},{10,2},{16,8},{18,10},{24,16},{26,18},{28,24},{30,26},{20,28... | collective-permute-start | bytes 1572872 | tf_op jit(solution)/shard_map/ppermute | solution.py:467
  75.5 16.5 %collective-permute-start.17 = (bf16[256,1024]{1,0:T(8,128)(2,1)S(1)}, bf16[256,1024]{1,0:T(8,128)(2,1)S(1)}, u32[]{:S(2)}, u32[]{:S(2)}) collective-permute-start(bf16[256,1024]{1,0:T(8,128)(2,1)S(1)} %collective-permute-done.7.refs_16_), channel_id=1, source_target_pairs={{0,8},{2,10},{8,16},{10,18},{16,24},{18,26},{24,28},{26,30},{28,20... | collective-permute-start | bytes 1572872 | tf_op jit(solution)/shard_map/ppermute | solution.py:467
  79.0 13.5 %collective-permute-start.18 = (bf16[256,1024]{1,0:T(8,128)(2,1)S(1)}, bf16[256,1024]{1,0:T(8,128)(2,1)S(1)}, u32[]{:S(2)}, u32[]{:S(2)}) collective-permute-start(bf16[256,1024]{1,0:T(8,128)(2,1)S(1)} %collective-permute-done.7.refs_16_), channel_id=1, source_target_pairs={{8,0},{10,2},{16,8},{18,10},{24,16},{26,18},{28,24},{30,26},{20,28... | collective-permute-start | bytes 1572872 | tf_op jit(solution)/shard_map/ppermute | solution.py:467
  79.0 13.5 %collective-permute-start.13 = (bf16[128,2048]{1,0:T(8,128)(2,1)S(1)}, bf16[128,2048]{1,0:T(8,128)(2,1)S(1)}, u32[]{:S(2)}, u32[]{:S(2)}) collective-permute-start(bf16[128,2048]{1,0:T(8,128)(2,1)S(1)} %get-tuple-element.80.refs_0_), channel_id=1, source_target_pairs={{0,2},{2,0},{4,6},{6,4},{8,10},{10,8},{12,14},{14,12},{16,18},{18,... | collective-permute-start | bytes 1572872 | tf_op jit(solution)/shard_map/ppermute | solution.py:535
  92.5 12.7 %collective-permute-start.21 = (bf16[256,1024]{1,0:T(8,128)(2,1)S(1)}, bf16[256,1024]{1,0:T(8,128)(2,1)S(1)}, u32[]{:S(2)}, u32[]{:S(2)}) collective-permute-start(bf16[256,1024]{1,0:T(8,128)(2,1)S(1)} %collective-permute-done.17.refs_17_), channel_id=1, source_target_pairs={{0,8},{2,10},{8,16},{10,18},{16,24},{18,26},{24,28},{26,30},{28,20... | collective-permute-start | bytes 1572872 | tf_op jit(solution)/shard_map/ppermute | solution.py:467
  96.0 17.0 %collective-permute-start.28 = (bf16[128,2048]{1,0:T(8,128)(2,1)S(1)}, bf16[128,2048]{1,0:T(8,128)(2,1)S(1)}, u32[]{:S(2)}, u32[]{:S(2)}) collective-permute-start(bf16[128,2048]{1,0:T(8,128)(2,1)S(1)} %get-tuple-element.69.refs_2_), channel_id=1, source_target_pairs={{0,1},{1,0},{2,3},{3,2},{4,5},{5,4},{6,7},{7,6},{8,9},{9,8},{10,11... | collective-permute-start | bytes 1572872 | tf_op jit(solution)/shard_map/ppermute | solution.py:528
  106.7 15.5 %collective-permute-start.26 = (bf16[256,1024]{1,0:T(8,128)(2,1)S(1)}, bf16[256,1024]{1,0:T(8,128)(2,1)S(1)}, u32[]{:S(2)}, u32[]{:S(2)}) collective-permute-start(bf16[256,1024]{1,0:T(8,128)(2,1)S(1)} %collective-permute-done.21.refs_19_), channel_id=1, source_target_pairs={{0,8},{2,10},{8,16},{10,18},{16,24},{18,26},{24,28},{26,30},{28,20... | collective-permute-start | bytes 1572872 | tf_op jit(solution)/shard_map/ppermute | solution.py:467
  124.9 12.4 %collective-permute-start.31 = (bf16[256,1024]{1,0:T(8,128)(2,1)}, bf16[256,1024]{1,0:T(8,128)(2,1)}, u32[]{:S(2)}, u32[]{:S(2)}) collective-permute-start(bf16[256,1024]{1,0:T(8,128)(2,1)} %collective-permute-done.15.refs_13_), channel_id=1, source_target_pairs={{0,8},{2,10},{8,16},{10,18},{16,24},{18,26},{24,28},{26,30},{28,20... | collective-permute-start | bytes 1572872 | tf_op jit(solution)/shard_map/ppermute | solution.py:467
  136.0 16.2 %collective-permute-start.33 = (bf16[128,2048]{1,0:T(8,128)(2,1)}, bf16[128,2048]{1,0:T(8,128)(2,1)}, u32[]{:S(2)}, u32[]{:S(2)}) collective-permute-start(bf16[128,2048]{1,0:T(8,128)(2,1)} %get-tuple-element.73.refs_4_), channel_id=1, source_target_pairs={{0,1},{1,0},{2,3},{3,2},{4,5},{5,4},{6,7},{7,6},{8,9},{9,8},{10,11... | collective-permute-start | bytes 1572872 | tf_op jit(solution)/shard_map/ppermute | solution.py:528
  137.3 14.9 %collective-permute-start.34 = (bf16[128,2048]{1,0:T(8,128)(2,1)}, bf16[128,2048]{1,0:T(8,128)(2,1)}, u32[]{:S(2)}, u32[]{:S(2)}) collective-permute-start(bf16[128,2048]{1,0:T(8,128)(2,1)} %get-tuple-element.77.refs_6_), channel_id=1, source_target_pairs={{0,1},{1,0},{2,3},{3,2},{4,5},{5,4},{6,7},{7,6},{8,9},{9,8},{10,11... | collective-permute-start | bytes 1572872 | tf_op jit(solution)/shard_map/ppermute | solution.py:528
  144.1 17.7 %collective-permute-start.35 = (bf16[512,512]{1,0:T(8,128)(2,1)S(1)}, bf16[512,512]{1,0:T(8,128)(2,1)S(1)}, u32[]{:S(2)}, u32[]{:S(2)}) collective-permute-start(bf16[512,512]{1,0:T(8,128)(2,1)S(1)} %shard_map.81), channel_id=1, source_target_pairs={{0,2},{2,0},{4,6},{6,4},{8,10},{10,8},{12,14},{14,12},{16,18},{18,... | collective-permute-start | bytes 1572872 | tf_op jit(solution)/shard_map/ppermute | solution.py:554
  150.5 18.9 %collective-permute-start.36 = (bf16[512,512]{1,0:T(8,128)(2,1)S(1)}, bf16[512,512]{1,0:T(8,128)(2,1)S(1)}, u32[]{:S(2)}, u32[]{:S(2)}) collective-permute-start(bf16[512,512]{1,0:T(8,128)(2,1)S(1)} %shard_map.79), channel_id=1, source_target_pairs={{0,2},{2,0},{4,6},{6,4},{8,10},{10,8},{12,14},{14,12},{16,18},{18,... | collective-permute-start | bytes 1572872 | tf_op jit(solution)/shard_map/ppermute | solution.py:554
  (39 other events, 558.9 us)

commit v5 on v4

--- a/solution.py
+++ b/solution.py
@@ -271,7 +271,7 @@
             pl.BlockSpec((length, value_size), lambda h: (0, h)),
             per_head(length, LANES),
         ),
-        compiler_params=pltpu.CompilerParams(vmem_limit_bytes=40 * MIB),
+        compiler_params=pltpu.CompilerParams(vmem_limit_bytes=50 * MIB),
     )(queries, keys, values, gate_in[:, None], g[:, None])
 
 
@@ -317,7 +317,7 @@
         ],
         out_specs=(pl.BlockSpec((piece, value_size), lambda h: (0, h)),) * chunks,
         scratch_shapes=[pltpu.VMEM((key_size, value_size), BF16)],
-        compiler_params=pltpu.CompilerParams(vmem_limit_bytes=40 * MIB),
+        compiler_params=pltpu.CompilerParams(vmem_limit_bytes=50 * MIB),
     )(info, queries, *carries, part, stat)
 
 
@@ -541,11 +541,12 @@
         for ring in rings:
             if ring.more() and (ring is ring_other or late):
                 ring.step(*gate)
-        own.append(all_heads(a))
+        own.append(a)
         sent.append(all_heads(come))
-        gate = (come, *ends, *ring_other.ends, *own[-2:-1], *sent[-2:-1])
+        gate = (come, *ends, *ring_other.ends, *sent[-2:-1])
         gate = jax.tree.leaves(gate)
     pieces = ring_mine.got + ring_other.got
+    own = [all_heads(a) for a in own]
     halves = 2
     width = share // halves
     returned = []

time: 171 us -> 168 us (0.982)
  Pallas kernels: 37.3 us -> 41.2 us
  starting transfers between devices: 49.8 us -> 46.9 us
  local copies, waits for them, and re-layouts: 9.07 us -> 6.79 us
    ppermute x14, starting transfers between devices: 25.8 us -> 21.2 us  [step(): self.ends = tuple((lax.ppermute(e, 'seq', p) for e, p in zip(ends, perms)))]
    unnamed x52 -> x42, local copies, waits for them, and re-layouts: 5.29 us -> 3.01 us
    ppermute x14, waiting for transfers between devices: 32.3 us -> 34.6 us  [step(): self.ends = tuple((lax.ppermute(e, 'seq', p) for e, p in zip(ends, perms)))]
    ppermute x4, starting transfers between devices: 2.54 us -> 4.67 us  [body(): come = lax.ppermute(a, 'seq', swap)]
    ppermute x4, waiting for transfers between devices: 10.6 us -> 8.64 us  [body(): come = lax.ppermute(a, 'seq', swap)]
    pallas_call x1, Pallas kernels: 5.12 us -> 6.95 us  [intra(): pl.pallas_call(intra_kernel, grid=(heads,), out_shape=(jax.ShapeDtypeStru...]
  transfers between devices with their start and end apart: 37 -> 37, of which waited for: 18 -> 19; matrix products, arithmetic and copies ran while one was open for 1% -> 1% of each run, Pallas kernels for 20% -> 23%
where the time goes in v5:
time: 168 us
  waiting for transfers between devices  72.9 us (43%)
  starting transfers between devices  46.9 us (28%)
  Pallas kernels  41.2 us (25%)
  local copies, waits for them, and re-layouts  6.79 us (4%)
    ppermute x14, waiting for transfers between devices, step(): self.ends = tuple((lax.ppermute(e, 'seq', p) for e, p in zip(ends, perms)))  34.6 us
    pallas_call x3, Pallas kernels, project(): pl.pallas_call(functools.partial(project_kernel, (len(operands), len(oper...  22 us
    ppermute x14, starting transfers between devices, step(): self.ends = tuple((lax.ppermute(e, 'seq', p) for e, p in zip(ends, perms)))  21.2 us
    ppermute x3, waiting for transfers between devices, body(): lax.ppermute(memory[r], 'seq', xor_perm(n, r))  15.5 us
    ppermute x2, starting transfers between devices, body(): come = lax.ppermute(window, 'seq', [(s, s + step) for s in range(n - step)])  9.48 us
    ppermute x4, waiting for transfers between devices, body(): come = lax.ppermute(a, 'seq', swap)  8.64 us
    ppermute x2, waiting for transfers between devices, body(): come = lax.ppermute(window, 'seq', [(s, s + step) for s in range(n - step)])  7.67 us
    pallas_call x1, Pallas kernels, intra(): pl.pallas_call(intra_kernel, grid=(heads,), out_shape=(jax.ShapeDtypeStru...  6.95 us
  transfers between devices with their start and end apart: 37, of which 19 were waited for; matrix products, arithmetic and copies ran while one was open for 1% of the time, Pallas kernels for 23%

profile of v5, /device:TPU:0, one launch (start us, length us, event | category | flops | bytes accessed | tf_op | source)
XLA Modules:
  0.0 168.0 jit_solution(12571803273143353066)
XLA Ops:
  1.4 3.1 %collective-permute-start.3 = (bf16[256,1024]{1,0:T(8,128)(2,1)S(1)}, bf16[256,1024]{1,0:T(8,128)(2,1)}, u32[]{:S(2)}, u32[]{:S(2)}) collective-permute-start(bf16[256,1024]{1,0:T(8,128)(2,1)S(1)} %get-tuple-element.82.refs_8_), channel_id=1, source_target_pairs={{0,8},{2,10},{8,16},{10,18},{16,24},{18,26},{24,28},{26,30},{28,20... | collective-permute-start | bytes 1572872 | tf_op jit(solution)/shard_map/ppermute | solution.py:467
  6.5 2.8 %shard_map.73 = (bf16[4,272,128]{2,1,0:T(8,128)(2,1)S(1)}, bf16[4,272,128]{2,1,0:T(8,128)(2,1)S(1)}, bf16[4,272,128]{2,1,0:T(8,128)(2,1)S(1)}, bf16[4,272,128]{2,1,0:T(8,128)(2,1)S(1)}, f32[4,512]{1,0:T(4,128)S(1)}) custom-call(s32[19]{0:T(128)S(1)} %fusion.info_ref, bf16[512,1024]{1,0:T(8,128)(2,1)S(1)} %copy-done.1, bf16[512,2048]{1,0:T(8,128)(2,1)S(1)} %copy-done, ...), custom_call_target="tpu_custom_call" | custom-call | tf_op jit(solution)/shard_map/pallas_call | solution.py:117
  12.9 6.1 %collective-permute-done.refs_1_ = bf16[4,272,128]{2,1,0:T(8,128)(2,1)S(1)} collective-permute-done((bf16[4,272,128]{2,1,0:T(8,128)(2,1)S(1)}, bf16[4,272,128]{2,1,0:T(8,128)(2,1)S(1)}, u32[]{:S(2)}, u32[]{:S(2)}) %collective-permute-start) | collective-permute-done | bytes 278560 | tf_op jit(solution)/shard_map/ppermute | solution.py:488
  19.0 9.4 %collective-permute-done.1.refs_2_ = bf16[4,272,128]{2,1,0:T(8,128)(2,1)S(1)} collective-permute-done((bf16[4,272,128]{2,1,0:T(8,128)(2,1)S(1)}, bf16[4,272,128]{2,1,0:T(8,128)(2,1)S(1)}, u32[]{:S(2)}, u32[]{:S(2)}) %collective-permute-start.1) | collective-permute-done | bytes 278560 | tf_op jit(solution)/shard_map/ppermute | solution.py:488
  34.5 3.3 %collective-permute-done.5.one_ref.two_ref = bf16[4,272,128]{2,1,0:T(8,128)(2,1)S(1)} collective-permute-done((bf16[4,272,128]{2,1,0:T(8,128)(2,1)S(1)}, bf16[4,272,128]{2,1,0:T(8,128)(2,1)S(1)}, u32[]{:S(2)}, u32[]{:S(2)}) %collective-permute-start.5) | collective-permute-done | bytes 278560 | tf_op jit(solution)/shard_map/ppermute | solution.py:499
  38.6 8.2 %collective-permute-start.6 = (bf16[4,272,128]{2,1,0:T(8,128)(2,1)S(1)}, bf16[4,272,128]{2,1,0:T(8,128)(2,1)S(1)}, u32[]{:S(2)}, u32[]{:S(2)}) collective-permute-start(bf16[4,272,128]{2,1,0:T(8,128)(2,1)S(1)} %shard_map.75), channel_id=1, source_target_pairs={{0,16},{2,18},{4,20},{6,22},{8,24},{10,26},{12,28},{14,30},{1,17},... | collective-permute-start | bytes 835592 | tf_op jit(solution)/shard_map/ppermute | solution.py:499
  46.8 2.3 %collective-permute-done.8.refs_11_ = bf16[256,1024]{1,0:T(8,128)(2,1)S(1)} collective-permute-done((bf16[256,1024]{1,0:T(8,128)(2,1)}, bf16[256,1024]{1,0:T(8,128)(2,1)S(1)}, u32[]{:S(2)}, u32[]{:S(2)}) %collective-permute-start.8) | collective-permute-done | bytes 524320 | tf_op jit(solution)/shard_map/ppermute | solution.py:467
  49.1 4.4 %collective-permute-done.6.one_ref = bf16[4,272,128]{2,1,0:T(8,128)(2,1)S(1)} collective-permute-done((bf16[4,272,128]{2,1,0:T(8,128)(2,1)S(1)}, bf16[4,272,128]{2,1,0:T(8,128)(2,1)S(1)}, u32[]{:S(2)}, u32[]{:S(2)}) %collective-permute-start.6) | collective-permute-done | bytes 278560 | tf_op jit(solution)/shard_map/ppermute | solution.py:499
  59.1 6.9 %shard_map.77 = (f32[512,2048]{1,0:T(8,128)}, f32[4,512,128]{2,1,0:T(8,128)S(1)}) custom-call(bf16[512,1024]{1,0:T(8,128)(2,1)S(1)} %copy-done.3, bf16[512,1024]{1,0:T(8,128)(2,1)S(1)} %copy-done.2, bf16[512,2048]{1,0:T(8,128)(2,1)} %v_ref.3, f32[4,1,512]{2,1,0:T(1,128)S(1)} %broadcast_in_dim.6.in_ref, f32[4,1,512]{2,1,0:T(1,128)S(1)} %broadcast_in_dim.7.g_ref), custom_call_target="tpu_custom_call" | custom-call | tf_op jit(solution)/shard_map/pallas_call | solution.py:256
  67.1 7.1 %collective-permute-start.15 = (bf16[256,1024]{1,0:T(8,128)(2,1)S(1)}, bf16[256,1024]{1,0:T(8,128)(2,1)S(1)}, u32[]{:S(2)}, u32[]{:S(2)}) collective-permute-start(bf16[256,1024]{1,0:T(8,128)(2,1)S(1)} %collective-permute-done.8.refs_11_), channel_id=1, source_target_pairs={{0,8},{2,10},{8,16},{10,18},{16,24},{18,26},{24,28},{26,30},{28,20... | collective-permute-start | bytes 1572872 | tf_op jit(solution)/shard_map/ppermute | solution.py:467
  74.2 5.6 %shard_map.78 = (bf16[128,2048]{1,0:T(8,128)(2,1)}, bf16[128,2048]{1,0:T(8,128)(2,1)}, bf16[128,2048]{1,0:T(8,128)(2,1)}, bf16[128,2048]{1,0:T(8,128)(2,1)}) custom-call(s32[19]{0:T(128)S(1)} %fusion.info_ref, bf16[512,1024]{1,0:T(8,128)(2,1)} %q_ref.3, bf16[4,272,128]{2,1,0:T(8,128)(2,1)S(1)} %get-tuple-element.53.refs_0_, ...), custom_call_target="tpu_custom_call" | custom-call | tf_op jit(solution)/shard_map/pallas_call | solution.py:308
  82.3 3.6 %collective-permute-done.15.refs_13_ = bf16[256,1024]{1,0:T(8,128)(2,1)S(1)} collective-permute-done((bf16[256,1024]{1,0:T(8,128)(2,1)S(1)}, bf16[256,1024]{1,0:T(8,128)(2,1)S(1)}, u32[]{:S(2)}, u32[]{:S(2)}) %collective-permute-start.15) | collective-permute-done | bytes 524320 | tf_op jit(solution)/shard_map/ppermute | solution.py:467
  87.7 5.4 %collective-permute-done.17.refs_17_ = bf16[256,1024]{1,0:T(8,128)(2,1)S(1)} collective-permute-done((bf16[256,1024]{1,0:T(8,128)(2,1)S(1)}, bf16[256,1024]{1,0:T(8,128)(2,1)S(1)}, u32[]{:S(2)}, u32[]{:S(2)}) %collective-permute-start.17) | collective-permute-done | bytes 524320 | tf_op jit(solution)/shard_map/ppermute | solution.py:467
  93.1 2.2 %collective-permute-done.18.refs_18_ = bf16[256,1024]{1,0:T(8,128)(2,1)S(1)} collective-permute-done((bf16[256,1024]{1,0:T(8,128)(2,1)S(1)}, bf16[256,1024]{1,0:T(8,128)(2,1)S(1)}, u32[]{:S(2)}, u32[]{:S(2)}) %collective-permute-start.18) | collective-permute-done | bytes 524320 | tf_op jit(solution)/shard_map/ppermute | solution.py:467
  95.3 2.2 %collective-permute-start.21 = (bf16[256,1024]{1,0:T(8,128)(2,1)S(1)}, bf16[256,1024]{1,0:T(8,128)(2,1)S(1)}, u32[]{:S(2)}, u32[]{:S(2)}) collective-permute-start(bf16[256,1024]{1,0:T(8,128)(2,1)S(1)} %collective-permute-done.17.refs_17_), channel_id=1, source_target_pairs={{0,8},{2,10},{8,16},{10,18},{16,24},{18,26},{24,28},{26,30},{28,20... | collective-permute-start | bytes 1572872 | tf_op jit(solution)/shard_map/ppermute | solution.py:467
  98.0 8.4 %collective-permute-done.21.refs_19_ = bf16[256,1024]{1,0:T(8,128)(2,1)S(1)} collective-permute-done((bf16[256,1024]{1,0:T(8,128)(2,1)S(1)}, bf16[256,1024]{1,0:T(8,128)(2,1)S(1)}, u32[]{:S(2)}, u32[]{:S(2)}) %collective-permute-start.21) | collective-permute-done | bytes 524320 | tf_op jit(solution)/shard_map/ppermute | solution.py:467
  107.2 2.7 %collective-permute-start.25 = (bf16[256,1024]{1,0:T(8,128)(2,1)S(1)}, bf16[256,1024]{1,0:T(8,128)(2,1)S(1)}, u32[]{:S(2)}, u32[]{:S(2)}) collective-permute-start(bf16[256,1024]{1,0:T(8,128)(2,1)S(1)} %collective-permute-done.21.refs_19_), channel_id=1, source_target_pairs={{0,8},{2,10},{8,16},{10,18},{16,24},{18,26},{24,28},{26,30},{28,20... | collective-permute-start | bytes 1572872 | tf_op jit(solution)/shard_map/ppermute | solution.py:467
  111.8 5.3 %collective-permute-done.25.refs_21_ = bf16[256,1024]{1,0:T(8,128)(2,1)S(1)} collective-permute-done((bf16[256,1024]{1,0:T(8,128)(2,1)S(1)}, bf16[256,1024]{1,0:T(8,128)(2,1)S(1)}, u32[]{:S(2)}, u32[]{:S(2)}) %collective-permute-start.25) | collective-permute-done | bytes 524320 | tf_op jit(solution)/shard_map/ppermute | solution.py:467
  119.3 2.8 %collective-permute-done.23.refs_4_ = bf16[128,2048]{1,0:T(8,128)(2,1)S(1)} collective-permute-done((bf16[128,2048]{1,0:T(8,128)(2,1)}, bf16[128,2048]{1,0:T(8,128)(2,1)S(1)}, u32[]{:S(2)}, u32[]{:S(2)}) %collective-permute-start.23) | collective-permute-done | bytes 524320 | tf_op jit(solution)/shard_map/ppermute | solution.py:535
  125.9 5.7 %collective-permute-done.27.refs_6_ = bf16[128,2048]{1,0:T(8,128)(2,1)} collective-permute-done((bf16[128,2048]{1,0:T(8,128)(2,1)}, bf16[128,2048]{1,0:T(8,128)(2,1)}, u32[]{:S(2)}, u32[]{:S(2)}) %collective-permute-start.27) | collective-permute-done | bytes 524320 | tf_op jit(solution)/shard_map/ppermute | solution.py:535
  135.7 5.9 %shard_map.81 = bf16[512,512]{1,0:T(8,128)(2,1)S(1)} custom-call(s32[19]{0:T(128)S(1)} %fusion.info_ref, bf16[128,2048]{1,0:T(8,128)(2,1)S(1)} %collective-permute-done.13.refs_0_, bf16[128,2048]{1,0:T(8,128)(2,1)S(1)} %collective-permute-done.14.refs_1_, bf16[128,2048]{1,0:T(8,128)(2,1)S(1)} %collective-permute-done.19.refs_2_, ...), custom_call_target="tpu_custom_call" | custom-call | flops 2147483648 | bytes 8912896 | tf_op jit(solution)/shard_map/pallas_call | solution.py:383
  141.9 5.9 %shard_map.79 = bf16[512,512]{1,0:T(8,128)(2,1)S(1)} custom-call(s32[19]{0:T(128)S(1)} %fusion.info_ref, bf16[128,2048]{1,0:T(8,128)(2,1)S(1)} %collective-permute-done.13.refs_0_, bf16[128,2048]{1,0:T(8,128)(2,1)S(1)} %collective-permute-done.14.refs_1_, bf16[128,2048]{1,0:T(8,128)(2,1)S(1)} %collective-permute-done.19.refs_2_, ...), custom_call_target="tpu_custom_call" | custom-call | flops 2147483648 | bytes 8912896 | tf_op jit(solution)/shard_map/pallas_call | solution.py:383
  149.6 10.3 %shard_map.80 = bf16[512,2048]{1,0:T(8,128)(2,1)} custom-call(s32[19]{0:T(128)S(1)} %fusion.info_ref, bf16[128,2048]{1,0:T(8,128)(2,1)} %get-tuple-element.80.refs_0_, bf16[128,2048]{1,0:T(8,128)(2,1)} %collective-permute-done.31.refs_1_, bf16[128,2048]{1,0:T(8,128)(2,1)} %get-tuple-element.69.refs_2_, bf16[128,2048]{1,0:T(8,128)(2,1)} %collective-permute-done.32.refs_3_, ...), custom_call_target="tpu_custom_call" | custom-call | flops 4294967296 | bytes 13631488 | tf_op jit(solution)/shard_map/pallas_call | solution.py:383
  160.7 6.5 %collective-permute-done.36 = bf16[512,512]{1,0:T(8,128)(2,1)S(1)} collective-permute-done((bf16[512,512]{1,0:T(8,128)(2,1)S(1)}, bf16[512,512]{1,0:T(8,128)(2,1)S(1)}, u32[]{:S(2)}, u32[]{:S(2)}) %collective-permute-start.36) | collective-permute-done | bytes 524320 | tf_op jit(solution)/shard_map/ppermute | solution.py:555
  (107 shorter events, 41.9 us)
Async XLA Ops:
  1.4 26.9 %collective-permute-start.3 = (bf16[256,1024]{1,0:T(8,128)(2,1)S(1)}, bf16[256,1024]{1,0:T(8,128)(2,1)}, u32[]{:S(2)}, u32[]{:S(2)}) collective-permute-start(bf16[256,1024]{1,0:T(8,128)(2,1)S(1)} %get-tuple-element.82.refs_8_), channel_id=1, source_target_pairs={{0,8},{2,10},{8,16},{10,18},{16,24},{18,26},{24,28},{26,30},{28,20... | collective-permute-start | bytes 1572872 | tf_op jit(solution)/shard_map/ppermute | solution.py:467
  4.5 23.8 %collective-permute-start.4 = (bf16[256,1024]{1,0:T(8,128)(2,1)S(1)}, bf16[256,1024]{1,0:T(8,128)(2,1)}, u32[]{:S(2)}, u32[]{:S(2)}) collective-permute-start(bf16[256,1024]{1,0:T(8,128)(2,1)S(1)} %get-tuple-element.82.refs_8_), channel_id=1, source_target_pairs={{8,0},{10,2},{16,8},{18,10},{24,16},{26,18},{28,24},{30,26},{20,28... | collective-permute-start | bytes 1572872 | tf_op jit(solution)/shard_map/ppermute | solution.py:467
  11.3 17.0 %collective-permute-start.1 = (bf16[4,272,128]{2,1,0:T(8,128)(2,1)S(1)}, bf16[4,272,128]{2,1,0:T(8,128)(2,1)S(1)}, u32[]{:S(2)}, u32[]{:S(2)}) collective-permute-start(bf16[4,272,128]{2,1,0:T(8,128)(2,1)S(1)} %get-tuple-element.45), channel_id=1, source_target_pairs={{0,4},{2,6},{4,0},{6,2},{8,12},{10,14},{12,8},{14,10},{16,20},{18,... | collective-permute-start | bytes 835592 | tf_op jit(solution)/shard_map/ppermute | solution.py:488
  12.8 15.5 %collective-permute-start.2 = (bf16[4,272,128]{2,1,0:T(8,128)(2,1)S(1)}, bf16[4,272,128]{2,1,0:T(8,128)(2,1)S(1)}, u32[]{:S(2)}, u32[]{:S(2)}) collective-permute-start(bf16[4,272,128]{2,1,0:T(8,128)(2,1)S(1)} %get-tuple-element.46), channel_id=1, source_target_pairs={{0,6},{2,4},{4,2},{6,0},{8,14},{10,12},{12,10},{14,8},{16,22},{18,... | collective-permute-start | bytes 835592 | tf_op jit(solution)/shard_map/ppermute | solution.py:488
  30.7 16.1 %collective-permute-start.7 = (bf16[256,1024]{1,0:T(8,128)(2,1)S(1)}, bf16[256,1024]{1,0:T(8,128)(2,1)S(1)}, u32[]{:S(2)}, u32[]{:S(2)}) collective-permute-start(bf16[256,1024]{1,0:T(8,128)(2,1)S(1)} %get-tuple-element.51), channel_id=1, source_target_pairs={{0,2},{2,0},{4,6},{6,4},{8,10},{10,8},{12,14},{14,12},{16,18},{18,... | collective-permute-start | bytes 1572872 | tf_op jit(solution)/shard_map/ppermute | solution.py:494
  32.5 16.6 %collective-permute-start.8 = (bf16[256,1024]{1,0:T(8,128)(2,1)}, bf16[256,1024]{1,0:T(8,128)(2,1)S(1)}, u32[]{:S(2)}, u32[]{:S(2)}) collective-permute-start(bf16[256,1024]{1,0:T(8,128)(2,1)} %collective-permute-done.3.refs_9_), channel_id=1, source_target_pairs={{0,8},{2,10},{8,16},{10,18},{16,24},{18,26},{24,28},{26,30},{28,20... | collective-permute-start | bytes 1572872 | tf_op jit(solution)/shard_map/ppermute | solution.py:467
  32.5 16.7 %collective-permute-start.9 = (bf16[256,1024]{1,0:T(8,128)(2,1)}, bf16[256,1024]{1,0:T(8,128)(2,1)S(1)}, u32[]{:S(2)}, u32[]{:S(2)}) collective-permute-start(bf16[256,1024]{1,0:T(8,128)(2,1)} %collective-permute-done.4.refs_10_), channel_id=1, source_target_pairs={{8,0},{10,2},{16,8},{18,10},{24,16},{26,18},{28,24},{30,26},{20,28... | collective-permute-start | bytes 1572872 | tf_op jit(solution)/shard_map/ppermute | solution.py:467
  38.6 14.9 %collective-permute-start.6 = (bf16[4,272,128]{2,1,0:T(8,128)(2,1)S(1)}, bf16[4,272,128]{2,1,0:T(8,128)(2,1)S(1)}, u32[]{:S(2)}, u32[]{:S(2)}) collective-permute-start(bf16[4,272,128]{2,1,0:T(8,128)(2,1)S(1)} %shard_map.75), channel_id=1, source_target_pairs={{0,16},{2,18},{4,20},{6,22},{8,24},{10,26},{12,28},{14,30},{1,17},... | collective-permute-start | bytes 835592 | tf_op jit(solution)/shard_map/ppermute | solution.py:499
  55.6 18.6 %collective-permute-start.10 = (bf16[4,272,128]{2,1,0:T(8,128)(2,1)S(1)}, bf16[4,272,128]{2,1,0:T(8,128)(2,1)S(1)}, u32[]{:S(2)}, u32[]{:S(2)}) collective-permute-start(bf16[4,272,128]{2,1,0:T(8,128)(2,1)S(1)} %get-tuple-element.54), channel_id=1, source_target_pairs={{0,2},{2,0},{4,6},{6,4},{8,10},{10,8},{12,14},{14,12},{16,18},{18,... | collective-permute-start | bytes 835592 | tf_op jit(solution)/shard_map/ppermute | solution.py:518
  57.0 17.1 %collective-permute-start.11 = (bf16[4,272,128]{2,1,0:T(8,128)(2,1)S(1)}, bf16[4,272,128]{2,1,0:T(8,128)(2,1)S(1)}, u32[]{:S(2)}, u32[]{:S(2)}) collective-permute-start(bf16[4,272,128]{2,1,0:T(8,128)(2,1)S(1)} %get-tuple-element.55), channel_id=1, source_target_pairs={{0,4},{2,6},{4,0},{6,2},{8,12},{10,14},{12,8},{14,10},{16,20},{18,... | collective-permute-start | bytes 835592 | tf_op jit(solution)/shard_map/ppermute | solution.py:518
  58.4 15.7 %collective-permute-start.12 = (bf16[4,272,128]{2,1,0:T(8,128)(2,1)S(1)}, bf16[4,272,128]{2,1,0:T(8,128)(2,1)S(1)}, u32[]{:S(2)}, u32[]{:S(2)}) collective-permute-start(bf16[4,272,128]{2,1,0:T(8,128)(2,1)S(1)} %get-tuple-element.56), channel_id=1, source_target_pairs={{0,6},{2,4},{4,2},{6,0},{8,14},{10,12},{12,10},{14,8},{16,22},{18,... | collective-permute-start | bytes 835592 | tf_op jit(solution)/shard_map/ppermute | solution.py:518
  67.1 18.9 %collective-permute-start.15 = (bf16[256,1024]{1,0:T(8,128)(2,1)S(1)}, bf16[256,1024]{1,0:T(8,128)(2,1)S(1)}, u32[]{:S(2)}, u32[]{:S(2)}) collective-permute-start(bf16[256,1024]{1,0:T(8,128)(2,1)S(1)} %collective-permute-done.8.refs_11_), channel_id=1, source_target_pairs={{0,8},{2,10},{8,16},{10,18},{16,24},{18,26},{24,28},{26,30},{28,20... | collective-permute-start | bytes 1572872 | tf_op jit(solution)/shard_map/ppermute | solution.py:467
  74.1 13.5 %collective-permute-start.16 = (bf16[256,1024]{1,0:T(8,128)(2,1)S(1)}, bf16[256,1024]{1,0:T(8,128)(2,1)S(1)}, u32[]{:S(2)}, u32[]{:S(2)}) collective-permute-start(bf16[256,1024]{1,0:T(8,128)(2,1)S(1)} %collective-permute-done.9.refs_12_), channel_id=1, source_target_pairs={{8,0},{10,2},{16,8},{18,10},{24,16},{26,18},{28,24},{30,26},{20,28... | collective-permute-start | bytes 1572872 | tf_op jit(solution)/shard_map/ppermute | solution.py:467
  79.7 13.3 %collective-permute-start.17 = (bf16[256,1024]{1,0:T(8,128)(2,1)S(1)}, bf16[256,1024]{1,0:T(8,128)(2,1)S(1)}, u32[]{:S(2)}, u32[]{:S(2)}) collective-permute-start(bf16[256,1024]{1,0:T(8,128)(2,1)S(1)} %collective-permute-done.7.refs_16_), channel_id=1, source_target_pairs={{0,8},{2,10},{8,16},{10,18},{16,24},{18,26},{24,28},{26,30},{28,20... | collective-permute-start | bytes 1572872 | tf_op jit(solution)/shard_map/ppermute | solution.py:467
  81.8 13.5 %collective-permute-start.18 = (bf16[256,1024]{1,0:T(8,128)(2,1)S(1)}, bf16[256,1024]{1,0:T(8,128)(2,1)S(1)}, u32[]{:S(2)}, u32[]{:S(2)}) collective-permute-start(bf16[256,1024]{1,0:T(8,128)(2,1)S(1)} %collective-permute-done.7.refs_16_), channel_id=1, source_target_pairs={{8,0},{10,2},{16,8},{18,10},{24,16},{26,18},{28,24},{30,26},{20,28... | collective-permute-start | bytes 1572872 | tf_op jit(solution)/shard_map/ppermute | solution.py:467
  81.8 13.5 %collective-permute-start.13 = (bf16[128,2048]{1,0:T(8,128)(2,1)}, bf16[128,2048]{1,0:T(8,128)(2,1)S(1)}, u32[]{:S(2)}, u32[]{:S(2)}) collective-permute-start(bf16[128,2048]{1,0:T(8,128)(2,1)} %get-tuple-element.80.refs_0_), channel_id=1, source_target_pairs={{0,2},{2,0},{4,6},{6,4},{8,10},{10,8},{12,14},{14,12},{16,18},{18,... | collective-permute-start | bytes 1572872 | tf_op jit(solution)/shard_map/ppermute | solution.py:535
  95.3 11.1 %collective-permute-start.21 = (bf16[256,1024]{1,0:T(8,128)(2,1)S(1)}, bf16[256,1024]{1,0:T(8,128)(2,1)S(1)}, u32[]{:S(2)}, u32[]{:S(2)}) collective-permute-start(bf16[256,1024]{1,0:T(8,128)(2,1)S(1)} %collective-permute-done.17.refs_17_), channel_id=1, source_target_pairs={{0,8},{2,10},{8,16},{10,18},{16,24},{18,26},{24,28},{26,30},{28,20... | collective-permute-start | bytes 1572872 | tf_op jit(solution)/shard_map/ppermute | solution.py:467
  110.0 12.1 %collective-permute-start.23 = (bf16[128,2048]{1,0:T(8,128)(2,1)}, bf16[128,2048]{1,0:T(8,128)(2,1)S(1)}, u32[]{:S(2)}, u32[]{:S(2)}) collective-permute-start(bf16[128,2048]{1,0:T(8,128)(2,1)} %get-tuple-element.73.refs_4_), channel_id=1, source_target_pairs={{0,2},{2,0},{4,6},{6,4},{8,10},{10,8},{12,14},{14,12},{16,18},{18,... | collective-permute-start | bytes 1572872 | tf_op jit(solution)/shard_map/ppermute | solution.py:535
  131.5 16.3 %collective-permute-start.31 = (bf16[128,2048]{1,0:T(8,128)(2,1)}, bf16[128,2048]{1,0:T(8,128)(2,1)}, u32[]{:S(2)}, u32[]{:S(2)}) collective-permute-start(bf16[128,2048]{1,0:T(8,128)(2,1)} %get-tuple-element.80.refs_0_), channel_id=1, source_target_pairs={{0,1},{1,0},{2,3},{3,2},{4,5},{5,4},{6,7},{7,6},{8,9},{9,8},{10,11... | collective-permute-start | bytes 1572872 | tf_op jit(solution)/shard_map/ppermute | solution.py:528
  133.0 16.6 %collective-permute-start.32 = (bf16[128,2048]{1,0:T(8,128)(2,1)}, bf16[128,2048]{1,0:T(8,128)(2,1)}, u32[]{:S(2)}, u32[]{:S(2)}) collective-permute-start(bf16[128,2048]{1,0:T(8,128)(2,1)} %get-tuple-element.69.refs_2_), channel_id=1, source_target_pairs={{0,1},{1,0},{2,3},{3,2},{4,5},{5,4},{6,7},{7,6},{8,9},{9,8},{10,11... | collective-permute-start | bytes 1572872 | tf_op jit(solution)/shard_map/ppermute | solution.py:528
  134.9 14.7 %collective-permute-start.33 = (bf16[128,2048]{1,0:T(8,128)(2,1)}, bf16[128,2048]{1,0:T(8,128)(2,1)}, u32[]{:S(2)}, u32[]{:S(2)}) collective-permute-start(bf16[128,2048]{1,0:T(8,128)(2,1)} %get-tuple-element.73.refs_4_), channel_id=1, source_target_pairs={{0,1},{1,0},{2,3},{3,2},{4,5},{5,4},{6,7},{7,6},{8,9},{9,8},{10,11... | collective-permute-start | bytes 1572872 | tf_op jit(solution)/shard_map/ppermute | solution.py:528
  135.7 13.9 %collective-permute-start.34 = (bf16[128,2048]{1,0:T(8,128)(2,1)}, bf16[128,2048]{1,0:T(8,128)(2,1)}, u32[]{:S(2)}, u32[]{:S(2)}) collective-permute-start(bf16[128,2048]{1,0:T(8,128)(2,1)} %get-tuple-element.77.refs_6_), channel_id=1, source_target_pairs={{0,1},{1,0},{2,3},{3,2},{4,5},{5,4},{6,7},{7,6},{8,9},{9,8},{10,11... | collective-permute-start | bytes 1572872 | tf_op jit(solution)/shard_map/ppermute | solution.py:528
  141.6 18.3 %collective-permute-start.35 = (bf16[512,512]{1,0:T(8,128)(2,1)S(1)}, bf16[512,512]{1,0:T(8,128)(2,1)S(1)}, u32[]{:S(2)}, u32[]{:S(2)}) collective-permute-start(bf16[512,512]{1,0:T(8,128)(2,1)S(1)} %shard_map.81), channel_id=1, source_target_pairs={{0,2},{2,0},{4,6},{6,4},{8,10},{10,8},{12,14},{14,12},{16,18},{18,... | collective-permute-start | bytes 1572872 | tf_op jit(solution)/shard_map/ppermute | solution.py:555
  147.8 19.4 %collective-permute-start.36 = (bf16[512,512]{1,0:T(8,128)(2,1)S(1)}, bf16[512,512]{1,0:T(8,128)(2,1)S(1)}, u32[]{:S(2)}, u32[]{:S(2)}) collective-permute-start(bf16[512,512]{1,0:T(8,128)(2,1)S(1)} %shard_map.79), channel_id=1, source_target_pairs={{0,2},{2,0},{4,6},{6,4},{8,10},{10,8},{12,14},{14,12},{16,18},{18,... | collective-permute-start | bytes 1572872 | tf_op jit(solution)/shard_map/ppermute | solution.py:555
  (34 other events, 576.7 us)

commit v6 on v5

--- a/solution.py
+++ b/solution.py
@@ -484,6 +484,7 @@
     ring_mine = Ring(mine, n, True)
     ring_mine.step()
     *memory, g = summarize(info, keys, values, input_gate, forget_gate)
+    memory[PARTS - 1] = after(memory[PARTS - 1], *ring_mine.ends)
     got = [memory[0]] + [
         lax.ppermute(memory[r], "seq", xor_perm(n, r)) for r in range(1, PARTS)
     ]

time: 168 us -> 168 us (level)
  waiting for transfers between devices: 72.9 us -> 70.2 us
  starting transfers between devices: 46.9 us -> 48.7 us
    ppermute x3, waiting for transfers between devices: 15.5 us -> 7.48 us  [body(): lax.ppermute(memory[r], 'seq', xor_perm(n, r))]
    ppermute x14, waiting for transfers between devices: 34.6 us -> 39.4 us  [step(): self.ends = tuple((lax.ppermute(e, 'seq', p) for e, p in zip(ends, perms)))]
    ppermute x3, starting transfers between devices: 3.55 us -> 6.36 us  [body(): lax.ppermute(memory[r], 'seq', xor_perm(n, r))]
where the time goes in v6:
time: 168 us; the launch traced here: 167 us
  waiting for transfers between devices  70.2 us (42%)
  starting transfers between devices  48.7 us (29%)
  Pallas kernels  41.1 us (24%)
  local copies, waits for them, and re-layouts  6.79 us (4%)
    ppermute x14, waiting for transfers between devices, step(): self.ends = tuple((lax.ppermute(e, 'seq', p) for e, p in zip(ends, perms)))  39.4 us
    pallas_call x3, Pallas kernels, project(): pl.pallas_call(functools.partial(project_kernel, (len(operands), len(oper...  21.9 us
    ppermute x14, starting transfers between devices, step(): self.ends = tuple((lax.ppermute(e, 'seq', p) for e, p in zip(ends, perms)))  21.7 us
    ppermute x2, starting transfers between devices, body(): come = lax.ppermute(window, 'seq', [(s, s + step) for s in range(n - step)])  9.48 us
    ppermute x4, waiting for transfers between devices, body(): come = lax.ppermute(a, 'seq', swap)  9.11 us
    ppermute x2, waiting for transfers between devices, body(): come = lax.ppermute(window, 'seq', [(s, s + step) for s in range(n - step)])  7.7 us
    ppermute x3, waiting for transfers between devices, body(): lax.ppermute(memory[r], 'seq', xor_perm(n, r))  7.48 us
    pallas_call x1, Pallas kernels, intra(): pl.pallas_call(intra_kernel, grid=(heads,), out_shape=(jax.ShapeDtypeStru...  6.95 us
  transfers between devices with their start and end apart: 37, of which 19 were waited for; matrix products, arithmetic and copies ran while one was open for 1% of the time, Pallas kernels for 23%

profile of v6, /device:TPU:0, one launch (start us, length us, event | category | flops | bytes accessed | tf_op | source)
XLA Modules:
  0.0 167.2 jit_solution(5790230007069168040)
XLA Ops:
  1.4 3.1 %collective-permute-start.2 = (bf16[256,1024]{1,0:T(8,128)(2,1)S(1)}, bf16[256,1024]{1,0:T(8,128)(2,1)}, u32[]{:S(2)}, u32[]{:S(2)}) collective-permute-start(bf16[256,1024]{1,0:T(8,128)(2,1)S(1)} %get-tuple-element.84.refs_8_), channel_id=1, source_target_pairs={{0,8},{2,10},{8,16},{10,18},{16,24},{18,26},{24,28},{26,30},{28,20... | collective-permute-start | bytes 1572872 | tf_op jit(solution)/shard_map/ppermute | solution.py:467
  6.5 2.8 %shard_map.73 = (bf16[4,272,128]{2,1,0:T(8,128)(2,1)S(1)}, bf16[4,272,128]{2,1,0:T(8,128)(2,1)S(1)}, bf16[4,272,128]{2,1,0:T(8,128)(2,1)S(1)}, bf16[4,272,128]{2,1,0:T(8,128)(2,1)S(1)}, f32[4,512]{1,0:T(4,128)S(1)}) custom-call(s32[19]{0:T(128)S(1)} %fusion.info_ref, bf16[512,1024]{1,0:T(8,128)(2,1)S(1)} %copy-done.1, bf16[512,2048]{1,0:T(8,128)(2,1)S(1)} %copy-done, ...), custom_call_target="tpu_custom_call" | custom-call | tf_op jit(solution)/shard_map/pallas_call | solution.py:117
  12.8 4.5 %collective-permute-done.2.refs_9_ = bf16[256,1024]{1,0:T(8,128)(2,1)} collective-permute-done((bf16[256,1024]{1,0:T(8,128)(2,1)S(1)}, bf16[256,1024]{1,0:T(8,128)(2,1)}, u32[]{:S(2)}, u32[]{:S(2)}) %collective-permute-start.2) | collective-permute-done | bytes 524320 | tf_op jit(solution)/shard_map/ppermute | solution.py:467
  18.0 2.8 %collective-permute-start.4 = (bf16[4,272,128]{2,1,0:T(8,128)(2,1)S(1)}, bf16[4,272,128]{2,1,0:T(8,128)(2,1)S(1)}, u32[]{:S(2)}, u32[]{:S(2)}) collective-permute-start(bf16[4,272,128]{2,1,0:T(8,128)(2,1)S(1)} %get-tuple-element.48), channel_id=1, source_target_pairs={{0,6},{2,4},{4,2},{6,0},{8,14},{10,12},{12,10},{14,8},{16,22},{18,... | collective-permute-start | bytes 835592 | tf_op jit(solution)/shard_map/ppermute | solution.py:489
  20.9 7.5 %collective-permute-done.1.refs_2_ = bf16[4,272,128]{2,1,0:T(8,128)(2,1)S(1)} collective-permute-done((bf16[4,272,128]{2,1,0:T(8,128)(2,1)S(1)}, bf16[4,272,128]{2,1,0:T(8,128)(2,1)S(1)}, u32[]{:S(2)}, u32[]{:S(2)}) %collective-permute-start.1) | collective-permute-done | bytes 278560 | tf_op jit(solution)/shard_map/ppermute | solution.py:489
  34.5 3.3 %collective-permute-done.5.one_ref.two_ref = bf16[4,272,128]{2,1,0:T(8,128)(2,1)S(1)} collective-permute-done((bf16[4,272,128]{2,1,0:T(8,128)(2,1)S(1)}, bf16[4,272,128]{2,1,0:T(8,128)(2,1)S(1)}, u32[]{:S(2)}, u32[]{:S(2)}) %collective-permute-start.5) | collective-permute-done | bytes 278560 | tf_op jit(solution)/shard_map/ppermute | solution.py:500
  38.6 8.2 %collective-permute-start.6 = (bf16[4,272,128]{2,1,0:T(8,128)(2,1)S(1)}, bf16[4,272,128]{2,1,0:T(8,128)(2,1)S(1)}, u32[]{:S(2)}, u32[]{:S(2)}) collective-permute-start(bf16[4,272,128]{2,1,0:T(8,128)(2,1)S(1)} %shard_map.75), channel_id=1, source_target_pairs={{0,16},{2,18},{4,20},{6,22},{8,24},{10,26},{12,28},{14,30},{1,17},... | collective-permute-start | bytes 835592 | tf_op jit(solution)/shard_map/ppermute | solution.py:500
  46.8 2.3 %collective-permute-done.8.refs_11_ = bf16[256,1024]{1,0:T(8,128)(2,1)S(1)} collective-permute-done((bf16[256,1024]{1,0:T(8,128)(2,1)}, bf16[256,1024]{1,0:T(8,128)(2,1)S(1)}, u32[]{:S(2)}, u32[]{:S(2)}) %collective-permute-start.8) | collective-permute-done | bytes 524320 | tf_op jit(solution)/shard_map/ppermute | solution.py:467
  49.1 4.4 %collective-permute-done.6.one_ref = bf16[4,272,128]{2,1,0:T(8,128)(2,1)S(1)} collective-permute-done((bf16[4,272,128]{2,1,0:T(8,128)(2,1)S(1)}, bf16[4,272,128]{2,1,0:T(8,128)(2,1)S(1)}, u32[]{:S(2)}, u32[]{:S(2)}) %collective-permute-start.6) | collective-permute-done | bytes 278560 | tf_op jit(solution)/shard_map/ppermute | solution.py:500
  59.1 6.9 %shard_map.77 = (f32[512,2048]{1,0:T(8,128)}, f32[4,512,128]{2,1,0:T(8,128)S(1)}) custom-call(bf16[512,1024]{1,0:T(8,128)(2,1)S(1)} %copy-done.3, bf16[512,1024]{1,0:T(8,128)(2,1)S(1)} %copy-done.2, bf16[512,2048]{1,0:T(8,128)(2,1)} %v_ref.3, f32[4,1,512]{2,1,0:T(1,128)S(1)} %broadcast_in_dim.6.in_ref, f32[4,1,512]{2,1,0:T(1,128)S(1)} %broadcast_in_dim.7.g_ref), custom_call_target="tpu_custom_call" | custom-call | tf_op jit(solution)/shard_map/pallas_call | solution.py:256
  67.1 5.9 %collective-permute-start.15 = (bf16[256,1024]{1,0:T(8,128)(2,1)S(1)}, bf16[256,1024]{1,0:T(8,128)(2,1)S(1)}, u32[]{:S(2)}, u32[]{:S(2)}) collective-permute-start(bf16[256,1024]{1,0:T(8,128)(2,1)S(1)} %collective-permute-done.8.refs_11_), channel_id=1, source_target_pairs={{0,8},{2,10},{8,16},{10,18},{16,24},{18,26},{24,28},{26,30},{28,20... | collective-permute-start | bytes 1572872 | tf_op jit(solution)/shard_map/ppermute | solution.py:467
  73.0 5.6 %shard_map.78 = (bf16[128,2048]{1,0:T(8,128)(2,1)}, bf16[128,2048]{1,0:T(8,128)(2,1)}, bf16[128,2048]{1,0:T(8,128)(2,1)}, bf16[128,2048]{1,0:T(8,128)(2,1)}) custom-call(s32[19]{0:T(128)S(1)} %fusion.info_ref, bf16[512,1024]{1,0:T(8,128)(2,1)} %q_ref.3, bf16[4,272,128]{2,1,0:T(8,128)(2,1)S(1)} %get-tuple-element.55.refs_0_, ...), custom_call_target="tpu_custom_call" | custom-call | tf_op jit(solution)/shard_map/pallas_call | solution.py:308
  82.1 3.0 %collective-permute-done.15.refs_13_ = bf16[256,1024]{1,0:T(8,128)(2,1)S(1)} collective-permute-done((bf16[256,1024]{1,0:T(8,128)(2,1)S(1)}, bf16[256,1024]{1,0:T(8,128)(2,1)S(1)}, u32[]{:S(2)}, u32[]{:S(2)}) %collective-permute-start.15) | collective-permute-done | bytes 524320 | tf_op jit(solution)/shard_map/ppermute | solution.py:467
  86.8 5.4 %collective-permute-done.17.refs_17_ = bf16[256,1024]{1,0:T(8,128)(2,1)S(1)} collective-permute-done((bf16[256,1024]{1,0:T(8,128)(2,1)S(1)}, bf16[256,1024]{1,0:T(8,128)(2,1)S(1)}, u32[]{:S(2)}, u32[]{:S(2)}) %collective-permute-start.17) | collective-permute-done | bytes 524320 | tf_op jit(solution)/shard_map/ppermute | solution.py:467
  94.4 2.2 %collective-permute-start.21 = (bf16[256,1024]{1,0:T(8,128)(2,1)S(1)}, bf16[256,1024]{1,0:T(8,128)(2,1)S(1)}, u32[]{:S(2)}, u32[]{:S(2)}) collective-permute-start(bf16[256,1024]{1,0:T(8,128)(2,1)S(1)} %collective-permute-done.17.refs_17_), channel_id=1, source_target_pairs={{0,8},{2,10},{8,16},{10,18},{16,24},{18,26},{24,28},{26,30},{28,20... | collective-permute-start | bytes 1572872 | tf_op jit(solution)/shard_map/ppermute | solution.py:467
  98.1 7.4 %collective-permute-done.21.refs_19_ = bf16[256,1024]{1,0:T(8,128)(2,1)S(1)} collective-permute-done((bf16[256,1024]{1,0:T(8,128)(2,1)S(1)}, bf16[256,1024]{1,0:T(8,128)(2,1)S(1)}, u32[]{:S(2)}, u32[]{:S(2)}) %collective-permute-start.21) | collective-permute-done | bytes 524320 | tf_op jit(solution)/shard_map/ppermute | solution.py:467
  106.4 4.3 %collective-permute-start.25 = (bf16[256,1024]{1,0:T(8,128)(2,1)S(1)}, bf16[256,1024]{1,0:T(8,128)(2,1)S(1)}, u32[]{:S(2)}, u32[]{:S(2)}) collective-permute-start(bf16[256,1024]{1,0:T(8,128)(2,1)S(1)} %collective-permute-done.21.refs_19_), channel_id=1, source_target_pairs={{0,8},{2,10},{8,16},{10,18},{16,24},{18,26},{24,28},{26,30},{28,20... | collective-permute-start | bytes 1572872 | tf_op jit(solution)/shard_map/ppermute | solution.py:467
  110.8 8.0 %collective-permute-done.25.refs_21_ = bf16[256,1024]{1,0:T(8,128)(2,1)S(1)} collective-permute-done((bf16[256,1024]{1,0:T(8,128)(2,1)S(1)}, bf16[256,1024]{1,0:T(8,128)(2,1)S(1)}, u32[]{:S(2)}, u32[]{:S(2)}) %collective-permute-start.25) | collective-permute-done | bytes 524320 | tf_op jit(solution)/shard_map/ppermute | solution.py:467
  118.8 2.7 %collective-permute-done.26.refs_22_ = bf16[256,1024]{1,0:T(8,128)(2,1)S(1)} collective-permute-done((bf16[256,1024]{1,0:T(8,128)(2,1)S(1)}, bf16[256,1024]{1,0:T(8,128)(2,1)S(1)}, u32[]{:S(2)}, u32[]{:S(2)}) %collective-permute-start.26) | collective-permute-done | bytes 524320 | tf_op jit(solution)/shard_map/ppermute | solution.py:467
  125.0 7.6 %collective-permute-done.27.refs_6_ = bf16[128,2048]{1,0:T(8,128)(2,1)} collective-permute-done((bf16[128,2048]{1,0:T(8,128)(2,1)}, bf16[128,2048]{1,0:T(8,128)(2,1)}, u32[]{:S(2)}, u32[]{:S(2)}) %collective-permute-start.27) | collective-permute-done | bytes 524320 | tf_op jit(solution)/shard_map/ppermute | solution.py:536
  134.8 5.8 %shard_map.81 = bf16[512,512]{1,0:T(8,128)(2,1)S(1)} custom-call(s32[19]{0:T(128)S(1)} %fusion.info_ref, bf16[128,2048]{1,0:T(8,128)(2,1)S(1)} %collective-permute-done.13.refs_0_, bf16[128,2048]{1,0:T(8,128)(2,1)S(1)} %collective-permute-done.14.refs_1_, bf16[128,2048]{1,0:T(8,128)(2,1)S(1)} %collective-permute-done.19.refs_2_, ...), custom_call_target="tpu_custom_call" | custom-call | flops 2147483648 | bytes 8912896 | tf_op jit(solution)/shard_map/pallas_call | solution.py:383
  142.5 5.8 %shard_map.79 = bf16[512,512]{1,0:T(8,128)(2,1)S(1)} custom-call(s32[19]{0:T(128)S(1)} %fusion.info_ref, bf16[128,2048]{1,0:T(8,128)(2,1)S(1)} %collective-permute-done.13.refs_0_, bf16[128,2048]{1,0:T(8,128)(2,1)S(1)} %collective-permute-done.14.refs_1_, bf16[128,2048]{1,0:T(8,128)(2,1)S(1)} %collective-permute-done.19.refs_2_, ...), custom_call_target="tpu_custom_call" | custom-call | flops 2147483648 | bytes 8912896 | tf_op jit(solution)/shard_map/pallas_call | solution.py:383
  148.8 10.3 %shard_map.80 = bf16[512,2048]{1,0:T(8,128)(2,1)} custom-call(s32[19]{0:T(128)S(1)} %fusion.info_ref, bf16[128,2048]{1,0:T(8,128)(2,1)} %get-tuple-element.82.refs_0_, bf16[128,2048]{1,0:T(8,128)(2,1)} %collective-permute-done.31.refs_1_, bf16[128,2048]{1,0:T(8,128)(2,1)} %get-tuple-element.71.refs_2_, bf16[128,2048]{1,0:T(8,128)(2,1)} %collective-permute-done.32.refs_3_, ...), custom_call_target="tpu_custom_call" | custom-call | flops 4294967296 | bytes 13631488 | tf_op jit(solution)/shard_map/pallas_call | solution.py:383
  159.9 6.5 %collective-permute-done.36 = bf16[512,512]{1,0:T(8,128)(2,1)S(1)} collective-permute-done((bf16[512,512]{1,0:T(8,128)(2,1)S(1)}, bf16[512,512]{1,0:T(8,128)(2,1)S(1)}, u32[]{:S(2)}, u32[]{:S(2)}) %collective-permute-start.36) | collective-permute-done | bytes 524320 | tf_op jit(solution)/shard_map/ppermute | solution.py:556
  (107 shorter events, 40.5 us)
Async XLA Ops:
  1.4 15.9 %collective-permute-start.2 = (bf16[256,1024]{1,0:T(8,128)(2,1)S(1)}, bf16[256,1024]{1,0:T(8,128)(2,1)}, u32[]{:S(2)}, u32[]{:S(2)}) collective-permute-start(bf16[256,1024]{1,0:T(8,128)(2,1)S(1)} %get-tuple-element.84.refs_8_), channel_id=1, source_target_pairs={{0,8},{2,10},{8,16},{10,18},{16,24},{18,26},{24,28},{26,30},{28,20... | collective-permute-start | bytes 1572872 | tf_op jit(solution)/shard_map/ppermute | solution.py:467
  4.5 13.5 %collective-permute-start.3 = (bf16[256,1024]{1,0:T(8,128)(2,1)S(1)}, bf16[256,1024]{1,0:T(8,128)(2,1)}, u32[]{:S(2)}, u32[]{:S(2)}) collective-permute-start(bf16[256,1024]{1,0:T(8,128)(2,1)S(1)} %get-tuple-element.84.refs_8_), channel_id=1, source_target_pairs={{8,0},{10,2},{16,8},{18,10},{24,16},{26,18},{28,24},{30,26},{20,28... | collective-permute-start | bytes 1572872 | tf_op jit(solution)/shard_map/ppermute | solution.py:467
  11.3 17.0 %collective-permute-start.1 = (bf16[4,272,128]{2,1,0:T(8,128)(2,1)S(1)}, bf16[4,272,128]{2,1,0:T(8,128)(2,1)S(1)}, u32[]{:S(2)}, u32[]{:S(2)}) collective-permute-start(bf16[4,272,128]{2,1,0:T(8,128)(2,1)S(1)} %get-tuple-element.46), channel_id=1, source_target_pairs={{0,4},{2,6},{4,0},{6,2},{8,12},{10,14},{12,8},{14,10},{16,20},{18,... | collective-permute-start | bytes 835592 | tf_op jit(solution)/shard_map/ppermute | solution.py:489
  30.7 18.4 %collective-permute-start.8 = (bf16[256,1024]{1,0:T(8,128)(2,1)}, bf16[256,1024]{1,0:T(8,128)(2,1)S(1)}, u32[]{:S(2)}, u32[]{:S(2)}) collective-permute-start(bf16[256,1024]{1,0:T(8,128)(2,1)} %collective-permute-done.2.refs_9_), channel_id=1, source_target_pairs={{0,8},{2,10},{8,16},{10,18},{16,24},{18,26},{24,28},{26,30},{28,20... | collective-permute-start | bytes 1572872 | tf_op jit(solution)/shard_map/ppermute | solution.py:467
  32.3 16.8 %collective-permute-start.9 = (bf16[256,1024]{1,0:T(8,128)(2,1)}, bf16[256,1024]{1,0:T(8,128)(2,1)S(1)}, u32[]{:S(2)}, u32[]{:S(2)}) collective-permute-start(bf16[256,1024]{1,0:T(8,128)(2,1)} %collective-permute-done.3.refs_10_), channel_id=1, source_target_pairs={{8,0},{10,2},{16,8},{18,10},{24,16},{26,18},{28,24},{30,26},{20,28... | collective-permute-start | bytes 1572872 | tf_op jit(solution)/shard_map/ppermute | solution.py:467
  32.8 16.3 %collective-permute-start.7 = (bf16[256,1024]{1,0:T(8,128)(2,1)S(1)}, bf16[256,1024]{1,0:T(8,128)(2,1)S(1)}, u32[]{:S(2)}, u32[]{:S(2)}) collective-permute-start(bf16[256,1024]{1,0:T(8,128)(2,1)S(1)} %get-tuple-element.53), channel_id=1, source_target_pairs={{0,2},{2,0},{4,6},{6,4},{8,10},{10,8},{12,14},{14,12},{16,18},{18,... | collective-permute-start | bytes 1572872 | tf_op jit(solution)/shard_map/ppermute | solution.py:495
  38.6 14.9 %collective-permute-start.6 = (bf16[4,272,128]{2,1,0:T(8,128)(2,1)S(1)}, bf16[4,272,128]{2,1,0:T(8,128)(2,1)S(1)}, u32[]{:S(2)}, u32[]{:S(2)}) collective-permute-start(bf16[4,272,128]{2,1,0:T(8,128)(2,1)S(1)} %shard_map.75), channel_id=1, source_target_pairs={{0,16},{2,18},{4,20},{6,22},{8,24},{10,26},{12,28},{14,30},{1,17},... | collective-permute-start | bytes 835592 | tf_op jit(solution)/shard_map/ppermute | solution.py:500
  55.5 17.4 %collective-permute-start.10 = (bf16[4,272,128]{2,1,0:T(8,128)(2,1)S(1)}, bf16[4,272,128]{2,1,0:T(8,128)(2,1)S(1)}, u32[]{:S(2)}, u32[]{:S(2)}) collective-permute-start(bf16[4,272,128]{2,1,0:T(8,128)(2,1)S(1)} %get-tuple-element.56), channel_id=1, source_target_pairs={{0,2},{2,0},{4,6},{6,4},{8,10},{10,8},{12,14},{14,12},{16,18},{18,... | collective-permute-start | bytes 835592 | tf_op jit(solution)/shard_map/ppermute | solution.py:519
  57.0 16.0 %collective-permute-start.11 = (bf16[4,272,128]{2,1,0:T(8,128)(2,1)S(1)}, bf16[4,272,128]{2,1,0:T(8,128)(2,1)S(1)}, u32[]{:S(2)}, u32[]{:S(2)}) collective-permute-start(bf16[4,272,128]{2,1,0:T(8,128)(2,1)S(1)} %get-tuple-element.57), channel_id=1, source_target_pairs={{0,4},{2,6},{4,0},{6,2},{8,12},{10,14},{12,8},{14,10},{16,20},{18,... | collective-permute-start | bytes 835592 | tf_op jit(solution)/shard_map/ppermute | solution.py:519
  58.4 14.6 %collective-permute-start.12 = (bf16[4,272,128]{2,1,0:T(8,128)(2,1)S(1)}, bf16[4,272,128]{2,1,0:T(8,128)(2,1)S(1)}, u32[]{:S(2)}, u32[]{:S(2)}) collective-permute-start(bf16[4,272,128]{2,1,0:T(8,128)(2,1)S(1)} %get-tuple-element.58), channel_id=1, source_target_pairs={{0,6},{2,4},{4,2},{6,0},{8,14},{10,12},{12,10},{14,8},{16,22},{18,... | collective-permute-start | bytes 835592 | tf_op jit(solution)/shard_map/ppermute | solution.py:519
  67.1 18.0 %collective-permute-start.15 = (bf16[256,1024]{1,0:T(8,128)(2,1)S(1)}, bf16[256,1024]{1,0:T(8,128)(2,1)S(1)}, u32[]{:S(2)}, u32[]{:S(2)}) collective-permute-start(bf16[256,1024]{1,0:T(8,128)(2,1)S(1)} %collective-permute-done.8.refs_11_), channel_id=1, source_target_pairs={{0,8},{2,10},{8,16},{10,18},{16,24},{18,26},{24,28},{26,30},{28,20... | collective-permute-start | bytes 1572872 | tf_op jit(solution)/shard_map/ppermute | solution.py:467
  73.0 13.9 %collective-permute-start.16 = (bf16[256,1024]{1,0:T(8,128)(2,1)S(1)}, bf16[256,1024]{1,0:T(8,128)(2,1)S(1)}, u32[]{:S(2)}, u32[]{:S(2)}) collective-permute-start(bf16[256,1024]{1,0:T(8,128)(2,1)S(1)} %collective-permute-done.9.refs_12_), channel_id=1, source_target_pairs={{8,0},{10,2},{16,8},{18,10},{24,16},{26,18},{28,24},{30,26},{20,28... | collective-permute-start | bytes 1572872 | tf_op jit(solution)/shard_map/ppermute | solution.py:467
  78.6 13.6 %collective-permute-start.17 = (bf16[256,1024]{1,0:T(8,128)(2,1)S(1)}, bf16[256,1024]{1,0:T(8,128)(2,1)S(1)}, u32[]{:S(2)}, u32[]{:S(2)}) collective-permute-start(bf16[256,1024]{1,0:T(8,128)(2,1)S(1)} %collective-permute-done.7.refs_16_), channel_id=1, source_target_pairs={{0,8},{2,10},{8,16},{10,18},{16,24},{18,26},{24,28},{26,30},{28,20... | collective-permute-start | bytes 1572872 | tf_op jit(solution)/shard_map/ppermute | solution.py:467
  80.6 13.8 %collective-permute-start.18 = (bf16[256,1024]{1,0:T(8,128)(2,1)S(1)}, bf16[256,1024]{1,0:T(8,128)(2,1)S(1)}, u32[]{:S(2)}, u32[]{:S(2)}) collective-permute-start(bf16[256,1024]{1,0:T(8,128)(2,1)S(1)} %collective-permute-done.7.refs_16_), channel_id=1, source_target_pairs={{8,0},{10,2},{16,8},{18,10},{24,16},{26,18},{28,24},{30,26},{20,28... | collective-permute-start | bytes 1572872 | tf_op jit(solution)/shard_map/ppermute | solution.py:467
  80.6 13.8 %collective-permute-start.13 = (bf16[128,2048]{1,0:T(8,128)(2,1)}, bf16[128,2048]{1,0:T(8,128)(2,1)S(1)}, u32[]{:S(2)}, u32[]{:S(2)}) collective-permute-start(bf16[128,2048]{1,0:T(8,128)(2,1)} %get-tuple-element.82.refs_0_), channel_id=1, source_target_pairs={{0,2},{2,0},{4,6},{6,4},{8,10},{10,8},{12,14},{14,12},{16,18},{18,... | collective-permute-start | bytes 1572872 | tf_op jit(solution)/shard_map/ppermute | solution.py:536
  106.4 12.4 %collective-permute-start.25 = (bf16[256,1024]{1,0:T(8,128)(2,1)S(1)}, bf16[256,1024]{1,0:T(8,128)(2,1)S(1)}, u32[]{:S(2)}, u32[]{:S(2)}) collective-permute-start(bf16[256,1024]{1,0:T(8,128)(2,1)S(1)} %collective-permute-done.21.refs_19_), channel_id=1, source_target_pairs={{0,8},{2,10},{8,16},{10,18},{16,24},{18,26},{24,28},{26,30},{28,20... | collective-permute-start | bytes 1572872 | tf_op jit(solution)/shard_map/ppermute | solution.py:467
  110.7 12.1 %collective-permute-start.23 = (bf16[128,2048]{1,0:T(8,128)(2,1)}, bf16[128,2048]{1,0:T(8,128)(2,1)S(1)}, u32[]{:S(2)}, u32[]{:S(2)}) collective-permute-start(bf16[128,2048]{1,0:T(8,128)(2,1)} %get-tuple-element.75.refs_4_), channel_id=1, source_target_pairs={{0,2},{2,0},{4,6},{6,4},{8,10},{10,8},{12,14},{14,12},{16,18},{18,... | collective-permute-start | bytes 1572872 | tf_op jit(solution)/shard_map/ppermute | solution.py:536
  110.8 12.0 %collective-permute-start.20 = (bf16[128,2048]{1,0:T(8,128)(2,1)S(1)}, bf16[128,2048]{1,0:T(8,128)(2,1)S(1)}, u32[]{:S(2)}, u32[]{:S(2)}) collective-permute-start(bf16[128,2048]{1,0:T(8,128)(2,1)S(1)} %collective-permute-done.19.refs_2_), channel_id=1, source_target_pairs={{0,1},{1,0},{2,3},{3,2},{4,5},{5,4},{6,7},{7,6},{8,9},{9,8},{10,11... | collective-permute-start | bytes 1572872 | tf_op jit(solution)/shard_map/ppermute | solution.py:529
  132.5 15.8 %collective-permute-start.31 = (bf16[128,2048]{1,0:T(8,128)(2,1)}, bf16[128,2048]{1,0:T(8,128)(2,1)}, u32[]{:S(2)}, u32[]{:S(2)}) collective-permute-start(bf16[128,2048]{1,0:T(8,128)(2,1)} %get-tuple-element.82.refs_0_), channel_id=1, source_target_pairs={{0,1},{1,0},{2,3},{3,2},{4,5},{5,4},{6,7},{7,6},{8,9},{9,8},{10,11... | collective-permute-start | bytes 1572872 | tf_op jit(solution)/shard_map/ppermute | solution.py:529
  133.1 15.7 %collective-permute-start.32 = (bf16[128,2048]{1,0:T(8,128)(2,1)}, bf16[128,2048]{1,0:T(8,128)(2,1)}, u32[]{:S(2)}, u32[]{:S(2)}) collective-permute-start(bf16[128,2048]{1,0:T(8,128)(2,1)} %get-tuple-element.71.refs_2_), channel_id=1, source_target_pairs={{0,1},{1,0},{2,3},{3,2},{4,5},{5,4},{6,7},{7,6},{8,9},{9,8},{10,11... | collective-permute-start | bytes 1572872 | tf_op jit(solution)/shard_map/ppermute | solution.py:529
  134.0 14.7 %collective-permute-start.33 = (bf16[128,2048]{1,0:T(8,128)(2,1)}, bf16[128,2048]{1,0:T(8,128)(2,1)}, u32[]{:S(2)}, u32[]{:S(2)}) collective-permute-start(bf16[128,2048]{1,0:T(8,128)(2,1)} %get-tuple-element.75.refs_4_), channel_id=1, source_target_pairs={{0,1},{1,0},{2,3},{3,2},{4,5},{5,4},{6,7},{7,6},{8,9},{9,8},{10,11... | collective-permute-start | bytes 1572872 | tf_op jit(solution)/shard_map/ppermute | solution.py:529
  134.8 13.9 %collective-permute-start.34 = (bf16[128,2048]{1,0:T(8,128)(2,1)}, bf16[128,2048]{1,0:T(8,128)(2,1)}, u32[]{:S(2)}, u32[]{:S(2)}) collective-permute-start(bf16[128,2048]{1,0:T(8,128)(2,1)} %get-tuple-element.79.refs_6_), channel_id=1, source_target_pairs={{0,1},{1,0},{2,3},{3,2},{4,5},{5,4},{6,7},{7,6},{8,9},{9,8},{10,11... | collective-permute-start | bytes 1572872 | tf_op jit(solution)/shard_map/ppermute | solution.py:529
  140.7 18.3 %collective-permute-start.35 = (bf16[512,512]{1,0:T(8,128)(2,1)S(1)}, bf16[512,512]{1,0:T(8,128)(2,1)S(1)}, u32[]{:S(2)}, u32[]{:S(2)}) collective-permute-start(bf16[512,512]{1,0:T(8,128)(2,1)S(1)} %shard_map.81), channel_id=1, source_target_pairs={{0,2},{2,0},{4,6},{6,4},{8,10},{10,8},{12,14},{14,12},{16,18},{18,... | collective-permute-start | bytes 1572872 | tf_op jit(solution)/shard_map/ppermute | solution.py:556
  148.4 18.0 %collective-permute-start.36 = (bf16[512,512]{1,0:T(8,128)(2,1)S(1)}, bf16[512,512]{1,0:T(8,128)(2,1)S(1)}, u32[]{:S(2)}, u32[]{:S(2)}) collective-permute-start(bf16[512,512]{1,0:T(8,128)(2,1)S(1)} %shard_map.79), channel_id=1, source_target_pairs={{0,2},{2,0},{4,6},{6,4},{8,10},{10,8},{12,14},{14,12},{16,18},{18,... | collective-permute-start | bytes 1572872 | tf_op jit(solution)/shard_map/ppermute | solution.py:556
  (34 other events, 570.2 us)
